TPU v7x, 32 devices: a whole 2x2x4 slice. The times are simulated.
32 devices in a mesh: groups: 2 (over y), gx: 4 (over z), gy: 2 (over x), vert: 2 (over core).
Axes of the slice: x: 2, y: 2, z: 4, core: 2. Of those that a mesh axis runs over, the one named last changes fastest.
Arguments:
- right_side: float32 [4, 512, 1024], P(('groups', 'vert'), 'gx', 'gy'), parts along dimension 0
- initial_guess: float32 [4, 512, 1024], P(('groups', 'vert'), 'gx', 'gy'), parts along dimension 0, may hold values from -4 to 4
- kappa_sq: float32 [4, 512, 1024], P(('groups', 'vert'), 'gx', 'gy'), parts along dimension 0, may hold values from 0.05 to 1
- smooth_weight: float32 [4], P(('groups', 'vert')), parts along dimension 0, may hold values from 0.5 to 2
- precond_scale: float32 [4, 512, 1024], P(('groups', 'vert'), 'gx', 'gy'), parts along dimension 0, may hold values from 0.01 to 0.05
- phi_vals: float32 [4, 4, 2, 16, 2, 256, 256], P(('groups', 'vert'), 'gx', 'gy'), parts along dimension 0, may hold values from -0.75 to 0.75
- phi_cols: int32 [4, 4, 2, 16, 2], P(('groups', 'vert'), 'gx', 'gy'), parts along dimension 0, may hold values from 0 to 511
- coarse_slots: int32 [8, 136], P(('groups', 'gx')), parts along dimension 0, may hold values from 0 to 271, as said below
- slot_count: int32 [8], P(('groups', 'gx')), parts along dimension 0, may hold values from 0 to 136, as said below
- coarse_rows: float32 [8, 136, 272], P(('groups', 'gx')), parts along dimension 0, as said below
Outputs:
- solution: float32 [4, 512, 1024], P(('groups', 'vert'), 'gx', 'gy'), parts along dimension 0
- residual: float32 [4, 512, 1024], P(('groups', 'vert'), 'gx', 'gy'), parts along dimension 0
There are 2 independent parts, one for each index of `groups`. A program takes and returns all parts, laid end to end along the dimension named above; each array names one. Nothing has to cross between parts.
Inputs may be any that keep to these rules, and one draw needn't show every extreme that they name: `coarse_slots`: slots 0 to slot_count[d] - 1 of owner d hold coarse rows; over all owners these live slots name each of the 272 coarse rows exactly once. Other slots hold arbitrary row numbers. `slot_count`: the busiest owner has exactly 136 live slots; the counts sum to 272. `coarse_rows`: live slot s of owner d holds row coarse_slots[d, s] of one symmetric positive definite matrix G; rows of other slots are arbitrary.
All inputs are finite; a program needn't handle non-finite values.
Results may differ from a plain program's by a relative error of at most 0.0003.
Values sent between devices are 32-bit elements; how exact they have to be, the bound alone decides.
No kernel may reach another device: no remote copies, remote signals or barrier semaphores. Data moves between devices by JAX's collectives and lax.ppermute only.
A program may use at most 64 MiB of HBM per device.

v0:
```python
import functools
import math

import jax
import jax.numpy as jnp
import numpy as np
from jax import lax
from jax.experimental import pallas as pl
from jax.experimental.pallas import tpu as pltpu
from jax.sharding import PartitionSpec as P

BSIDE = 16
PATCH = 64
LANES = 128
PAD = 8
ALL = ("gx", "gy", "vert")
F32 = jnp.float32
VMEM = pl.BlockSpec(memory_space=pltpu.VMEM)
SMEM = pl.BlockSpec(memory_space=pltpu.SMEM)
ANY = pl.BlockSpec(memory_space=pl.ANY)
PARAMS = pltpu.CompilerParams(vmem_limit_bytes=40 * 1024 * 1024)


class Sizes:
    def __init__(self, tx, ty, tile_shape, obs, reach, nco):
        self.tx, self.ty = tx, ty
        self.rows, self.cols = tile_shape
        self.obs, self.reach = obs, reach
        self.nco = nco
        self.px, self.py = self.rows // PATCH, self.cols // PATCH
        self.groups = self.cols // LANES
        self.ext = (self.rows + 2 * PAD, self.cols + 2 * LANES)
        self.devices = tx * ty * 2
        self.per_var = tx * ty * (1 + self.px * self.py)
        self.vec_rows = -(-nco // LANES)
        self.head = PAD * (-(-(self.vec_rows + 1) // PAD))
        self.ext_patches = (self.px + 2) * (self.py + 2)
        self.lift_rows = PAD * (-(-(self.ext_patches + self.px * self.py) // PAD))
        self.blocks = (self.rows // BSIDE) * (self.cols // BSIDE)
        self.top_div = math.sqrt(self.rows * self.cols)
        self.mid_div = float(PATCH)


def iota(shape, dim):
    return lax.broadcasted_iota(jnp.int32, shape, dim)


def lift_ids(sz):
    mid = np.full((sz.tx, sz.ty, 2, sz.lift_rows), -1, np.int32)
    top = np.full((sz.tx, sz.ty, 2, sz.lift_rows), -1, np.int32)
    tiles = sz.tx * sz.ty
    for x in range(sz.tx):
        for y in range(sz.ty):
            for v in range(2):
                for i in range(-1, sz.px + 1):
                    for j in range(-1, sz.py + 1):
                        gi, gj = x * sz.px + i, y * sz.py + j
                        if 0 <= gi < sz.tx * sz.px and 0 <= gj < sz.ty * sz.py:
                            at = (i + 1) * (sz.py + 2) + j + 1
                            mid[x, y, v, at] = v * sz.per_var + tiles + gi * sz.ty * sz.py + gj
                            top[x, y, v, at] = (
                                v * sz.per_var + (gi // sz.px) * sz.ty + gj // sz.py
                            )
                for i in range(sz.px):
                    for j in range(sz.py):
                        gi, gj = x * sz.px + i, y * sz.py + j
                        at = sz.ext_patches + i * sz.py + j
                        mid[x, y, v, at] = (1 - v) * sz.per_var + tiles + gi * sz.ty * sz.py + gj
                        top[x, y, v, at] = (1 - v) * sz.per_var + x * sz.ty + y
    order = np.arange(sz.tx)[:, None] ^ np.arange(sz.tx)[None, :]
    shape = (sz.tx, sz.tx, sz.ty, 2, sz.lift_rows)
    moved = [a[order.reshape(-1)].reshape(shape).transpose(0, 2, 3, 1, 4) for a in (mid, top)]
    return np.stack(moved, axis=3)


def pack_edges(sz, x0_ref, s_ref, k_ref, xe_ref, xo_ref, ye_ref, yo_ref):
    xi, yi = lax.axis_index("gx"), lax.axis_index("gy")
    even_x, even_y = lax.rem(xi, 2) == 0, lax.rem(yi, 2) == 0
    r, g = sz.rows, sz.groups
    for at, (ref, width) in enumerate(((x0_ref, 2), (s_ref, 2), (k_ref, 1))):
        for j in range(g):
            lane = pl.ds(j * LANES, LANES)
            low = ref[0, pl.ds(0, width), lane]
            high = ref[0, pl.ds(r - width, width), lane]
            dst = pl.ds(at * 2 * g + j * width, width)
            xe_ref[dst, :] = jnp.where(even_x, high, low)
            xo_ref[dst, :] = jnp.where(even_x, low, high)
        low = ref[0, :, pl.ds(0, LANES)].T[0:width]
        high = ref[0, :, pl.ds(sz.cols - LANES, LANES)].T[LANES - width : LANES]
        dst = pl.ds(at * 2, width)
        ye_ref[dst, :] = jnp.where(even_y, high, low)
        yo_ref[dst, :] = jnp.where(even_y, low, high)


def put_sides(sz, ref, low, high):
    width = low.shape[0]
    zeros = jnp.zeros((LANES - width, LANES), F32)
    mid = pl.ds(PAD, sz.rows)
    ref[mid, pl.ds(0, LANES)] = jnp.concatenate([zeros, low], axis=0).T
    ref[mid, pl.ds(LANES + sz.cols, LANES)] = jnp.concatenate([high, zeros], axis=0).T


def clear_bands(sz, ref):
    blank = jnp.zeros((PAD, sz.ext[1]), F32)
    ref[pl.ds(0, PAD), :] = blank
    ref[pl.ds(PAD + sz.rows, PAD), :] = blank


def gather_patches(sz, v2_ref, cols_ref, chosen_ref):
    lane = iota((BSIDE, LANES), 1)
    row = iota((PAD, LANES), 0)
    diag = row == iota((PAD, LANES), 1) // BSIDE
    per_row = sz.cols // BSIDE
    per_lanes = LANES // BSIDE
    for q in range(sz.obs * sz.reach):
        m = cols_ref[0, 0, 0, q // sz.reach, q % sz.reach]
        var, n = m // sz.blocks, lax.rem(m, sz.blocks)
        i, j = n // per_row, lax.rem(n, per_row)
        at = pl.ds(pl.multiple_of(PAD + i * BSIDE, PAD), BSIDE)
        lanes = pl.ds(pl.multiple_of(LANES + (j // per_lanes) * LANES, LANES), LANES)
        block = v2_ref[var, at, lanes]
        block = jnp.where(lane // BSIDE == lax.rem(j, per_lanes), block, 0.0)
        for step in (16, 32, 64):
            block = block + pltpu.roll(block, step, 1)
        for h in range(2):
            part = jnp.where(diag, block[h * PAD : (h + 1) * PAD], 0.0)
            chosen_ref[q // sz.reach, pl.ds(q % sz.reach, 1), pl.ds(h * LANES, LANES)] = jnp.sum(
                part, axis=0, keepdims=True
            )


def scatter_patches(sz, t_ref, cols_ref, spread_ref, sign):
    lane = iota((PAD, LANES), 1)
    row = iota((PAD, LANES), 0)
    diag = row == lane // BSIDE
    per_row = sz.cols // BSIDE
    per_lanes = LANES // BSIDE
    for q in range(sz.obs * sz.reach):
        m = cols_ref[0, 0, 0, q // sz.reach, q % sz.reach]
        var, n = m // sz.blocks, lax.rem(m, sz.blocks)
        i, j = n // per_row, lax.rem(n, per_row)
        lanes = pl.ds(pl.multiple_of((j // per_lanes) * LANES, LANES), LANES)
        here = lane // BSIDE == lax.rem(j, per_lanes)
        for h in range(2):
            line = spread_ref[q // sz.reach, pl.ds(q % sz.reach, 1), pl.ds(h * LANES, LANES)]
            part = jnp.where(diag, line, 0.0)
            for step in (16, 32, 64):
                part = part + pltpu.roll(part, step, 1)
            at = pl.ds(pl.multiple_of(i * BSIDE + h * PAD, PAD), PAD)
            t_ref[var, at, lanes] = t_ref[var, at, lanes] + sign * jnp.where(here, part, 0.0)


def start_phi(sz, phi_ref, buf_ref, sems):
    for o in range(sz.obs):
        pltpu.make_async_copy(phi_ref.at[0, 0, 0, o], buf_ref.at[o], sems.at[o]).start()


def observe_spread(sz, phi_ref, buf_ref, sems, chosen_ref, spread_ref):
    halves = (BSIDE * BSIDE) // LANES

    def body(o, carry):
        pltpu.make_async_copy(phi_ref.at[0, 0, 0, o], buf_ref.at[o], sems.at[o]).wait()
        acc = None
        for k in range(sz.reach):
            line = chosen_ref[o, pl.ds(k, 1), :]
            for h in range(halves):
                lanes = pl.ds(h * LANES, LANES)
                term = buf_ref[o, k, :, lanes] * line[:, h * LANES : (h + 1) * LANES]
                acc = term if acc is None else acc + term
        observed = jnp.sum(acc, axis=1, keepdims=True)
        for k in range(sz.reach):
            for h in range(halves):
                lanes = pl.ds(h * LANES, LANES)
                spread_ref[o, pl.ds(k, 1), lanes] = jnp.sum(
                    buf_ref[o, k, :, lanes] * observed, axis=0, keepdims=True
                )
        return carry

    lax.fori_loop(0, sz.obs, body, 0)


def smooth(sz, v2_ref, ke_ref, y_ref):
    xi, yi = lax.axis_index("gx"), lax.axis_index("gy")
    rows, cols = sz.ext
    v = v2_ref[0]
    beside = (
        pltpu.roll(v, 1, 0)
        + pltpu.roll(v, rows - 1, 0)
        + pltpu.roll(v, 1, 1)
        + pltpu.roll(v, cols - 1, 1)
    )
    y_ref[...] = (4.0 + ke_ref[...]) * v - beside

    @pl.when(xi == 0)
    def _():
        y_ref[pl.ds(0, PAD), :] = jnp.zeros((PAD, cols), F32)

    @pl.when(xi == sz.tx - 1)
    def _():
        y_ref[pl.ds(PAD + sz.rows, PAD), :] = jnp.zeros((PAD, cols), F32)

    @pl.when(yi == 0)
    def _():
        y_ref[:, pl.ds(0, LANES)] = jnp.zeros((rows, LANES), F32)

    @pl.when(yi == sz.ty - 1)
    def _():
        y_ref[:, pl.ds(LANES + sz.cols, LANES)] = jnp.zeros((rows, LANES), F32)

    inner = pl.ds(LANES, sz.cols)
    mid = y_ref[pl.ds(PAD, sz.rows), :]
    side = pltpu.roll(mid, 1, 1) + pltpu.roll(mid, cols - 1, 1)
    beside = y_ref[pl.ds(PAD - 1, sz.rows), inner] + y_ref[pl.ds(PAD + 1, sz.rows), inner]
    beside = beside + side[:, LANES : LANES + sz.cols]
    kappa = ke_ref[pl.ds(PAD, sz.rows), inner]
    return (4.0 + kappa) * mid[:, LANES : LANES + sz.cols] - beside


def device_at(sz, x, y, v):
    return (x * sz.ty + y) * 2 + v


def pack_payload(sz, t_ref, pay_ref):
    xi, yi, vi = lax.axis_index("gx"), lax.axis_index("gy"), lax.axis_index("vert")
    flat = iota((sz.head, LANES), 0) * LANES + iota((sz.head, LANES), 1)
    lane = iota((1, LANES), 1)
    vec = jnp.zeros((sz.head, LANES), F32)
    tiles = sz.tx * sz.ty
    for t in range(2):
        var = vi if t == 0 else 1 - vi
        total = jnp.zeros((1, LANES), F32)
        for a in range(sz.px):
            for j in range(sz.groups):
                seg = jnp.sum(
                    t_ref[t, pl.ds(a * PATCH, PATCH), pl.ds(j * LANES, LANES)],
                    axis=0,
                    keepdims=True,
                )
                total = total + seg
                for half in range(2):
                    keep = (lane >= PATCH) if half else (lane < PATCH)
                    value = jnp.sum(jnp.where(keep, seg, 0.0), axis=1, keepdims=True)
                    at = (
                        var * sz.per_var
                        + tiles
                        + (xi * sz.px + a) * (sz.ty * sz.py)
                        + yi * sz.py
                        + 2 * j
                        + half
                    )
                    vec = jnp.where(flat == at, value * (1.0 / sz.mid_div), vec)
        value = jnp.sum(total, axis=1, keepdims=True)
        at = var * sz.per_var + xi * sz.ty + yi
        vec = jnp.where(flat == at, value * (1.0 / sz.top_div), vec)

    def fill(s, carry):
        pay_ref[s, pl.ds(0, sz.head), :] = vec
        return carry

    lax.fori_loop(0, sz.devices, fill, 0, unroll=True if sz.devices <= 16 else 1)

    r, c = sz.rows, sz.cols
    for t in range(2):
        var = vi if t == 0 else 1 - vi
        for dx, first in ((-1, 0), (1, r - 2)):
            @pl.when((xi + dx >= 0) & (xi + dx < sz.tx))
            def _(t=t, var=var, dx=dx, first=first):
                dest = device_at(sz, xi + dx, yi, var)
                for j in range(sz.groups):
                    pay_ref[dest, pl.ds(sz.head + 2 * j, 2), :] = t_ref[
                        t, pl.ds(first, 2), pl.ds(j * LANES, LANES)
                    ]

        for dy in (-1, 1):
            @pl.when((yi + dy >= 0) & (yi + dy < sz.ty))
            def _(t=t, var=var, dy=dy):
                dest = device_at(sz, xi, yi + dy, var)
                if dy < 0:
                    pair = t_ref[t, :, pl.ds(0, LANES)].T[0:2]
                else:
                    pair = t_ref[t, :, pl.ds(c - LANES, LANES)].T[LANES - 2 : LANES]
                pay_ref[dest, pl.ds(sz.head, 2), :] = pair

            for dx in (-1, 1):
                @pl.when(
                    (xi + dx >= 0) & (xi + dx < sz.tx) & (yi + dy >= 0) & (yi + dy < sz.ty)
                )
                def _(t=t, var=var, dx=dx, dy=dy):
                    dest = device_at(sz, xi + dx, yi + dy, var)
                    lanes = pl.ds(0 if dy < 0 else c - LANES, LANES)
                    pay_ref[dest, pl.ds(sz.head, 1), :] = t_ref[
                        t, pl.ds(0 if dx < 0 else r - 1, 1), lanes
                    ]


def from_neighbour(sz, recv_ref, dx, dy, count):
    xi, yi = lax.axis_index("gx"), lax.axis_index("gy")
    x, y = xi + dx, yi + dy
    inside = (x >= 0) & (x < sz.tx) & (y >= 0) & (y < sz.ty)
    source = device_at(sz, jnp.clip(x, 0, sz.tx - 1), jnp.clip(y, 0, sz.ty - 1), 0)
    rows = pl.ds(sz.head, count)
    both = recv_ref[source, rows, :] + recv_ref[source + 1, rows, :]
    return jnp.where(inside, both, 0.0)


def first_kernel(sz, x0_ref, s_ref, k_ref, b_ref, xp_ref, he_ref, ho_ref, hye_ref, hyo_ref,
                 cols_ref, w_ref, phi_ref, t_ref, pay_ref, se_ref, ke_ref,
                 v2_ref, y_ref, chosen_ref, spread_ref, buf_ref, sems):
    start_phi(sz, phi_ref, buf_ref, sems)
    xi, yi = lax.axis_index("gx"), lax.axis_index("gy")
    even_x, even_y = lax.rem(xi, 2) == 0, lax.rem(yi, 2) == 0
    r, c, g = sz.rows, sz.cols, sz.groups
    edge = PAD * (-(-5 * g // PAD))
    lane = iota((1, LANES), 1)
    mid, inner = pl.ds(PAD, r), pl.ds(LANES, c)

    def pick(odd_ref, even_ref, rows, inside_low, inside_high, parity):
        from_e, from_o = even_ref[rows, :], odd_ref[rows, :]
        low = jnp.where(inside_low, jnp.where(parity, from_o, from_e), 0.0)
        high = jnp.where(inside_high, jnp.where(parity, from_e, from_o), 0.0)
        return low, high

    for at, (ref, src, width) in enumerate(
        ((v2_ref.at[0], x0_ref, 2), (se_ref, s_ref, 2), (ke_ref, k_ref, 1))
    ):
        clear_bands(sz, ref)
        ref[mid, inner] = src[0]
        low, high = pick(
            hyo_ref, hye_ref, pl.ds(2 * at, width), yi > 0, yi < sz.ty - 1, even_y
        )
        put_sides(sz, ref, low, high)
        for j in range(g):
            low, high = pick(
                ho_ref, he_ref, pl.ds(at * 2 * g + j * width, width),
                xi > 0, xi < sz.tx - 1, even_x,
            )
            lanes = pl.ds(LANES + j * LANES, LANES)
            ref[pl.ds(PAD - width, width), lanes] = low
            ref[pl.ds(PAD + r, width), lanes] = high
        if width == 2:
            for side in range(2):
                y_in = (yi > 0) if side == 0 else (yi < sz.ty - 1)
                beside_e = even_y if side else jnp.logical_not(even_y)
                column = 2 * at + (1 if side == 0 else 0)
                low_e, high_e = pick(
                    ho_ref, he_ref, pl.ds(edge + column, 1),
                    (xi > 0) & y_in, (xi < sz.tx - 1) & y_in, even_x,
                )
                low_o, high_o = pick(
                    ho_ref, he_ref, pl.ds(edge + PAD + column, 1),
                    (xi > 0) & y_in, (xi < sz.tx - 1) & y_in, even_x,
                )
                low = jnp.where(beside_e, low_e, low_o)
                high = jnp.where(beside_e, high_e, high_o)
                spot = lane == (LANES - 1 if side == 0 else 0)
                lanes = pl.ds(0 if side == 0 else LANES + c, LANES)
                last = jnp.sum(jnp.where(lane == LANES - 1, low, 0.0), axis=1, keepdims=True)
                ref[pl.ds(PAD - 1, 1), lanes] = jnp.where(spot, last, 0.0)
                first = jnp.sum(jnp.where(lane == 0, high, 0.0), axis=1, keepdims=True)
                ref[pl.ds(PAD + r, 1), lanes] = jnp.where(spot, first, 0.0)
    v2_ref[1, mid, inner] = xp_ref[0]
    gather_patches(sz, v2_ref, cols_ref, chosen_ref)
    observe_spread(sz, phi_ref, buf_ref, sems, chosen_ref, spread_ref)
    t_ref[0] = b_ref[0] - w_ref[0] * smooth(sz, v2_ref, ke_ref, y_ref)
    t_ref[1] = jnp.zeros((r, c), F32)
    scatter_patches(sz, t_ref, cols_ref, spread_ref, -1.0)
    pack_payload(sz, t_ref, pay_ref)


def precondition(sz, recv_ref, lg_ref, to_ref, tm_ref, se_ref, sp_ref, v2_ref, res_ref):
    r, c, g = sz.rows, sz.cols, sz.groups
    lane = iota((1, LANES), 1)
    mid, inner = pl.ds(PAD, r), pl.ds(LANES, c)

    def add_head(s, vec):
        return vec + recv_ref[s, pl.ds(0, sz.head), :]

    vec = lax.fori_loop(
        1, sz.devices, add_head, recv_ref[0, pl.ds(0, sz.head), :],
        unroll=True if sz.devices <= 16 else 1,
    )
    acc = None
    for i in range(sz.vec_rows):
        term = lg_ref[pl.ds(i * sz.lift_rows, sz.lift_rows), :] * vec[i : i + 1]
        acc = term if acc is None else acc + term
    lift = jnp.broadcast_to(jnp.sum(acc, axis=1, keepdims=True), (sz.lift_rows, LANES))

    ext = v2_ref.at[0]
    clear_bands(sz, ext)
    whole = to_ref[0] + tm_ref[1]
    res_ref[...] = whole
    ext[mid, inner] = whole
    put_sides(
        sz, ext, from_neighbour(sz, recv_ref, 0, -1, 2), from_neighbour(sz, recv_ref, 0, 1, 2)
    )
    up = from_neighbour(sz, recv_ref, -1, 0, 2 * g)
    down = from_neighbour(sz, recv_ref, 1, 0, 2 * g)
    for j in range(g):
        lanes = pl.ds(LANES + j * LANES, LANES)
        ext[pl.ds(PAD - 2, 2), lanes] = up[2 * j : 2 * j + 2]
        ext[pl.ds(PAD + r, 2), lanes] = down[2 * j : 2 * j + 2]
    for dx in (-1, 1):
        for dy in (-1, 1):
            line = from_neighbour(sz, recv_ref, dx, dy, 1)
            lanes = pl.ds(0 if dy < 0 else LANES + c, LANES)
            ext[pl.ds(PAD - 1 if dx < 0 else PAD + r, 1), lanes] = line

    bands = [(0, PAD)] + [(PAD + a * PATCH, PATCH) for a in range(sz.px)] + [(PAD + r, PAD)]
    wide = sz.py + 2
    for a, (first, count) in enumerate(bands):
        rows = pl.ds(first, count)
        for j in range(g + 2):
            lanes = pl.ds(j * LANES, LANES)
            if j == 0:
                line = lift[a * wide : a * wide + 1]
            elif j == g + 1:
                line = lift[a * wide + wide - 1 : a * wide + wide]
            else:
                at = a * wide + 2 * j - 1
                line = jnp.where(lane < PATCH, lift[at : at + 1], lift[at + 1 : at + 2])
            ext[rows, lanes] = se_ref[rows, lanes] * ext[rows, lanes] + line
    for a in range(sz.px):
        rows = pl.ds(a * PATCH, PATCH)
        for j in range(g):
            lanes = pl.ds(j * LANES, LANES)
            at = sz.ext_patches + a * sz.py + 2 * j
            line = jnp.where(lane < PATCH, lift[at : at + 1], lift[at + 1 : at + 2])
            other = tm_ref[0, rows, lanes] + to_ref[1, rows, lanes]
            v2_ref[1, pl.ds(PAD + a * PATCH, PATCH), pl.ds(LANES + j * LANES, LANES)] = (
                sp_ref[0, rows, lanes] * other + line
            )


def fold(product):
    return jnp.sum(product, axis=0, keepdims=True)


def row_dot(sz, left, right):
    line = jnp.sum(left * right, axis=0, keepdims=True)
    total = line[:, 0:LANES]
    for j in range(1, sz.groups):
        total = total + line[:, j * LANES : (j + 1) * LANES]
    return total


def apply_kernel(sz, last, recv_ref, lg_ref, to_ref, tm_ref, se_ref, ke_ref, sp_ref, cols_ref,
                 w_ref, dots_ref, phi_ref, t_ref, pay_ref, res_ref, pre_ref, out_dots_ref,
                 v2_ref, y_ref, chosen_ref, spread_ref, buf_ref, sems):
    start_phi(sz, phi_ref, buf_ref, sems)
    r, c = sz.rows, sz.cols
    mid, inner = pl.ds(PAD, r), pl.ds(LANES, c)
    precondition(sz, recv_ref, lg_ref, to_ref, tm_ref, se_ref, sp_ref, v2_ref, res_ref)
    gather_patches(sz, v2_ref, cols_ref, chosen_ref)
    observe_spread(sz, phi_ref, buf_ref, sems, chosen_ref, spread_ref)
    t_ref[0] = w_ref[0] * smooth(sz, v2_ref, ke_ref, y_ref)
    t_ref[1] = jnp.zeros((r, c), F32)
    scatter_patches(sz, t_ref, cols_ref, spread_ref, 1.0)
    own = v2_ref[0, mid, inner]
    pre_ref[...] = own
    gamma = row_dot(sz, res_ref[...], own)
    curve = row_dot(sz, own, t_ref[0]) + row_dot(sz, v2_ref[1, mid, inner], t_ref[1])
    if last:
        lines = jnp.concatenate(
            [dots_ref[0:2], gamma, curve, jnp.zeros((PAD - 4, LANES), F32)], axis=0
        )
        out_dots_ref[...] = lines

        def fill(s, carry):
            pay_ref[s] = lines
            return carry

        lax.fori_loop(0, sz.devices, fill, 0, unroll=True if sz.devices <= 16 else 1)
    else:
        out_dots_ref[...] = jnp.concatenate(
            [gamma, curve, jnp.zeros((PAD - 2, LANES), F32)], axis=0
        )
        pack_payload(sz, t_ref, pay_ref)


def final_kernel(sz, recv_ref, x0_ref, r_ref, p_ref, w_ref, z_ref, to_ref, tm_ref, x_ref, res_ref):
    def add(s, lines):
        return lines + recv_ref[s]

    lines = lax.fori_loop(
        1, sz.devices, add, recv_ref[0], unroll=True if sz.devices <= 16 else 1
    )
    sums = jnp.sum(lines, axis=1, keepdims=True)
    gamma, delta, cross, far = (sums[i : i + 1] for i in range(4))
    step = gamma / delta
    gamma_new = step * step * cross - gamma
    growth = step * cross / delta
    curve = step * step * (far - cross * cross / delta)
    step_new = gamma_new / curve
    along = step + step_new * growth
    back = step_new * step
    x_ref[0] = x0_ref[0] + (along * p_ref[...] - back * z_ref[...])
    image = to_ref[0] + tm_ref[1]
    res_ref[0] = r_ref[...] - (along * w_ref[...] - back * image)


def shape(*dims):
    return jax.ShapeDtypeStruct(dims, F32)


def work_space(sz):
    block = BSIDE * BSIDE
    return [
        pltpu.VMEM((2,) + sz.ext, F32),
        pltpu.VMEM(sz.ext, F32),
        pltpu.VMEM((sz.obs, sz.reach, block), F32),
        pltpu.VMEM((sz.obs, sz.reach, block), F32),
        pltpu.VMEM((sz.obs, sz.reach, block, block), F32),
        pltpu.SemaphoreType.DMA((sz.obs,)),
    ]


def local(right_side, initial_guess, kappa_sq, smooth_weight, precond_scale, phi_vals, phi_cols,
          coarse_slots, slot_count, coarse_rows):
    tx, ty = lax.axis_size("gx"), lax.axis_size("gy")
    xi, yi, vi = lax.axis_index("gx"), lax.axis_index("gy"), lax.axis_index("vert")
    sz = Sizes(tx, ty, right_side.shape[1:], phi_vals.shape[3], phi_vals.shape[4],
               coarse_rows.shape[2])
    swap = [(0, 1), (1, 0)]
    edge_rows = PAD * (-(-5 * sz.groups // PAD))

    def paired(axis_size, k):
        return [(i, i ^ k) for i in range(axis_size)]

    def even_pairs(n):
        return [(i, i ^ 1) for i in range(n)]

    def odd_pairs(n):
        return [(i, (i + 1) % n if i % 2 else (i - 1) % n) for i in range(n)]

    x_partner = lax.ppermute(initial_guess, "vert", swap)
    s_partner = lax.ppermute(precond_scale, "vert", swap)

    xe, xo, ye, yo = pl.pallas_call(
        functools.partial(pack_edges, sz),
        out_shape=[shape(edge_rows, LANES)] * 2 + [shape(PAD, LANES)] * 2,
        in_specs=[VMEM] * 3,
        out_specs=[VMEM] * 4,
        compiler_params=PARAMS,
    )(initial_guess, precond_scale, kappa_sq)

    hye = lax.ppermute(ye, "gy", even_pairs(ty))
    hyo = lax.ppermute(yo, "gy", odd_pairs(ty)) if ty > 2 else hye

    ids = jnp.asarray(lift_ids(sz))[xi, yi, vi]
    ids = ids.reshape(2, tx * sz.lift_rows, 1)
    live = jnp.arange(coarse_slots.shape[1], dtype=jnp.int32) < slot_count[0]
    slots = jnp.where(live, coarse_slots[0], -2)[None, :]
    select = jnp.where(ids[0] == slots, 1.0 / sz.mid_div, 0.0) + jnp.where(
        ids[1] == slots, 1.0 / sz.top_div, 0.0
    )
    cleaned = jnp.where(live[:, None], coarse_rows[0], 0.0)
    padded = jnp.pad(cleaned, ((0, 0), (0, sz.vec_rows * LANES - sz.nco)))
    shares = jnp.dot(select, padded, precision=lax.Precision.HIGHEST)
    shares = shares.reshape(tx, sz.lift_rows, sz.vec_rows, LANES).transpose(0, 2, 1, 3)
    shares = shares.reshape(tx, sz.vec_rows * sz.lift_rows, LANES)
    messages = {}
    for k in range(1, tx):
        messages.setdefault(tuple(paired(tx, k)), []).append(("g", shares[k]))
    messages.setdefault(tuple(even_pairs(tx)), []).append(
        ("e", jnp.concatenate([xe, hye, hyo], axis=0))
    )
    messages.setdefault(tuple(odd_pairs(tx)), []).append(
        ("o", jnp.concatenate([xo, hye, hyo], axis=0))
    )
    lift_matrix = shares[0]
    edges = {}
    for perm, parts in messages.items():
        whole = parts[0][1] if len(parts) == 1 else jnp.concatenate([p[1] for p in parts], axis=0)
        got = lax.ppermute(whole, "gx", list(perm))
        at = 0
        for kind, part in parts:
            piece = got[at : at + part.shape[0]]
            at += part.shape[0]
            if kind == "g":
                lift_matrix = lift_matrix + piece
            else:
                edges[kind] = piece

    r, c = sz.rows, sz.cols
    pair = shape(2, r, c)
    payload = shape(sz.devices, sz.head + PAD, LANES)
    parts, sent, s_ext, k_ext = pl.pallas_call(
        functools.partial(first_kernel, sz),
        out_shape=[pair, payload, shape(*sz.ext), shape(*sz.ext)],
        in_specs=[VMEM] * 9 + [SMEM, SMEM, ANY],
        out_specs=[VMEM] * 4,
        scratch_shapes=work_space(sz),
        compiler_params=PARAMS,
    )(initial_guess, precond_scale, kappa_sq, right_side, x_partner, edges["e"], edges["o"],
      hye, hyo, phi_cols, smooth_weight, phi_vals)

    def exchange(array):
        return lax.all_to_all(array, ALL, 0, 0, tiled=True)

    def apply(last, received, parts, mirrored, dots):
        return pl.pallas_call(
            functools.partial(apply_kernel, sz, last),
            out_shape=[pair, shape(sz.devices, PAD, LANES) if last else payload,
                       shape(r, c), shape(r, c), shape(PAD, LANES)],
            in_specs=[VMEM] * 7 + [SMEM, SMEM, VMEM, ANY],
            out_specs=[VMEM] * 5,
            scratch_shapes=work_space(sz),
            compiler_params=PARAMS,
        )(received, lift_matrix, parts, mirrored, s_ext, k_ext, s_partner, phi_cols,
          smooth_weight, dots, phi_vals)

    dots = jnp.zeros((PAD, LANES), F32)
    mirrored = lax.ppermute(parts, "vert", swap)
    parts, sent, residual, precond, dots = apply(False, exchange(sent), parts, mirrored, dots)
    mirrored = lax.ppermute(parts, "vert", swap)
    parts, sent, image, second, dots = apply(True, exchange(sent), parts, mirrored, dots)
    mirrored = lax.ppermute(parts, "vert", swap)
    return tuple(pl.pallas_call(
        functools.partial(final_kernel, sz),
        out_shape=[shape(1, r, c)] * 2,
        in_specs=[VMEM] * 8,
        out_specs=[VMEM] * 2,
        compiler_params=PARAMS,
    )(exchange(sent), initial_guess, residual, precond, image, second, parts, mirrored))


def solution(mesh):
    return jax.shard_map(
        local,
        mesh=mesh,
        in_specs=(
            P(("groups", "vert"), "gx", "gy"),
            P(("groups", "vert"), "gx", "gy"),
            P(("groups", "vert"), "gx", "gy"),
            P(("groups", "vert")),
            P(("groups", "vert"), "gx", "gy"),
            P(("groups", "vert"), "gx", "gy", None, None, None, None),
            P(("groups", "vert"), "gx", "gy", None, None),
            P(("groups", "gx"), None),
            P(("groups", "gx")),
            P(("groups", "gx"), None, None),
        ),
        out_specs=(P(("groups", "vert"), "gx", "gy"), P(("groups", "vert"), "gx", "gy")),
        check_vma=False,
    )
```

profile of v0, /device:TPU:0, one launch (start us, length us, event | category | flops | bytes accessed | tf_op | source)
XLA Modules:
  0.0 85.6 jit_solution(13774917986096929577)
XLA Ops:
  1.1 0.9 %copy-done.2 = f32[1,128,512]{2,1,0:T(8,128)S(1)} copy-done((f32[1,128,512]{2,1,0:T(8,128)S(1)}, f32[1,128,512]{2,1,0:T(8,128)}, u32[]{:S(2)}) %copy-start.2) | copy-done | bytes 262168
  2.1 0.9 %copy-done.5 = f32[1,128,512]{2,1,0:T(8,128)S(1)} copy-done((f32[1,128,512]{2,1,0:T(8,128)S(1)}, f32[1,128,512]{2,1,0:T(8,128)}, u32[]{:S(2)}) %copy-start.5) | copy-done | bytes 262168
  3.0 1.7 %shard_map.122 = (f32[24,128]{1,0:T(8,128)S(1)}, f32[24,128]{1,0:T(8,128)S(1)}, f32[8,128]{1,0:T(8,128)S(1)}, f32[8,128]{1,0:T(8,128)}) custom-call(f32[1,128,512]{2,1,0:T(8,128)S(1)} %copy-done.2, f32[1,128,512]{2,1,0:T(8,128)} %s_ref.3, f32[1,128,512]{2,1,0:T(8,128)S(1)} %copy-done.5), custom_call_target="tpu_custom_call" | custom-call | tf_op jit(solution)/shard_map/pallas_call | solution.py:538
  4.8 2.5 %collective-permute-start.1 = (f32[8,128]{1,0:T(8,128)S(1)}, f32[8,128]{1,0:T(8,128)S(1)}, u32[]{:S(2)}, u32[]{:S(2)}) collective-permute-start(f32[8,128]{1,0:T(8,128)S(1)} %get-tuple-element.19), channel_id=1, source_target_pairs={{0,2},{2,0},{1,3},{3,1},{4,6},{6,4},{5,7},{7,5},{8,10},{10,8},{9,1... | collective-permute-start | bytes 12296 | tf_op jit(solution)/shard_map/ppermute | solution.py:546
  7.9 0.7 constant_dynamic-slice_fusion
  9.5 1.0 %bitcast_select_fusion = f32[136,272]{1,0:T(8,128)S(1)} fusion(f32[1,136,272]{2,1,0:T(8,128)} %param.20, pred[136]{0:T(512)(128)(4,1)S(1)} %iota_compare_fusion), kind=kLoop, calls=%fused_computation.6 | loop fusion | flops 36992 | bytes 296072 | tf_op jit(solution)/shard_map/jit(_where)/select_n | solution.py:556
  11.4 3.7 %collective-permute-start.3 = (f32[208,128]{1,0:T(8,128)S(1)}, f32[208,128]{1,0:T(8,128)S(1)}, u32[]{:S(2)}, u32[]{:S(2)}) collective-permute-start(f32[208,128]{1,0:T(8,128)S(1)} %get-tuple-element.40), channel_id=1, source_target_pairs={{0,12},{4,8},{8,4},{12,0},{1,13},{5,9},{9,5},{13,1},{2,14},{6,10},... | collective-permute-start | bytes 319496 | tf_op jit(solution)/shard_map/ppermute | solution.py:574
  15.7 0.8 copy.19.cols_ref
  16.5 2.6 %collective-permute-done.3 = f32[208,128]{1,0:T(8,128)S(1)} collective-permute-done((f32[208,128]{1,0:T(8,128)S(1)}, f32[208,128]{1,0:T(8,128)S(1)}, u32[]{:S(2)}, u32[]{:S(2)}) %collective-permute-start.3) | collective-permute-done | bytes 106528 | tf_op jit(solution)/shard_map/ppermute | solution.py:574
  19.1 1.7 %collective-permute-done.2 = f32[208,128]{1,0:T(8,128)S(1)} collective-permute-done((f32[208,128]{1,0:T(8,128)S(1)}, f32[208,128]{1,0:T(8,128)S(1)}, u32[]{:S(2)}, u32[]{:S(2)}) %collective-permute-start.2) | collective-permute-done | bytes 106528 | tf_op jit(solution)/shard_map/ppermute | solution.py:574
  20.8 3.4 %copy-done = f32[1,1,1,16,2,256,256]{6,5,4,3,2,1,0:T(8,128)S(1)} copy-done((f32[1,1,1,16,2,256,256]{6,5,4,3,2,1,0:T(8,128)S(1)}, f32[1,1,1,16,2,256,256]{6,5,4,3,2,1,0:T(8,128)}, u32[]{:S(2)}) %copy-start) | copy-done | bytes 8388632
  24.2 0.9 %copy-done.3 = f32[1,128,512]{2,1,0:T(8,128)S(1)} copy-done((f32[1,128,512]{2,1,0:T(8,128)S(1)}, f32[1,128,512]{2,1,0:T(8,128)}, u32[]{:S(2)}) %copy-start.3) | copy-done | bytes 262168
  25.2 0.9 %copy-done.6 = f32[1,128,512]{2,1,0:T(8,128)S(1)} copy-done((f32[1,128,512]{2,1,0:T(8,128)S(1)}, f32[1,128,512]{2,1,0:T(8,128)}, u32[]{:S(2)}) %copy-start.6) | copy-done | bytes 262168
  26.1 0.9 %copy-done.7 = f32[1,128,512]{2,1,0:T(8,128)S(1)} copy-done((f32[1,128,512]{2,1,0:T(8,128)S(1)}, f32[1,128,512]{2,1,0:T(8,128)}, u32[]{:S(2)}) %copy-start.7) | copy-done | bytes 262168
  27.1 8.1 %shard_map.123 = (f32[2,128,512]{2,1,0:T(8,128)S(1)}, f32[16,16,128]{2,1,0:T(8,128)}, f32[144,768]{1,0:T(8,128)S(1)}, f32[144,768]{1,0:T(8,128)S(1)}) custom-call(f32[1,128,512]{2,1,0:T(8,128)S(1)} %copy-done.3, f32[1,128,512]{2,1,0:T(8,128)} %s_ref.3, f32[1,128,512]{2,1,0:T(8,128)S(1)} %copy-done.6, f32[1,128,512]{2,1,0:T(8,128)S(1)} %copy-done.7, ...), custom_call_target="tpu_custom_call" | custom-call | tf_op jit(solution)/shard_map/pallas_call | solution.py:587
  36.0 4.9 %all-to-all-start = ((f32[16,16,128]{2,1,0:T(8,128)}), f32[16,16,128]{2,1,0:T(8,128)S(1)}, u32[]{:S(2)}, u32[]{:S(2)}) async-start(f32[16,16,128]{2,1,0:T(8,128)} %get-tuple-element.21), calls=%async_computation | async-start | bytes 262144 | tf_op jit(solution)/shard_map/all_to_all | solution.py:598
  41.0 2.0 %collective-permute-done.4 = f32[168,128]{1,0:T(8,128)S(1)} collective-permute-done((f32[168,128]{1,0:T(8,128)S(1)}, f32[168,128]{1,0:T(8,128)S(1)}, u32[]{:S(2)}, u32[]{:S(2)}) %collective-permute-start.4) | collective-permute-done | bytes 86048 | tf_op jit(solution)/shard_map/ppermute | solution.py:574
  43.0 5.9 %all-to-all-done.recv_ref = f32[16,16,128]{2,1,0:T(8,128)S(1)} async-done(((f32[16,16,128]{2,1,0:T(8,128)}), f32[16,16,128]{2,1,0:T(8,128)S(1)}, u32[]{:S(2)}, u32[]{:S(2)}) %all-to-all-start) | async-done | bytes 131104 | tf_op jit(solution)/shard_map/all_to_all | solution.py:598
  48.9 3.4 %copy-done.1 = f32[1,1,1,16,2,256,256]{6,5,4,3,2,1,0:T(8,128)S(1)} copy-done((f32[1,1,1,16,2,256,256]{6,5,4,3,2,1,0:T(8,128)S(1)}, f32[1,1,1,16,2,256,256]{6,5,4,3,2,1,0:T(8,128)}, u32[]{:S(2)}) %copy-start.1) | copy-done | bytes 8388632
  52.3 5.9 %shard_map.124 = (f32[2,128,512]{2,1,0:T(8,128)S(1)}, f32[16,16,128]{2,1,0:T(8,128)S(1)}, f32[128,512]{1,0:T(8,128)S(1)}, f32[128,512]{1,0:T(8,128)S(1)}, f32[8,128]{1,0:T(8,128)S(1)}) custom-call(f32[16,16,128]{2,1,0:T(8,128)S(1)} %all-to-all-done.recv_ref, f32[168,128]{1,0:T(8,128)S(1)} %slice_add_fusion.lg_ref, ...), custom_call_target="tpu_custom_call" | custom-call | tf_op jit(solution)/shard_map/pallas_call | solution.py:601
  58.3 10.5 %all_to_all.15.recv_ref = f32[16,16,128]{2,1,0:T(8,128)S(1)} all-to-all(f32[16,16,128]{2,1,0:T(8,128)S(1)} %get-tuple-element.25), channel_id=1, replica_groups=mesh['groups'=2,'gx'=4,'gy'=2,'vert'=2] {'gx','gy','vert'}, dimensions={0} | all-to-all | bytes 262144 | tf_op jit(solution)/shard_map/all_to_all | solution.py:598
  68.8 6.2 %shard_map.125 = (f32[2,128,512]{2,1,0:T(8,128)S(1)}, f32[16,8,128]{2,1,0:T(8,128)S(1)}, f32[128,512]{1,0:T(8,128)S(1)}, f32[128,512]{1,0:T(8,128)S(1)}, f32[8,128]{1,0:T(8,128)}) custom-call(f32[16,16,128]{2,1,0:T(8,128)S(1)} %all_to_all.15.recv_ref, f32[168,128]{1,0:T(8,128)S(1)} %slice_add_fusion.lg_ref, f32[2,128,512]{2,1,0:T(8,128)S(1)} %get-tuple-element.26.to_ref, ...), custom_call_target="tpu_custom_call" | custom-call | tf_op jit(solution)/shard_map/pallas_call | solution.py:601
  75.1 9.5 %all_to_all.16.recv_ref = f32[16,8,128]{2,1,0:T(8,128)S(1)} all-to-all(f32[16,8,128]{2,1,0:T(8,128)S(1)} %get-tuple-element.28), channel_id=1, replica_groups=mesh['groups'=2,'gx'=4,'gy'=2,'vert'=2] {'gx','gy','vert'}, dimensions={0} | all-to-all | bytes 131072 | tf_op jit(solution)/shard_map/all_to_all | solution.py:598
  84.6 1.0 %shard_map.126 = (f32[1,128,512]{2,1,0:T(8,128)}, f32[1,128,512]{2,1,0:T(8,128)}) custom-call(f32[16,8,128]{2,1,0:T(8,128)S(1)} %all_to_all.16.recv_ref, f32[1,128,512]{2,1,0:T(8,128)S(1)} %copy-done.4, f32[128,512]{1,0:T(8,128)S(1)} %get-tuple-element.29.r_ref, f32[128,512]{1,0:T(8,128)S(1)} %get-tuple-element.30.p_ref, ...), custom_call_target="tpu_custom_call" | custom-call | tf_op jit(solution)/shard_map/pallas_call | solution.py:618
  (38 shorter events, 3.3 us)
Async XLA Ops:
  0.6 20.2 %collective-permute-start = (f32[1,128,512]{2,1,0:T(8,128)}, f32[1,128,512]{2,1,0:T(8,128)S(1)}, u32[]{:S(2)}, u32[]{:S(2)}) collective-permute-start(f32[1,128,512]{2,1,0:T(8,128)} %x0_ref.5), channel_id=1, source_target_pairs={{0,1},{1,0},{2,3},{3,2},{4,5},{5,4},{6,7},{7,6},{8,9},{9,8},{10,11... | collective-permute-start | bytes 786440 | tf_op jit(solution)/shard_map/ppermute | solution.py:535
  1.1 0.9 %copy-start.2 = (f32[1,128,512]{2,1,0:T(8,128)S(1)}, f32[1,128,512]{2,1,0:T(8,128)}, u32[]{:S(2)}) copy-start(f32[1,128,512]{2,1,0:T(8,128)} %x0_ref.5) | copy-start | bytes 786436
  2.1 0.9 %copy-start.5 = (f32[1,128,512]{2,1,0:T(8,128)S(1)}, f32[1,128,512]{2,1,0:T(8,128)}, u32[]{:S(2)}) copy-start(f32[1,128,512]{2,1,0:T(8,128)} %k_ref.3) | copy-start | bytes 786436
  4.8 6.6 %collective-permute-start.1 = (f32[8,128]{1,0:T(8,128)S(1)}, f32[8,128]{1,0:T(8,128)S(1)}, u32[]{:S(2)}, u32[]{:S(2)}) collective-permute-start(f32[8,128]{1,0:T(8,128)S(1)} %get-tuple-element.19), channel_id=1, source_target_pairs={{0,2},{2,0},{1,3},{3,1},{4,6},{6,4},{5,7},{7,5},{8,10},{10,8},{9,1... | collective-permute-start | bytes 12296 | tf_op jit(solution)/shard_map/ppermute | solution.py:546
  11.4 7.7 %collective-permute-start.3 = (f32[208,128]{1,0:T(8,128)S(1)}, f32[208,128]{1,0:T(8,128)S(1)}, u32[]{:S(2)}, u32[]{:S(2)}) collective-permute-start(f32[208,128]{1,0:T(8,128)S(1)} %get-tuple-element.40), channel_id=1, source_target_pairs={{0,12},{4,8},{8,4},{12,0},{1,13},{5,9},{9,5},{13,1},{2,14},{6,10},... | collective-permute-start | bytes 319496 | tf_op jit(solution)/shard_map/ppermute | solution.py:574
  15.1 5.7 %collective-permute-start.2 = (f32[208,128]{1,0:T(8,128)S(1)}, f32[208,128]{1,0:T(8,128)S(1)}, u32[]{:S(2)}, u32[]{:S(2)}) collective-permute-start(f32[208,128]{1,0:T(8,128)S(1)} %get-tuple-element.41), channel_id=1, source_target_pairs={{0,4},{4,0},{8,12},{12,8},{1,5},{5,1},{9,13},{13,9},{2,6},{6,2},{1... | collective-permute-start | bytes 319496 | tf_op jit(solution)/shard_map/ppermute | solution.py:574
  20.8 3.4 %copy-start = (f32[1,1,1,16,2,256,256]{6,5,4,3,2,1,0:T(8,128)S(1)}, f32[1,1,1,16,2,256,256]{6,5,4,3,2,1,0:T(8,128)}, u32[]{:S(2)}) copy-start(f32[1,1,1,16,2,256,256]{6,5,4,3,2,1,0:T(8,128)} %phi_ref.5) | copy-start | bytes 25165828
  24.2 0.9 %copy-start.3 = (f32[1,128,512]{2,1,0:T(8,128)S(1)}, f32[1,128,512]{2,1,0:T(8,128)}, u32[]{:S(2)}) copy-start(f32[1,128,512]{2,1,0:T(8,128)} %x0_ref.5) | copy-start | bytes 786436
  25.1 0.9 %copy-start.6 = (f32[1,128,512]{2,1,0:T(8,128)S(1)}, f32[1,128,512]{2,1,0:T(8,128)}, u32[]{:S(2)}) copy-start(f32[1,128,512]{2,1,0:T(8,128)} %k_ref.3) | copy-start | bytes 786436
  26.1 0.9 %copy-start.7 = (f32[1,128,512]{2,1,0:T(8,128)S(1)}, f32[1,128,512]{2,1,0:T(8,128)}, u32[]{:S(2)}) copy-start(f32[1,128,512]{2,1,0:T(8,128)} %b_ref.1) | copy-start | bytes 786436
  35.2 13.7 %collective-permute-start.5 = (f32[2,128,512]{2,1,0:T(8,128)S(1)}, f32[2,128,512]{2,1,0:T(8,128)S(1)}, u32[]{:S(2)}, u32[]{:S(2)}) collective-permute-start(f32[2,128,512]{2,1,0:T(8,128)S(1)} %get-tuple-element.22.to_ref), channel_id=1, source_target_pairs={{0,1},{1,0},{2,3},{3,2},{4,5},{5,4},{6,7},{7,6},{8,9},{9,8},{10,11... | collective-permute-start | bytes 1572872 | tf_op jit(solution)/shard_map/ppermute | solution.py:613
  35.3 7.7 %collective-permute-start.4 = (f32[168,128]{1,0:T(8,128)S(1)}, f32[168,128]{1,0:T(8,128)S(1)}, u32[]{:S(2)}, u32[]{:S(2)}) collective-permute-start(f32[168,128]{1,0:T(8,128)S(1)} %bitcast.15), channel_id=1, source_target_pairs={{0,8},{4,12},{8,0},{12,4},{1,9},{5,13},{9,1},{13,5},{2,10},{6,14},... | collective-permute-start | bytes 258056 | tf_op jit(solution)/shard_map/ppermute | solution.py:574
  35.9 7.1 %collective-permute-start.6 = (f32[1,128,512]{2,1,0:T(8,128)}, f32[1,128,512]{2,1,0:T(8,128)S(1)}, u32[]{:S(2)}, u32[]{:S(2)}) collective-permute-start(f32[1,128,512]{2,1,0:T(8,128)} %s_ref.3), channel_id=1, source_target_pairs={{0,1},{1,0},{2,3},{3,2},{4,5},{5,4},{6,7},{7,6},{8,9},{9,8},{10,11... | collective-permute-start | bytes 786440 | tf_op jit(solution)/shard_map/ppermute | solution.py:536
  36.0 12.9 %all-to-all-start = ((f32[16,16,128]{2,1,0:T(8,128)}), f32[16,16,128]{2,1,0:T(8,128)S(1)}, u32[]{:S(2)}, u32[]{:S(2)}) async-start(f32[16,16,128]{2,1,0:T(8,128)} %get-tuple-element.21), calls=%async_computation | async-start | bytes 262144 | tf_op jit(solution)/shard_map/all_to_all | solution.py:598
  48.9 3.4 %copy-start.1 = (f32[1,1,1,16,2,256,256]{6,5,4,3,2,1,0:T(8,128)S(1)}, f32[1,1,1,16,2,256,256]{6,5,4,3,2,1,0:T(8,128)}, u32[]{:S(2)}) copy-start(f32[1,1,1,16,2,256,256]{6,5,4,3,2,1,0:T(8,128)} %phi_ref.5) | copy-start | bytes 25165828
  52.3 32.3 %copy-start.4 = (f32[1,128,512]{2,1,0:T(8,128)S(1)}, f32[1,128,512]{2,1,0:T(8,128)}, u32[]{:S(2)}) copy-start(f32[1,128,512]{2,1,0:T(8,128)} %x0_ref.5) | copy-start | bytes 786436
  58.2 10.6 %collective-permute-start.7 = (f32[2,128,512]{2,1,0:T(8,128)S(1)}, f32[2,128,512]{2,1,0:T(8,128)S(1)}, u32[]{:S(2)}, u32[]{:S(2)}) collective-permute-start(f32[2,128,512]{2,1,0:T(8,128)S(1)} %get-tuple-element.26.to_ref), channel_id=1, source_target_pairs={{0,1},{1,0},{2,3},{3,2},{4,5},{5,4},{6,7},{7,6},{8,9},{9,8},{10,11... | collective-permute-start | bytes 1572872 | tf_op jit(solution)/shard_map/ppermute | solution.py:615
  75.0 9.6 %collective-permute-start.8 = (f32[2,128,512]{2,1,0:T(8,128)S(1)}, f32[2,128,512]{2,1,0:T(8,128)S(1)}, u32[]{:S(2)}, u32[]{:S(2)}) collective-permute-start(f32[2,128,512]{2,1,0:T(8,128)S(1)} %get-tuple-element.33.to_ref), channel_id=1, source_target_pairs={{0,1},{1,0},{2,3},{3,2},{4,5},{5,4},{6,7},{7,6},{8,9},{9,8},{10,11... | collective-permute-start | bytes 1572872 | tf_op jit(solution)/shard_map/ppermute | solution.py:617
where the time goes:
time: 86.3 us; the launch traced here: 85.6 us
  Pallas kernels  23 us (27%)
  blocking collectives  20 us (23%)
  local copies, waits for them, and re-layouts  13.4 us (16%)
  starting transfers between devices  12.6 us (15%)
  waiting for transfers between devices  12.2 us (14%)
  between operations  2.1 us (2%)
  other arithmetic  1.76 us (2%)
    all_to_all x2, blocking collectives, exchange(): return lax.all_to_all(array, ALL, 0, 0, tiled=True)  20 us
    unnamed x17, local copies, waits for them, and re-layouts  12.3 us
    pallas_call x2, Pallas kernels, apply(): pl.pallas_call(functools.partial(apply_kernel, sz, last), out_shape=[pair...  12.1 us
    pallas_call x1, Pallas kernels, local(): pl.pallas_call(functools.partial(first_kernel, sz), out_shape=[pair, payl...  8.15 us
    ppermute x3, waiting for transfers between devices, local(): got = lax.ppermute(whole, 'gx', list(perm))  6.31 us
    all_to_all x1, waiting for transfers between devices, exchange(): return lax.all_to_all(array, ALL, 0, 0, tiled=True)  5.88 us
    all_to_all x1, starting transfers between devices, exchange(): return lax.all_to_all(array, ALL, 0, 0, tiled=True)  4.91 us
    ppermute x3, starting transfers between devices, local(): got = lax.ppermute(whole, 'gx', list(perm))  4.25 us
  transfers between devices with their start and end apart: 10, of which 4 were waited for; matrix products, arithmetic and copies ran while one was open for 5% of the time, Pallas kernels for 2%

commit v1 on v0

v1 whole, which is shorter than its diff:
```python
import functools
import math

import jax
import jax.numpy as jnp
from jax import lax
from jax.experimental import pallas as pl
from jax.experimental.pallas import tpu as pltpu
from jax.sharding import PartitionSpec as P

BSIDE = 16
PATCH = 64
LANES = 128
PAD = 8
ALL = ("gx", "gy", "vert")
FIELDS = ((0, 2), (1, 2), (2, 1))
F32 = jnp.float32
VMEM = pl.BlockSpec(memory_space=pltpu.VMEM)
SMEM = pl.BlockSpec(memory_space=pltpu.SMEM)
ANY = pl.BlockSpec(memory_space=pl.ANY)
PARAMS = pltpu.CompilerParams(vmem_limit_bytes=20 * 1024 * 1024)
EDGE_PARAMS = pltpu.CompilerParams(vmem_limit_bytes=58 * 1024 * 1024)
DATA_PARAMS = pltpu.CompilerParams(vmem_limit_bytes=50 * 1024 * 1024)


class Sizes:
    def __init__(self, tx, ty, tile_shape, obs, reach, nco):
        self.tx, self.ty = tx, ty
        self.rows, self.cols = tile_shape
        self.obs, self.reach = obs, reach
        self.nco = nco
        self.px, self.py = self.rows // PATCH, self.cols // PATCH
        self.groups = self.cols // LANES
        self.ext = (self.rows + 2 * PAD, self.cols + 2 * LANES)
        self.devices = tx * ty * 2
        self.per_var = tx * ty * (1 + self.px * self.py)
        self.vec_rows = -(-nco // LANES)
        self.head = PAD * (-(-(self.vec_rows + 1) // PAD))
        self.ext_patches = (self.px + 2) * (self.py + 2)
        self.lift_rows = PAD * (-(-(self.ext_patches + self.px * self.py) // PAD))
        self.blocks = (self.rows // BSIDE) * (self.cols // BSIDE)
        self.top_div = math.sqrt(self.rows * self.cols)
        self.mid_div = float(PATCH)


def iota(shape, dim):
    return lax.broadcasted_iota(jnp.int32, shape, dim)


def lift_ids(sz, xt):
    yi, vi = lax.axis_index("gy"), lax.axis_index("vert")
    at = iota((sz.lift_rows, 1), 0)
    wide, tiles = sz.py + 2, sz.tx * sz.ty

    def steps(index, width, count):
        total = jnp.zeros_like(index)
        for a in range(1, count):
            total = total + jnp.where(index >= a * width, 1, 0)
        return total

    band = steps(at, wide, sz.px + 2)
    spot = at - band * wide
    gi, gj = xt * sz.px + band - 1, yi * sz.py + spot - 1
    near_x = xt - jnp.where(band == 0, 1, 0) + jnp.where(band == sz.px + 1, 1, 0)
    near_y = yi - jnp.where(spot == 0, 1, 0) + jnp.where(spot == sz.py + 1, 1, 0)
    inside = (near_x >= 0) & (near_x < sz.tx) & (near_y >= 0) & (near_y < sz.ty)
    mid = vi * sz.per_var + tiles + gi * (sz.ty * sz.py) + gj
    top = vi * sz.per_var + near_x * sz.ty + near_y
    mid, top = jnp.where(inside, mid, -1), jnp.where(inside, top, -1)
    rest = at - sz.ext_patches
    band = steps(rest, sz.py, sz.px)
    other = (1 - vi) * sz.per_var
    place = (xt * sz.px + band) * (sz.ty * sz.py) + yi * sz.py + rest - band * sz.py
    last = sz.ext_patches + sz.px * sz.py
    own = at < sz.ext_patches
    mid = jnp.where(own, mid, jnp.where(at < last, other + tiles + place, -1))
    top = jnp.where(own, top, jnp.where(at < last, other + xt * sz.ty + yi, -1))
    return mid, top


def share_rows(sz, slots_ref, count_ref, rows_ref, outs):
    slots = slots_ref[...]
    live = iota(slots.shape, 1) < count_ref[0]
    slots = jnp.where(live, slots, -2)
    for k, out_ref in enumerate(outs):
        mid, top = lift_ids(sz, lax.bitwise_xor(lax.axis_index("gx"), k))
        select = jnp.where(mid == slots, 1.0 / sz.mid_div, 0.0) + jnp.where(
            top == slots, 1.0 / sz.top_div, 0.0
        )
        share = jnp.dot(
            select, rows_ref[...], precision=lax.Precision.HIGHEST, preferred_element_type=F32
        )
        for i in range(sz.vec_rows):
            part = share[:, i * LANES : min((i + 1) * LANES, sz.nco)]
            if part.shape[1] < LANES:
                blank = jnp.zeros((sz.lift_rows, LANES - part.shape[1]), F32)
                part = jnp.concatenate([part, blank], axis=1)
            out_ref[pl.ds(i * sz.lift_rows, sz.lift_rows), :] = part


def setup_kernel(sz, x0_ref, s_ref, k_ref, rows_ref, slots_ref, count_ref, pay_ref, *refs):
    outs, (tiles_ref, held_ref, sems) = refs[: sz.tx], refs[sz.tx :]
    copies = [
        pltpu.make_async_copy(ref.at[0], tiles_ref.at[at], sems.at[at])
        for at, ref in enumerate((x0_ref, s_ref, k_ref))
    ]
    copies = [pltpu.make_async_copy(rows_ref.at[0], held_ref, sems.at[3])] + copies
    for copy in copies:
        copy.start()
    copies[0].wait()
    share_rows(sz, slots_ref, count_ref, held_ref, outs)
    for copy in copies[1:]:
        copy.wait()
    xi, yi, vi = lax.axis_index("gx"), lax.axis_index("gy"), lax.axis_index("vert")
    r, c, g = sz.rows, sz.cols, sz.groups
    for dx in (-1, 1):
        @pl.when((xi + dx >= 0) & (xi + dx < sz.tx))
        def _(dx=dx):
            dest = device_at(sz, xi + dx, yi, vi)
            for at, width in FIELDS:
                rows = pl.ds(0 if dx < 0 else r - width, width)
                for j in range(g):
                    pay_ref[dest, pl.ds(at * 2 * g + j * width, width), :] = tiles_ref[
                        at, rows, pl.ds(j * LANES, LANES)
                    ]

    for dy in (-1, 1):
        @pl.when((yi + dy >= 0) & (yi + dy < sz.ty))
        def _(dy=dy):
            dest = device_at(sz, xi, yi + dy, vi)
            lanes = pl.ds(0 if dy < 0 else c - LANES, LANES)
            for at, width in FIELDS:
                first = 0 if dy < 0 else LANES - width
                pay_ref[dest, pl.ds(at * 2 * g, width), :] = tiles_ref[at, :, lanes].T[
                    first : first + width
                ]

        for dx in (-1, 1):
            @pl.when((xi + dx >= 0) & (xi + dx < sz.tx) & (yi + dy >= 0) & (yi + dy < sz.ty))
            def _(dx=dx, dy=dy):
                dest = device_at(sz, xi + dx, yi + dy, vi)
                lanes = pl.ds(0 if dy < 0 else c - LANES, LANES)
                rows = pl.ds(0 if dx < 0 else r - 1, 1)
                for at, width in FIELDS:
                    if width == 2:
                        pay_ref[dest, pl.ds(at * 2 * g, 1), :] = tiles_ref[at, rows, lanes]


def put_sides(sz, ref, low, high):
    width = low.shape[0]
    zeros = jnp.zeros((LANES - width, LANES), F32)
    mid = pl.ds(PAD, sz.rows)
    ref[mid, pl.ds(0, LANES)] = jnp.concatenate([zeros, low], axis=0).T
    ref[mid, pl.ds(LANES + sz.cols, LANES)] = jnp.concatenate([high, zeros], axis=0).T


def clear_bands(sz, ref):
    blank = jnp.zeros((PAD, sz.ext[1]), F32)
    ref[pl.ds(0, PAD), :] = blank
    ref[pl.ds(PAD + sz.rows, PAD), :] = blank


def put_corners(sz, ref, beside):
    for dx in (-1, 1):
        for dy in (-1, 1):
            lanes = pl.ds(0 if dy < 0 else LANES + sz.cols, LANES)
            ref[pl.ds(PAD - 1 if dx < 0 else PAD + sz.rows, 1), lanes] = beside(dx, dy, 1)


def gather_patches(sz, v2_ref, cols_ref, chosen_ref):
    lane = iota((BSIDE, LANES), 1)
    row = iota((PAD, LANES), 0)
    diag = row == iota((PAD, LANES), 1) // BSIDE
    per_row = sz.cols // BSIDE
    per_lanes = LANES // BSIDE
    for q in range(sz.obs * sz.reach):
        m = cols_ref[0, 0, 0, q // sz.reach, q % sz.reach]
        var, n = m // sz.blocks, lax.rem(m, sz.blocks)
        i, j = n // per_row, lax.rem(n, per_row)
        at = pl.ds(pl.multiple_of(i * BSIDE, BSIDE), BSIDE)
        lanes = pl.ds(pl.multiple_of((j // per_lanes) * LANES, LANES), LANES)
        block = v2_ref[var, at, lanes]
        block = jnp.where(lane // BSIDE == lax.rem(j, per_lanes), block, 0.0)
        for step in (16, 32, 64):
            block = block + pltpu.roll(block, step, 1)
        for h in range(2):
            part = jnp.where(diag, block[h * PAD : (h + 1) * PAD], 0.0)
            chosen_ref[q // sz.reach, pl.ds(q % sz.reach, 1), pl.ds(h * LANES, LANES)] = jnp.sum(
                part, axis=0, keepdims=True
            )


def scatter_patches(sz, t_ref, cols_ref, spread_ref, sign, flat_ref=None, lift_ref=None):
    side = PATCH // BSIDE
    lifts = []
    if flat_ref is not None:
        for q in range(sz.obs * sz.reach):
            m = cols_ref[0, 0, 0, q // sz.reach, q % sz.reach]
            n = lax.rem(m, sz.blocks)
            a = (n // (sz.cols // BSIDE)) // side
            b = lax.rem(n, sz.cols // BSIDE) // side
            at = jnp.where(
                m < sz.blocks,
                (a + 1) * (sz.py + 2) + b + 1,
                sz.ext_patches + a * sz.py + b,
            )
            lifts.append(lift_ref[pl.ds(at, 1), :])
    lane = iota((PAD, LANES), 1)
    row = iota((PAD, LANES), 0)
    diag = row == lane // BSIDE
    per_row = sz.cols // BSIDE
    per_lanes = LANES // BSIDE
    for q in range(sz.obs * sz.reach):
        m = cols_ref[0, 0, 0, q // sz.reach, q % sz.reach]
        var, n = m // sz.blocks, lax.rem(m, sz.blocks)
        i, j = n // per_row, lax.rem(n, per_row)
        lanes = pl.ds(pl.multiple_of((j // per_lanes) * LANES, LANES), LANES)
        here = lane // BSIDE == lax.rem(j, per_lanes)
        for h in range(2):
            line = spread_ref[q // sz.reach, pl.ds(q % sz.reach, 1), pl.ds(h * LANES, LANES)]
            if flat_ref is not None:
                o, k = q // sz.reach, q % sz.reach
                for i_k in range(sz.reach):
                    line = line + lifts[sz.reach * o + i_k] * flat_ref[
                        o, pl.ds(sz.reach * i_k + k, 1), pl.ds(h * LANES, LANES)
                    ]
            part = jnp.where(diag, line, 0.0)
            for step in (16, 32, 64):
                part = part + pltpu.roll(part, step, 1)
            at = pl.ds(pl.multiple_of(i * BSIDE + h * PAD, PAD), PAD)
            t_ref[var, at, lanes] = t_ref[var, at, lanes] + sign * jnp.where(here, part, 0.0)


def start_phi(sz, phi_ref, buf_ref, sems):
    for o in range(sz.obs):
        pltpu.make_async_copy(phi_ref.at[0, 0, 0, o], buf_ref.at[o], sems.at[o]).start()


def observe_spread(sz, phi_ref, buf_ref, sems, chosen_ref, spread_ref, flat_ref=None):
    parts = [(k, h) for k in range(sz.reach) for h in range(BSIDE * BSIDE // LANES)]

    def body(o, carry):
        pltpu.make_async_copy(phi_ref.at[0, 0, 0, o], buf_ref.at[o], sems.at[o]).wait()

        def block(k, h):
            return buf_ref[o, k, :, pl.ds(h * LANES, LANES)]

        acc = None
        for k, h in parts:
            term = block(k, h) * chosen_ref[o, pl.ds(k, 1), pl.ds(h * LANES, LANES)]
            acc = term if acc is None else acc + term
        sources = [(spread_ref, 0, jnp.sum(acc, axis=1, keepdims=True))]
        if flat_ref is not None:
            for k in range(sz.reach):
                total = block(k, 0)
                for h in range(1, BSIDE * BSIDE // LANES):
                    total = total + block(k, h)
                sources.append((flat_ref, k, jnp.sum(total, axis=1, keepdims=True)))
        for k, h in parts:
            for ref, first, observed in sources:
                ref[o, pl.ds(sz.reach * first + k, 1), pl.ds(h * LANES, LANES)] = jnp.sum(
                    block(k, h) * observed, axis=0, keepdims=True
                )
        return carry

    lax.fori_loop(0, sz.obs, body, 0)


def smooth(sz, v2_ref, ke_ref, y_ref):
    xi, yi = lax.axis_index("gx"), lax.axis_index("gy")
    rows, cols = sz.ext
    v = v2_ref[0]
    beside = (
        pltpu.roll(v, 1, 0)
        + pltpu.roll(v, rows - 1, 0)
        + pltpu.roll(v, 1, 1)
        + pltpu.roll(v, cols - 1, 1)
    )
    y_ref[...] = (4.0 + ke_ref[...]) * v - beside

    @pl.when(xi == 0)
    def _():
        y_ref[pl.ds(0, PAD), :] = jnp.zeros((PAD, cols), F32)

    @pl.when(xi == sz.tx - 1)
    def _():
        y_ref[pl.ds(PAD + sz.rows, PAD), :] = jnp.zeros((PAD, cols), F32)

    @pl.when(yi == 0)
    def _():
        y_ref[:, pl.ds(0, LANES)] = jnp.zeros((rows, LANES), F32)

    @pl.when(yi == sz.ty - 1)
    def _():
        y_ref[:, pl.ds(LANES + sz.cols, LANES)] = jnp.zeros((rows, LANES), F32)

    inner = pl.ds(LANES, sz.cols)
    mid = y_ref[pl.ds(PAD, sz.rows), :]
    side = pltpu.roll(mid, 1, 1) + pltpu.roll(mid, cols - 1, 1)
    beside = y_ref[pl.ds(PAD - 1, sz.rows), inner] + y_ref[pl.ds(PAD + 1, sz.rows), inner]
    beside = beside + side[:, LANES : LANES + sz.cols]
    kappa = ke_ref[pl.ds(PAD, sz.rows), inner]
    return (4.0 + kappa) * mid[:, LANES : LANES + sz.cols] - beside


def device_at(sz, x, y, v):
    return (x * sz.ty + y) * 2 + v


def pack_payload(sz, t_ref, pay_ref):
    xi, yi, vi = lax.axis_index("gx"), lax.axis_index("gy"), lax.axis_index("vert")
    flat = iota((sz.head, LANES), 0) * LANES + iota((sz.head, LANES), 1)
    lane = iota((1, LANES), 1)
    vec = jnp.zeros((sz.head, LANES), F32)
    tiles = sz.tx * sz.ty
    for t in range(2):
        var = vi if t == 0 else 1 - vi
        total = jnp.zeros((1, LANES), F32)
        for a in range(sz.px):
            for j in range(sz.groups):
                seg = jnp.sum(
                    t_ref[t, pl.ds(a * PATCH, PATCH), pl.ds(j * LANES, LANES)],
                    axis=0,
                    keepdims=True,
                )
                total = total + seg
                for half in range(2):
                    keep = (lane >= PATCH) if half else (lane < PATCH)
                    value = jnp.sum(jnp.where(keep, seg, 0.0), axis=1, keepdims=True)
                    at = (
                        var * sz.per_var
                        + tiles
                        + (xi * sz.px + a) * (sz.ty * sz.py)
                        + yi * sz.py
                        + 2 * j
                        + half
                    )
                    vec = jnp.where(flat == at, value * (1.0 / sz.mid_div), vec)
        value = jnp.sum(total, axis=1, keepdims=True)
        at = var * sz.per_var + xi * sz.ty + yi
        vec = jnp.where(flat == at, value * (1.0 / sz.top_div), vec)

    def fill(s, carry):
        pay_ref[s, pl.ds(0, sz.head), :] = vec
        return carry

    lax.fori_loop(0, sz.devices, fill, 0, unroll=True if sz.devices <= 16 else 1)

    r, c = sz.rows, sz.cols
    for t in range(2):
        var = vi if t == 0 else 1 - vi
        for dx, first in ((-1, 0), (1, r - 2)):
            @pl.when((xi + dx >= 0) & (xi + dx < sz.tx))
            def _(t=t, var=var, dx=dx, first=first):
                dest = device_at(sz, xi + dx, yi, var)
                for j in range(sz.groups):
                    pay_ref[dest, pl.ds(sz.head + 2 * j, 2), :] = t_ref[
                        t, pl.ds(first, 2), pl.ds(j * LANES, LANES)
                    ]

        for dy in (-1, 1):
            @pl.when((yi + dy >= 0) & (yi + dy < sz.ty))
            def _(t=t, var=var, dy=dy):
                dest = device_at(sz, xi, yi + dy, var)
                if dy < 0:
                    pair = t_ref[t, :, pl.ds(0, LANES)].T[0:2]
                else:
                    pair = t_ref[t, :, pl.ds(c - LANES, LANES)].T[LANES - 2 : LANES]
                pay_ref[dest, pl.ds(sz.head, 2), :] = pair

            for dx in (-1, 1):
                @pl.when(
                    (xi + dx >= 0) & (xi + dx < sz.tx) & (yi + dy >= 0) & (yi + dy < sz.ty)
                )
                def _(t=t, var=var, dx=dx, dy=dy):
                    dest = device_at(sz, xi + dx, yi + dy, var)
                    lanes = pl.ds(0 if dy < 0 else c - LANES, LANES)
                    pay_ref[dest, pl.ds(sz.head, 1), :] = t_ref[
                        t, pl.ds(0 if dx < 0 else r - 1, 1), lanes
                    ]


def from_neighbour(sz, recv_ref, dx, dy, first, count, var=None):
    xi, yi = lax.axis_index("gx"), lax.axis_index("gy")
    x, y = xi + dx, yi + dy
    inside = (x >= 0) & (x < sz.tx) & (y >= 0) & (y < sz.ty)
    source = device_at(sz, jnp.clip(x, 0, sz.tx - 1), jnp.clip(y, 0, sz.ty - 1), 0)
    rows = pl.ds(first, count)
    if var is None:
        found = recv_ref[source, rows, :] + recv_ref[source + 1, rows, :]
    else:
        found = recv_ref[source + var, rows, :]
    return jnp.where(inside, found, 0.0)


def data_kernel(sz, stage, *refs):
    if stage == 0:
        x_ref, xp_ref, cols_ref, phi_ref, spread_ref = refs[:5]
        flat_ref = None
    else:
        to_ref, tm_ref, s_ref, sp_ref, cols_ref, phi_ref, spread_ref = refs[:7]
        flat_ref = refs[7] if stage == 1 else None
    v2_ref, chosen_ref, buf_ref, sems = refs[-4:]
    start_phi(sz, phi_ref, buf_ref, sems)
    if stage == 0:
        v2_ref[0] = x_ref[0]
        v2_ref[1] = xp_ref[0]
    else:
        scale = s_ref[pl.ds(PAD, sz.rows), pl.ds(LANES, sz.cols)]
        v2_ref[0] = scale * (to_ref[0] + tm_ref[1])
        v2_ref[1] = sp_ref[0] * (tm_ref[0] + to_ref[1])
    gather_patches(sz, v2_ref, cols_ref, chosen_ref)
    observe_spread(sz, phi_ref, buf_ref, sems, chosen_ref, spread_ref, flat_ref)


def first_kernel(sz, recv_ref, x0_ref, s_ref, k_ref, b_ref, spread_ref, cols_ref, w_ref,
                 t_ref, pay_ref, se_ref, ke_ref, v2_ref, y_ref):
    vi = lax.axis_index("vert")
    r, c, g = sz.rows, sz.cols, sz.groups
    mid, inner = pl.ds(PAD, r), pl.ds(LANES, c)
    for (at, width), ref, src in zip(
        FIELDS, (v2_ref.at[0], se_ref, ke_ref), (x0_ref, s_ref, k_ref)
    ):
        first = at * 2 * g
        clear_bands(sz, ref)
        ref[mid, inner] = src[0]

        def beside(dx, dy, count):
            return from_neighbour(sz, recv_ref, dx, dy, first, count, vi)

        put_sides(sz, ref, beside(0, -1, width), beside(0, 1, width))
        up, down = beside(-1, 0, width * g), beside(1, 0, width * g)
        for j in range(g):
            lanes = pl.ds(LANES + j * LANES, LANES)
            ref[pl.ds(PAD - width, width), lanes] = up[j * width : (j + 1) * width]
            ref[pl.ds(PAD + r, width), lanes] = down[j * width : (j + 1) * width]
        if width == 2:
            put_corners(sz, ref, beside)
    t_ref[0] = b_ref[0] - w_ref[0] * smooth(sz, v2_ref, ke_ref, y_ref)
    t_ref[1] = jnp.zeros((r, c), F32)
    scatter_patches(sz, t_ref, cols_ref, spread_ref, -1.0)
    pack_payload(sz, t_ref, pay_ref)


def precondition(sz, recv_ref, lg_ref, to_ref, tm_ref, se_ref, sp_ref, v2_ref, res_ref, lift_ref):
    r, c, g = sz.rows, sz.cols, sz.groups
    lane = iota((1, LANES), 1)
    mid, inner = pl.ds(PAD, r), pl.ds(LANES, c)

    def add_head(s, vec):
        return vec + recv_ref[s, pl.ds(0, sz.head), :]

    vec = lax.fori_loop(
        1, sz.devices, add_head, recv_ref[0, pl.ds(0, sz.head), :],
        unroll=True if sz.devices <= 16 else 1,
    )
    acc = None
    for i in range(sz.vec_rows):
        term = lg_ref[pl.ds(i * sz.lift_rows, sz.lift_rows), :] * vec[i : i + 1]
        acc = term if acc is None else acc + term
    lift = jnp.broadcast_to(jnp.sum(acc, axis=1, keepdims=True), (sz.lift_rows, LANES))
    lift_ref[...] = lift

    ext = v2_ref.at[0]
    clear_bands(sz, ext)
    whole = to_ref[0] + tm_ref[1]
    res_ref[...] = whole
    ext[mid, inner] = whole

    def beside(dx, dy, count):
        return from_neighbour(sz, recv_ref, dx, dy, sz.head, count)

    put_sides(sz, ext, beside(0, -1, 2), beside(0, 1, 2))
    up, down = beside(-1, 0, 2 * g), beside(1, 0, 2 * g)
    for j in range(g):
        lanes = pl.ds(LANES + j * LANES, LANES)
        ext[pl.ds(PAD - 2, 2), lanes] = up[2 * j : 2 * j + 2]
        ext[pl.ds(PAD + r, 2), lanes] = down[2 * j : 2 * j + 2]
    put_corners(sz, ext, beside)

    bands = [(0, PAD)] + [(PAD + a * PATCH, PATCH) for a in range(sz.px)] + [(PAD + r, PAD)]
    wide = sz.py + 2
    for a, (first, count) in enumerate(bands):
        rows = pl.ds(first, count)
        for j in range(g + 2):
            lanes = pl.ds(j * LANES, LANES)
            if j == 0:
                line = lift[a * wide : a * wide + 1]
            elif j == g + 1:
                line = lift[a * wide + wide - 1 : a * wide + wide]
            else:
                at = a * wide + 2 * j - 1
                line = jnp.where(lane < PATCH, lift[at : at + 1], lift[at + 1 : at + 2])
            ext[rows, lanes] = se_ref[rows, lanes] * ext[rows, lanes] + line
    for a in range(sz.px):
        rows = pl.ds(a * PATCH, PATCH)
        for j in range(g):
            lanes = pl.ds(j * LANES, LANES)
            at = sz.ext_patches + a * sz.py + 2 * j
            line = jnp.where(lane < PATCH, lift[at : at + 1], lift[at + 1 : at + 2])
            other = tm_ref[0, rows, lanes] + to_ref[1, rows, lanes]
            v2_ref[1, pl.ds(PAD + a * PATCH, PATCH), pl.ds(LANES + j * LANES, LANES)] = (
                sp_ref[0, rows, lanes] * other + line
            )


def fold(product):
    return jnp.sum(product, axis=0, keepdims=True)


def row_dot(sz, left, right):
    line = jnp.sum(left * right, axis=0, keepdims=True)
    total = line[:, 0:LANES]
    for j in range(1, sz.groups):
        total = total + line[:, j * LANES : (j + 1) * LANES]
    return total


def apply_kernel(sz, last, recv_ref, lg_ref, to_ref, tm_ref, se_ref, ke_ref, sp_ref, cols_ref,
                 w_ref, dots_ref, spread_ref, flat_ref, t_ref, pay_ref, res_ref, pre_ref,
                 out_dots_ref, v2_ref, y_ref, lift_ref):
    r, c = sz.rows, sz.cols
    mid, inner = pl.ds(PAD, r), pl.ds(LANES, c)
    precondition(sz, recv_ref, lg_ref, to_ref, tm_ref, se_ref, sp_ref, v2_ref, res_ref, lift_ref)
    t_ref[0] = w_ref[0] * smooth(sz, v2_ref, ke_ref, y_ref)
    t_ref[1] = jnp.zeros((r, c), F32)
    scatter_patches(sz, t_ref, cols_ref, spread_ref, 1.0, flat_ref, lift_ref)
    own = v2_ref[0, mid, inner]
    pre_ref[...] = own
    gamma = row_dot(sz, res_ref[...], own)
    curve = row_dot(sz, own, t_ref[0]) + row_dot(sz, v2_ref[1, mid, inner], t_ref[1])
    if last:
        lines = jnp.concatenate(
            [dots_ref[0:2], gamma, curve, jnp.zeros((PAD - 4, LANES), F32)], axis=0
        )
        out_dots_ref[...] = lines

        def fill(s, carry):
            pay_ref[s] = lines
            return carry

        lax.fori_loop(0, sz.devices, fill, 0, unroll=True if sz.devices <= 16 else 1)
    else:
        out_dots_ref[...] = jnp.concatenate(
            [gamma, curve, jnp.zeros((PAD - 2, LANES), F32)], axis=0
        )
        pack_payload(sz, t_ref, pay_ref)


def final_kernel(sz, recv_ref, x0_ref, r_ref, p_ref, w_ref, z_ref, to_ref, tm_ref, x_ref, res_ref):
    def add(s, lines):
        return lines + recv_ref[s]

    lines = lax.fori_loop(
        1, sz.devices, add, recv_ref[0], unroll=True if sz.devices <= 16 else 1
    )
    sums = jnp.sum(lines, axis=1, keepdims=True)
    gamma, delta, cross, far = (sums[i : i + 1] for i in range(4))
    step = gamma / delta
    gamma_new = step * step * cross - gamma
    growth = step * cross / delta
    curve = step * step * (far - cross * cross / delta)
    step_new = gamma_new / curve
    along = step + step_new * growth
    back = step_new * step
    x_ref[0] = x0_ref[0] + (along * p_ref[...] - back * z_ref[...])
    image = to_ref[0] + tm_ref[1]
    res_ref[0] = r_ref[...] - (along * w_ref[...] - back * image)


def shape(*dims):
    return jax.ShapeDtypeStruct(dims, F32)


def data_space(sz):
    block = BSIDE * BSIDE
    return [
        pltpu.VMEM((2, sz.rows, sz.cols), F32),
        pltpu.VMEM((sz.obs, sz.reach, block), F32),
        pltpu.VMEM((sz.obs, sz.reach, block, block), F32),
        pltpu.SemaphoreType.DMA((sz.obs,)),
    ]


def cost(micros):
    return pl.CostEstimate(flops=0, bytes_accessed=int(micros * 3.0e6), transcendentals=0)


def local(right_side, initial_guess, kappa_sq, smooth_weight, precond_scale, phi_vals, phi_cols,
          coarse_slots, slot_count, coarse_rows):
    tx, ty = lax.axis_size("gx"), lax.axis_size("gy")
    sz = Sizes(tx, ty, right_side.shape[1:], phi_vals.shape[3], phi_vals.shape[4],
               coarse_rows.shape[2])
    swap = [(0, 1), (1, 0)]
    x_partner = lax.ppermute(initial_guess, "vert", swap)
    s_partner = lax.ppermute(precond_scale, "vert", swap)

    def exchange(array):
        return lax.all_to_all(array, ALL, 0, 0, tiled=True)

    cap = coarse_slots.shape[1]
    edges, *shares = pl.pallas_call(
        functools.partial(setup_kernel, sz),
        out_shape=[shape(sz.devices, PAD * (-(-5 * sz.groups // PAD)), LANES)]
        + [shape(sz.vec_rows * sz.lift_rows, LANES)] * tx,
        in_specs=[ANY] * 4 + [VMEM, SMEM],
        out_specs=[VMEM] * (1 + tx),
        scratch_shapes=[pltpu.VMEM((3, sz.rows, sz.cols), F32), pltpu.VMEM((cap, sz.nco), F32),
                        pltpu.SemaphoreType.DMA((4,))],
        compiler_params=EDGE_PARAMS,
        cost_estimate=cost(1.5),
    )(initial_guess, precond_scale, kappa_sq, coarse_rows, coarse_slots, slot_count)
    got = [lax.ppermute(shares[k], "gx", [(i, i ^ k) for i in range(tx)]) for k in range(1, tx)]
    lift_matrix = sum(got, shares[0])
    edges = exchange(edges)

    r, c = sz.rows, sz.cols
    block = BSIDE * BSIDE
    pair = shape(2, r, c)
    payload = shape(sz.devices, sz.head + PAD, LANES)
    spread_shape = shape(sz.obs, sz.reach, block)
    flat_shape = shape(sz.obs, sz.reach * sz.reach, block)

    def data(stage, *fields):
        return pl.pallas_call(
            functools.partial(data_kernel, sz, stage),
            out_shape=[spread_shape, flat_shape] if stage == 1 else [spread_shape],
            in_specs=[VMEM] * len(fields) + [SMEM, ANY],
            out_specs=[VMEM] * (2 if stage == 1 else 1),
            scratch_shapes=data_space(sz),
            compiler_params=DATA_PARAMS,
            cost_estimate=cost(4),
        )(*fields, phi_cols, phi_vals)

    (spread,) = data(0, initial_guess, x_partner)
    parts, sent, s_ext, k_ext = pl.pallas_call(
        functools.partial(first_kernel, sz),
        out_shape=[pair, payload, shape(*sz.ext), shape(*sz.ext)],
        in_specs=[VMEM] * 6 + [SMEM, SMEM],
        out_specs=[VMEM] * 4,
        scratch_shapes=[pltpu.VMEM((1,) + sz.ext, F32), pltpu.VMEM(sz.ext, F32)],
        compiler_params=PARAMS,
        cost_estimate=cost(3),
    )(edges, initial_guess, precond_scale, kappa_sq, right_side, spread, phi_cols, smooth_weight)

    def apply(last, received, parts, mirrored, dots, spread, flat):
        return pl.pallas_call(
            functools.partial(apply_kernel, sz, last),
            out_shape=[pair, shape(sz.devices, PAD, LANES) if last else payload,
                       shape(r, c), shape(r, c), shape(PAD, LANES)],
            in_specs=[VMEM] * 7 + [SMEM, SMEM] + [VMEM] * 3,
            out_specs=[VMEM] * 5,
            scratch_shapes=[pltpu.VMEM((2,) + sz.ext, F32), pltpu.VMEM(sz.ext, F32),
                            pltpu.VMEM((sz.lift_rows, LANES), F32)],
            compiler_params=PARAMS,
            cost_estimate=cost(3),
        )(received, lift_matrix, parts, mirrored, s_ext, k_ext, s_partner, phi_cols,
          smooth_weight, dots, spread, flat)

    dots = jnp.zeros((PAD, LANES), F32)
    mirrored = lax.ppermute(parts, "vert", swap)
    received = exchange(sent)
    spread, flat = data(1, parts, mirrored, s_ext, s_partner)
    parts, sent, residual, precond, dots = apply(
        False, received, parts, mirrored, dots, spread, flat
    )
    mirrored = lax.ppermute(parts, "vert", swap)
    received = exchange(sent)
    (spread,) = data(2, parts, mirrored, s_ext, s_partner)
    parts, sent, image, second, dots = apply(
        True, received, parts, mirrored, dots, spread, flat
    )
    mirrored = lax.ppermute(parts, "vert", swap)
    return tuple(pl.pallas_call(
        functools.partial(final_kernel, sz),
        out_shape=[shape(1, r, c)] * 2,
        in_specs=[VMEM] * 8,
        out_specs=[VMEM] * 2,
        compiler_params=PARAMS,
        cost_estimate=cost(1),
    )(exchange(sent), initial_guess, residual, precond, image, second, parts, mirrored))


def solution(mesh):
    return jax.shard_map(
        local,
        mesh=mesh,
        in_specs=(
            P(("groups", "vert"), "gx", "gy"),
            P(("groups", "vert"), "gx", "gy"),
            P(("groups", "vert"), "gx", "gy"),
            P(("groups", "vert")),
            P(("groups", "vert"), "gx", "gy"),
            P(("groups", "vert"), "gx", "gy", None, None, None, None),
            P(("groups", "vert"), "gx", "gy", None, None),
            P(("groups", "gx"), None),
            P(("groups", "gx")),
            P(("groups", "gx"), None, None),
        ),
        out_specs=(P(("groups", "vert"), "gx", "gy"), P(("groups", "vert"), "gx", "gy")),
        check_vma=False,
    )
```

time: 86.3 us -> 73.4 us (0.85)
  blocking collectives: 20 us -> 9.85 us
  local copies, waits for them, and re-layouts: 13.4 us -> 4.48 us
  starting transfers between devices: 12.6 us -> 21.5 us
  waiting for transfers between devices: 12.2 us -> 5.97 us
  Pallas kernels: 23 us -> 28.8 us
  other arithmetic: 1.76 us -> 0.03 us
    pallas_call x1 -> x4, Pallas kernels: 1.71 us -> 18.7 us  [the longest x3 15.4 us: data(): pl.pallas_call(functools.partial(data_kernel, sz, stage), out_shape=[spre...]
    all_to_all x1 -> x3, starting transfers between devices: 4.91 us -> 16.7 us  [exchange(): return lax.all_to_all(array, ALL, 0, 0, tiled=True)]
    all_to_all x2 -> x1, blocking collectives: 20 us -> 9.85 us  [exchange(): return lax.all_to_all(array, ALL, 0, 0, tiled=True)]
    unnamed x17 -> x29, local copies, waits for them, and re-layouts: 12.3 us -> 4.48 us
    pallas_call x2, Pallas kernels: 12.1 us -> 5.92 us  [apply(): pl.pallas_call(functools.partial(apply_kernel, sz, last), out_shape=[pair...]
    pallas_call x1, Pallas kernels: 8.15 us -> 3.17 us  [local(): pl.pallas_call(functools.partial(first_kernel, sz), out_shape=[pair, payl...]
    ppermute x4 -> x3, waiting for transfers between devices: 6.32 us -> 1.39 us  [local(): lax.ppermute(shares[k], 'gx', [(i, i ^ k) for i in range(tx)])]
    ppermute x4 -> x3, starting transfers between devices: 6.76 us -> 4.39 us  [local(): lax.ppermute(shares[k], 'gx', [(i, i ^ k) for i in range(tx)])]
  transfers between devices with their start and end apart: 10 -> 11, of which waited for: 4 -> 4; matrix products, arithmetic and copies ran while one was open for 5% -> 1% of each run, Pallas kernels for 2% -> 21%
where the time goes in v1:
time: 73.4 us; the launch traced here: 72.8 us
  Pallas kernels  28.8 us (39%)
  starting transfers between devices  21.5 us (29%)
  blocking collectives  9.85 us (13%)
  waiting for transfers between devices  5.97 us (8%)
  local copies, waits for them, and re-layouts  4.48 us (6%)
  between operations  2.21 us (3%)
    all_to_all x3, starting transfers between devices, exchange(): return lax.all_to_all(array, ALL, 0, 0, tiled=True)  16.7 us
    pallas_call x3, Pallas kernels, data(): pl.pallas_call(functools.partial(data_kernel, sz, stage), out_shape=[spre...  15.4 us
    all_to_all x1, blocking collectives, exchange(): return lax.all_to_all(array, ALL, 0, 0, tiled=True)  9.85 us
    pallas_call x2, Pallas kernels, apply(): pl.pallas_call(functools.partial(apply_kernel, sz, last), out_shape=[pair...  5.92 us
    all_to_all x3, waiting for transfers between devices, exchange(): return lax.all_to_all(array, ALL, 0, 0, tiled=True)  4.57 us
    unnamed x29, local copies, waits for them, and re-layouts  4.48 us
    ppermute x3, starting transfers between devices, local(): lax.ppermute(shares[k], 'gx', [(i, i ^ k) for i in range(tx)])  4.39 us
    pallas_call x1, Pallas kernels, local(): pl.pallas_call(functools.partial(setup_kernel, sz), out_shape=[shape(sz.d...  3.24 us
  transfers between devices with their start and end apart: 11, of which 4 were waited for; matrix products, arithmetic and copies ran while one was open for 1% of the time, Pallas kernels for 21%

profile of v1, /device:TPU:0, one launch (start us, length us, event | category | flops | bytes accessed | tf_op | source)
XLA Modules:
  0.0 72.8 jit_solution(6658114828245048373)
XLA Ops:
  1.4 3.2 %shard_map.113 = (f32[16,24,128]{2,1,0:T(8,128)}, f32[168,128]{1,0:T(8,128)}, f32[168,128]{1,0:T(8,128)}, f32[168,128]{1,0:T(8,128)}, f32[168,128]{1,0:T(8,128)}) custom-call(f32[1,128,512]{2,1,0:T(8,128)} %x0_ref.5, f32[1,128,512]{2,1,0:T(8,128)} %s_ref.3, f32[1,128,512]{2,1,0:T(8,128)} %k_ref.3, f32[1,136,272]{2,1,0:T(8,128)} %rows_ref.1, ...), custom_call_target="tpu_custom_call" | custom-call | bytes 4500000 | tf_op jit(solution)/shard_map/pallas_call | solution.py:602
  4.7 7.5 %all-to-all-start = ((f32[16,24,128]{2,1,0:T(8,128)}), f32[16,24,128]{2,1,0:T(8,128)S(1)}, u32[]{:S(2)}, u32[]{:S(2)}) async-start(f32[16,24,128]{2,1,0:T(8,128)} %get-tuple-element.22), calls=%async_computation | async-start | bytes 393216 | tf_op jit(solution)/shard_map/all_to_all | solution.py:599
  13.2 0.8 %copy.12.refs_2_.cols_ref.refs_4_ = s32[1,1,1,16,2]{4,3,2,1,0:T(8,128)S(1)} copy(s32[1,1,1,16,2]{3,4,2,1,0:T(2,128)} %param.16) | data formatting | bytes 256 | tf_op args[6]
  14.0 0.9 %copy-done = f32[1,128,512]{2,1,0:T(8,128)S(1)} copy-done((f32[1,128,512]{2,1,0:T(8,128)S(1)}, f32[1,128,512]{2,1,0:T(8,128)}, u32[]{:S(2)}) %copy-start) | copy-done | bytes 262168
  14.9 4.9 %shard_map.114.spread_ref = f32[16,2,256]{2,1,0:T(2,128)S(1)} custom-call(f32[1,128,512]{2,1,0:T(8,128)S(1)} %copy-done, f32[1,128,512]{2,1,0:T(8,128)S(1)} %collective-permute-done.refs_1_, s32[1,1,1,16,2]{4,3,2,1,0:T(8,128)S(1)} %copy.12.refs_2_.cols_ref.refs_4_, f32[1,1,1,16,2,256,256]{6,5,4,3,2,1,0:T(8,128)} %refs_5_.3), custom_call_target="tpu_custom_call" | custom-call | bytes 12000000 | tf_op jit(solution)/shard_map/pallas_call | solution.py:625
  19.8 1.3 %all-to-all-done.recv_ref = f32[16,24,128]{2,1,0:T(8,128)S(1)} async-done(((f32[16,24,128]{2,1,0:T(8,128)}), f32[16,24,128]{2,1,0:T(8,128)S(1)}, u32[]{:S(2)}, u32[]{:S(2)}) %all-to-all-start) | async-done | bytes 196640 | tf_op jit(solution)/shard_map/all_to_all | solution.py:599
  21.2 3.2 %shard_map.115 = (f32[2,128,512]{2,1,0:T(8,128)S(1)}, f32[16,16,128]{2,1,0:T(8,128)}, f32[144,768]{1,0:T(8,128)S(1)}, f32[144,768]{1,0:T(8,128)S(1)}) custom-call(f32[16,24,128]{2,1,0:T(8,128)S(1)} %all-to-all-done.recv_ref, f32[1,128,512]{2,1,0:T(8,128)S(1)} %copy-done.1, f32[1,128,512]{2,1,0:T(8,128)S(1)} %copy-done.3, f32[1,128,512]{2,1,0:T(8,128)S(1)} %copy-done.2, ...), custom_call_target="tpu_custom_call" | custom-call | bytes 9000000 | tf_op jit(solution)/shard_map/pallas_call | solution.py:636
  24.3 0.8 %collective-permute-start.1 = (f32[168,128]{1,0:T(8,128)S(1)}, f32[168,128]{1,0:T(8,128)S(1)}, u32[]{:S(2)}, u32[]{:S(2)}) collective-permute-start(f32[168,128]{1,0:T(8,128)S(1)} %copy-done.13), channel_id=1, source_target_pairs={{0,4},{4,0},{8,12},{12,8},{1,5},{5,1},{9,13},{13,9},{2,6},{6,2},{1... | collective-permute-start | bytes 258056 | tf_op jit(solution)/shard_map/ppermute | solution.py:613
  25.1 2.3 %collective-permute-start.2 = (f32[168,128]{1,0:T(8,128)S(1)}, f32[168,128]{1,0:T(8,128)S(1)}, u32[]{:S(2)}, u32[]{:S(2)}) collective-permute-start(f32[168,128]{1,0:T(8,128)S(1)} %copy-done.12), channel_id=1, source_target_pairs={{0,8},{4,12},{8,0},{12,4},{1,9},{5,13},{9,1},{13,5},{2,10},{6,14},... | collective-permute-start | bytes 258056 | tf_op jit(solution)/shard_map/ppermute | solution.py:613
  27.5 1.3 %collective-permute-start.3 = (f32[168,128]{1,0:T(8,128)S(1)}, f32[168,128]{1,0:T(8,128)S(1)}, u32[]{:S(2)}, u32[]{:S(2)}) collective-permute-start(f32[168,128]{1,0:T(8,128)S(1)} %copy-done.11), channel_id=1, source_target_pairs={{0,12},{4,8},{8,4},{12,0},{1,13},{5,9},{9,5},{13,1},{2,14},{6,10},... | collective-permute-start | bytes 258056 | tf_op jit(solution)/shard_map/ppermute | solution.py:613
  28.7 4.8 %all-to-all-start.1 = ((f32[16,16,128]{2,1,0:T(8,128)}), f32[16,16,128]{2,1,0:T(8,128)S(1)}, u32[]{:S(2)}, u32[]{:S(2)}) async-start(f32[16,16,128]{2,1,0:T(8,128)} %get-tuple-element.23), calls=%async_computation.1 | async-start | bytes 262144 | tf_op jit(solution)/shard_map/all_to_all | solution.py:599
  33.6 1.4 %collective-permute-done.2 = f32[168,128]{1,0:T(8,128)S(1)} collective-permute-done((f32[168,128]{1,0:T(8,128)S(1)}, f32[168,128]{1,0:T(8,128)S(1)}, u32[]{:S(2)}, u32[]{:S(2)}) %collective-permute-start.2) | collective-permute-done | bytes 86048 | tf_op jit(solution)/shard_map/ppermute | solution.py:613
  35.1 5.6 %shard_map.116 = (f32[16,2,256]{2,1,0:T(2,128)S(1)}, f32[16,4,256]{2,1,0:T(4,128)S(1)}) custom-call(f32[2,128,512]{2,1,0:T(8,128)S(1)} %get-tuple-element.28.refs_0_.to_ref, f32[2,128,512]{2,1,0:T(8,128)S(1)} %collective-permute-done.4.refs_1_.tm_ref, f32[144,768]{1,0:T(8,128)S(1)} %get-tuple-element.29.refs_2_.se_ref, ...), custom_call_target="tpu_custom_call" | custom-call | bytes 12000000 | tf_op jit(solution)/shard_map/pallas_call | solution.py:625
  40.7 0.6 copy-done.8
  41.5 0.8 %copy-done.9 = f32[16,2,256]{2,1,0:T(2,128)S(1)} copy-done((f32[16,2,256]{2,1,0:T(2,128)S(1)}, f32[16,2,256]{2,1,0:T(2,128)}, u32[]{:S(2)}) %copy-start.9) | copy-done | bytes 32792
  42.3 2.8 %shard_map.117 = (f32[2,128,512]{2,1,0:T(8,128)S(1)}, f32[16,16,128]{2,1,0:T(8,128)S(1)}, f32[128,512]{1,0:T(8,128)S(1)}, f32[128,512]{1,0:T(8,128)S(1)}, f32[8,128]{1,0:T(8,128)S(1)}) custom-call(f32[16,16,128]{2,1,0:T(8,128)S(1)} %all-to-all-done.1.recv_ref, f32[168,128]{1,0:T(8,128)S(1)} %add_add_fusion.lg_ref, ...), custom_call_target="tpu_custom_call" | custom-call | bytes 9000000 | tf_op jit(solution)/shard_map/pallas_call | solution.py:647
  45.1 0.7 copy-done.4
  45.8 0.6 copy-done.7
  46.5 4.4 %all-to-all-start.2 = ((f32[16,16,128]{2,1,0:T(8,128)}), f32[16,16,128]{2,1,0:T(8,128)S(1)}, u32[]{:S(2)}, u32[]{:S(2)}) async-start(f32[16,16,128]{2,1,0:T(8,128)} %copy-done.7), calls=%async_computation.2 | async-start | bytes 262144 | tf_op jit(solution)/shard_map/all_to_all | solution.py:599
  50.9 4.9 %shard_map.118.spread_ref = f32[16,2,256]{2,1,0:T(2,128)S(1)} custom-call(f32[2,128,512]{2,1,0:T(8,128)S(1)} %get-tuple-element.34.refs_0_.to_ref, f32[2,128,512]{2,1,0:T(8,128)S(1)} %collective-permute-done.6.refs_1_.tm_ref, f32[144,768]{1,0:T(8,128)S(1)} %get-tuple-element.29.refs_2_.se_ref, f32[1,128,512]{2,1,0:T(8,128)S(1)} %collective-permute-done.5.refs_3_.sp_ref, ...), custom_call_target="tpu_custom_call" | custom-call | bytes 12000000 | tf_op jit(solution)/shard_map/pallas_call | solution.py:625
  55.8 3.0 %all-to-all-done.2.recv_ref = f32[16,16,128]{2,1,0:T(8,128)S(1)} async-done(((f32[16,16,128]{2,1,0:T(8,128)}), f32[16,16,128]{2,1,0:T(8,128)S(1)}, u32[]{:S(2)}, u32[]{:S(2)}) %all-to-all-start.2) | async-done | bytes 131104 | tf_op jit(solution)/shard_map/all_to_all | solution.py:599
  58.8 3.1 %shard_map.119 = (f32[2,128,512]{2,1,0:T(8,128)S(1)}, f32[16,8,128]{2,1,0:T(8,128)S(1)}, f32[128,512]{1,0:T(8,128)S(1)}, f32[128,512]{1,0:T(8,128)S(1)}, f32[8,128]{1,0:T(8,128)}) custom-call(f32[16,16,128]{2,1,0:T(8,128)S(1)} %all-to-all-done.2.recv_ref, f32[168,128]{1,0:T(8,128)S(1)} %add_add_fusion.lg_ref, ...), custom_call_target="tpu_custom_call" | custom-call | bytes 9000000 | tf_op jit(solution)/shard_map/pallas_call | solution.py:647
  61.9 9.9 %all_to_all.20.recv_ref = f32[16,8,128]{2,1,0:T(8,128)S(1)} all-to-all(f32[16,8,128]{2,1,0:T(8,128)S(1)} %get-tuple-element.36), channel_id=1, replica_groups=mesh['groups'=2,'gx'=4,'gy'=2,'vert'=2] {'gx','gy','vert'}, dimensions={0} | all-to-all | bytes 131072 | tf_op jit(solution)/shard_map/all_to_all | solution.py:599
  71.8 1.0 %shard_map.120 = (f32[1,128,512]{2,1,0:T(8,128)}, f32[1,128,512]{2,1,0:T(8,128)}) custom-call(f32[16,8,128]{2,1,0:T(8,128)S(1)} %all_to_all.20.recv_ref, f32[1,128,512]{2,1,0:T(8,128)S(1)} %copy-done.1, f32[128,512]{1,0:T(8,128)S(1)} %get-tuple-element.37.r_ref, f32[128,512]{1,0:T(8,128)S(1)} %copy-done.5, f32[128,512]{1,0:T(8,128)S(1)} %get-tuple-element.39.w_ref, ...), custom_call_target="tpu_custom_call" | custom-call | bytes 3000000 | tf_op jit(solution)/shard_map/pallas_call | solution.py:674
  (38 shorter events, 0.8 us)
Async XLA Ops:
  0.6 20.5 %copy-start.1 = (f32[1,128,512]{2,1,0:T(8,128)S(1)}, f32[1,128,512]{2,1,0:T(8,128)}, u32[]{:S(2)}) copy-start(f32[1,128,512]{2,1,0:T(8,128)} %x0_ref.5) | copy-start | bytes 786436
  0.6 20.5 %copy-start.3 = (f32[1,128,512]{2,1,0:T(8,128)S(1)}, f32[1,128,512]{2,1,0:T(8,128)}, u32[]{:S(2)}) copy-start(f32[1,128,512]{2,1,0:T(8,128)} %s_ref.3) | copy-start | bytes 786436
  0.7 20.5 %copy-start.2 = (f32[1,128,512]{2,1,0:T(8,128)S(1)}, f32[1,128,512]{2,1,0:T(8,128)}, u32[]{:S(2)}) copy-start(f32[1,128,512]{2,1,0:T(8,128)} %k_ref.3) | copy-start | bytes 786436
  0.7 20.5 %copy-start.6 = (f32[1,128,512]{2,1,0:T(8,128)S(1)}, f32[1,128,512]{2,1,0:T(8,128)}, u32[]{:S(2)}) copy-start(f32[1,128,512]{2,1,0:T(8,128)} %b_ref.1) | copy-start | bytes 786436
  4.7 19.7 %copy-start.13 = (f32[168,128]{1,0:T(8,128)S(1)}, f32[168,128]{1,0:T(8,128)}, u32[]{:S(2)}) copy-start(f32[168,128]{1,0:T(8,128)} %get-tuple-element.25) | copy-start | bytes 258052
  4.7 20.5 %copy-start.12 = (f32[168,128]{1,0:T(8,128)S(1)}, f32[168,128]{1,0:T(8,128)}, u32[]{:S(2)}) copy-start(f32[168,128]{1,0:T(8,128)} %get-tuple-element.26) | copy-start | bytes 258052
  4.7 22.8 %copy-start.11 = (f32[168,128]{1,0:T(8,128)S(1)}, f32[168,128]{1,0:T(8,128)}, u32[]{:S(2)}) copy-start(f32[168,128]{1,0:T(8,128)} %get-tuple-element.27) | copy-start | bytes 258052
  4.7 30.3 %copy-start.10 = (f32[168,128]{1,0:T(8,128)S(1)}, f32[168,128]{1,0:T(8,128)}, u32[]{:S(2)}) copy-start(f32[168,128]{1,0:T(8,128)} %get-tuple-element.24) | copy-start | bytes 258052
  4.7 16.5 %all-to-all-start = ((f32[16,24,128]{2,1,0:T(8,128)}), f32[16,24,128]{2,1,0:T(8,128)S(1)}, u32[]{:S(2)}, u32[]{:S(2)}) async-start(f32[16,24,128]{2,1,0:T(8,128)} %get-tuple-element.22), calls=%async_computation | async-start | bytes 393216 | tf_op jit(solution)/shard_map/all_to_all | solution.py:599
  12.2 1.8 %collective-permute-start = (f32[1,128,512]{2,1,0:T(8,128)}, f32[1,128,512]{2,1,0:T(8,128)S(1)}, u32[]{:S(2)}, u32[]{:S(2)}) collective-permute-start(f32[1,128,512]{2,1,0:T(8,128)} %x0_ref.5), channel_id=1, source_target_pairs={{0,1},{1,0},{2,3},{3,2},{4,5},{5,4},{6,7},{7,6},{8,9},{9,8},{10,11... | collective-permute-start | bytes 786440 | tf_op jit(solution)/shard_map/ppermute | solution.py:595
  14.0 1.0 %copy-start = (f32[1,128,512]{2,1,0:T(8,128)S(1)}, f32[1,128,512]{2,1,0:T(8,128)}, u32[]{:S(2)}) copy-start(f32[1,128,512]{2,1,0:T(8,128)} %x0_ref.5) | copy-start | bytes 786436
  24.3 10.7 %collective-permute-start.4 = (f32[2,128,512]{2,1,0:T(8,128)S(1)}, f32[2,128,512]{2,1,0:T(8,128)S(1)}, u32[]{:S(2)}, u32[]{:S(2)}) collective-permute-start(f32[2,128,512]{2,1,0:T(8,128)S(1)} %get-tuple-element.28.refs_0_.to_ref), channel_id=1, source_target_pairs={{0,1},{1,0},{2,3},{3,2},{4,5},{5,4},{6,7},{7,6},{8,9},{9,8},{10,11... | collective-permute-start | bytes 1572872 | tf_op jit(solution)/shard_map/ppermute | solution.py:661
  24.3 9.3 %collective-permute-start.1 = (f32[168,128]{1,0:T(8,128)S(1)}, f32[168,128]{1,0:T(8,128)S(1)}, u32[]{:S(2)}, u32[]{:S(2)}) collective-permute-start(f32[168,128]{1,0:T(8,128)S(1)} %copy-done.13), channel_id=1, source_target_pairs={{0,4},{4,0},{8,12},{12,8},{1,5},{5,1},{9,13},{13,9},{2,6},{6,2},{1... | collective-permute-start | bytes 258056 | tf_op jit(solution)/shard_map/ppermute | solution.py:613
  25.1 9.9 %collective-permute-start.2 = (f32[168,128]{1,0:T(8,128)S(1)}, f32[168,128]{1,0:T(8,128)S(1)}, u32[]{:S(2)}, u32[]{:S(2)}) collective-permute-start(f32[168,128]{1,0:T(8,128)S(1)} %copy-done.12), channel_id=1, source_target_pairs={{0,8},{4,12},{8,0},{12,4},{1,9},{5,13},{9,1},{13,5},{2,10},{6,14},... | collective-permute-start | bytes 258056 | tf_op jit(solution)/shard_map/ppermute | solution.py:613
  27.5 7.5 %collective-permute-start.3 = (f32[168,128]{1,0:T(8,128)S(1)}, f32[168,128]{1,0:T(8,128)S(1)}, u32[]{:S(2)}, u32[]{:S(2)}) collective-permute-start(f32[168,128]{1,0:T(8,128)S(1)} %copy-done.11), channel_id=1, source_target_pairs={{0,12},{4,8},{8,4},{12,0},{1,13},{5,9},{9,5},{13,1},{2,14},{6,10},... | collective-permute-start | bytes 258056 | tf_op jit(solution)/shard_map/ppermute | solution.py:613
  28.7 6.3 %collective-permute-start.5 = (f32[1,128,512]{2,1,0:T(8,128)S(1)}, f32[1,128,512]{2,1,0:T(8,128)S(1)}, u32[]{:S(2)}, u32[]{:S(2)}) collective-permute-start(f32[1,128,512]{2,1,0:T(8,128)S(1)} %copy-done.3), channel_id=1, source_target_pairs={{0,1},{1,0},{2,3},{3,2},{4,5},{5,4},{6,7},{7,6},{8,9},{9,8},{10,11... | collective-permute-start | bytes 786440 | tf_op jit(solution)/shard_map/ppermute | solution.py:596
  28.7 12.8 %all-to-all-start.1 = ((f32[16,16,128]{2,1,0:T(8,128)}), f32[16,16,128]{2,1,0:T(8,128)S(1)}, u32[]{:S(2)}, u32[]{:S(2)}) async-start(f32[16,16,128]{2,1,0:T(8,128)} %get-tuple-element.23), calls=%async_computation.1 | async-start | bytes 262144 | tf_op jit(solution)/shard_map/all_to_all | solution.py:599
  41.5 0.8 %copy-start.9 = (f32[16,2,256]{2,1,0:T(2,128)S(1)}, f32[16,2,256]{2,1,0:T(2,128)}, u32[]{:S(2)}) copy-start(f32[16,2,256]{2,1,0:T(2,128)} %copy-done.8) | copy-start | bytes 98308
  45.1 0.7 copy-start.4
  45.8 0.7 copy-start.7
  45.8 25.9 %copy-start.5 = (f32[128,512]{1,0:T(8,128)S(1)}, f32[128,512]{1,0:T(8,128)}, u32[]{:S(2)}) copy-start(f32[128,512]{1,0:T(8,128)} %copy-done.4) | copy-start | bytes 786436
  45.8 5.0 %collective-permute-start.6 = (f32[2,128,512]{2,1,0:T(8,128)S(1)}, f32[2,128,512]{2,1,0:T(8,128)S(1)}, u32[]{:S(2)}, u32[]{:S(2)}) collective-permute-start(f32[2,128,512]{2,1,0:T(8,128)S(1)} %get-tuple-element.34.refs_0_.to_ref), channel_id=1, source_target_pairs={{0,1},{1,0},{2,3},{3,2},{4,5},{5,4},{6,7},{7,6},{8,9},{9,8},{10,11... | collective-permute-start | bytes 1572872 | tf_op jit(solution)/shard_map/ppermute | solution.py:667
  46.5 12.3 %all-to-all-start.2 = ((f32[16,16,128]{2,1,0:T(8,128)}), f32[16,16,128]{2,1,0:T(8,128)S(1)}, u32[]{:S(2)}, u32[]{:S(2)}) async-start(f32[16,16,128]{2,1,0:T(8,128)} %copy-done.7), calls=%async_computation.2 | async-start | bytes 262144 | tf_op jit(solution)/shard_map/all_to_all | solution.py:599
  61.9 9.9 %collective-permute-start.7 = (f32[2,128,512]{2,1,0:T(8,128)S(1)}, f32[2,128,512]{2,1,0:T(8,128)S(1)}, u32[]{:S(2)}, u32[]{:S(2)}) collective-permute-start(f32[2,128,512]{2,1,0:T(8,128)S(1)} %get-tuple-element.41.to_ref), channel_id=1, source_target_pairs={{0,1},{1,0},{2,3},{3,2},{4,5},{5,4},{6,7},{7,6},{8,9},{9,8},{10,11... | collective-permute-start | bytes 1572872 | tf_op jit(solution)/shard_map/ppermute | solution.py:673
  (1 other events, 0.6 us)

commit v2 on v1

--- a/solution.py
+++ b/solution.py
@@ -31,7 +31,7 @@
         self.nco = nco
         self.px, self.py = self.rows // PATCH, self.cols // PATCH
         self.groups = self.cols // LANES
-        self.ext = (self.rows + 2 * PAD, self.cols + 2 * LANES)
+        self.ext = (self.rows + PAD, self.cols + LANES)
         self.devices = tx * ty * 2
         self.per_var = tx * ty * (1 + self.px * self.py)
         self.vec_rows = -(-nco // LANES)
@@ -146,35 +146,36 @@
                         pay_ref[dest, pl.ds(at * 2 * g, 1), :] = tiles_ref[at, rows, lanes]
 
 
-def put_sides(sz, ref, low, high):
-    width = low.shape[0]
-    zeros = jnp.zeros((LANES - width, LANES), F32)
-    mid = pl.ds(PAD, sz.rows)
-    ref[mid, pl.ds(0, LANES)] = jnp.concatenate([zeros, low], axis=0).T
-    ref[mid, pl.ds(LANES + sz.cols, LANES)] = jnp.concatenate([high, zeros], axis=0).T
-
-
-def clear_bands(sz, ref):
-    blank = jnp.zeros((PAD, sz.ext[1]), F32)
-    ref[pl.ds(0, PAD), :] = blank
-    ref[pl.ds(PAD + sz.rows, PAD), :] = blank
-
-
-def put_corners(sz, ref, beside):
-    for dx in (-1, 1):
-        for dy in (-1, 1):
-            lanes = pl.ds(0 if dy < 0 else LANES + sz.cols, LANES)
-            ref[pl.ds(PAD - 1 if dx < 0 else PAD + sz.rows, 1), lanes] = beside(dx, dy, 1)
-
-
-def gather_patches(sz, v2_ref, cols_ref, chosen_ref):
+def put_borders(sz, ref, width, beside):
+    r, c, g = sz.rows, sz.cols, sz.groups
+    gap = jnp.zeros((LANES - 2 * width, LANES), F32)
+    sides = [beside(0, 1, width), gap, beside(0, -1, width)]
+    ref[pl.ds(0, r), pl.ds(c, LANES)] = jnp.concatenate(sides, axis=0).T
+    up, down = beside(-1, 0, width * g), beside(1, 0, width * g)
+    gap = jnp.zeros((PAD - 2 * width, LANES), F32)
+    for j in range(g):
+        rows = slice(j * width, (j + 1) * width)
+        ref[pl.ds(r, PAD), pl.ds(j * LANES, LANES)] = jnp.concatenate(
+            [down[rows], gap, up[rows]], axis=0
+        )
+    if width == 2:
+        left = iota((1, LANES), 1) >= LANES // 2
+        lines = [jnp.where(left, beside(dx, -1, 1), beside(dx, 1, 1)) for dx in (1, -1)]
+        gap = jnp.zeros((PAD - 2, LANES), F32)
+        block = jnp.concatenate([lines[0], gap, lines[1]], axis=0)
+    else:
+        block = jnp.zeros((PAD, LANES), F32)
+    ref[pl.ds(r, PAD), pl.ds(c, LANES)] = block
+
+
+def gather_patches(sz, v2_ref, cols_ref, out_ref):
     lane = iota((BSIDE, LANES), 1)
     row = iota((PAD, LANES), 0)
     diag = row == iota((PAD, LANES), 1) // BSIDE
     per_row = sz.cols // BSIDE
     per_lanes = LANES // BSIDE
     for q in range(sz.obs * sz.reach):
-        m = cols_ref[0, 0, 0, q // sz.reach, q % sz.reach]
+        m = cols_ref[0, 0, 0, q % sz.reach, q // sz.reach]
         var, n = m // sz.blocks, lax.rem(m, sz.blocks)
         i, j = n // per_row, lax.rem(n, per_row)
         at = pl.ds(pl.multiple_of(i * BSIDE, BSIDE), BSIDE)
@@ -185,7 +186,7 @@
             block = block + pltpu.roll(block, step, 1)
         for h in range(2):
             part = jnp.where(diag, block[h * PAD : (h + 1) * PAD], 0.0)
-            chosen_ref[q // sz.reach, pl.ds(q % sz.reach, 1), pl.ds(h * LANES, LANES)] = jnp.sum(
+            out_ref[q // sz.reach, pl.ds(sz.reach + q % sz.reach, 1), pl.ds(h * LANES, LANES)] = jnp.sum(
                 part, axis=0, keepdims=True
             )
 
@@ -193,9 +194,10 @@
 def scatter_patches(sz, t_ref, cols_ref, spread_ref, sign, flat_ref=None, lift_ref=None):
     side = PATCH // BSIDE
     lifts = []
+    crossed = jnp.zeros((1, LANES), F32)
     if flat_ref is not None:
         for q in range(sz.obs * sz.reach):
-            m = cols_ref[0, 0, 0, q // sz.reach, q % sz.reach]
+            m = cols_ref[0, 0, 0, q % sz.reach, q // sz.reach]
             n = lax.rem(m, sz.blocks)
             a = (n // (sz.cols // BSIDE)) // side
             b = lax.rem(n, sz.cols // BSIDE) // side
@@ -211,7 +213,7 @@
     per_row = sz.cols // BSIDE
     per_lanes = LANES // BSIDE
     for q in range(sz.obs * sz.reach):
-        m = cols_ref[0, 0, 0, q // sz.reach, q % sz.reach]
+        m = cols_ref[0, 0, 0, q % sz.reach, q // sz.reach]
         var, n = m // sz.blocks, lax.rem(m, sz.blocks)
         i, j = n // per_row, lax.rem(n, per_row)
         lanes = pl.ds(pl.multiple_of((j // per_lanes) * LANES, LANES), LANES)
@@ -222,13 +224,16 @@
                 o, k = q // sz.reach, q % sz.reach
                 for i_k in range(sz.reach):
                     line = line + lifts[sz.reach * o + i_k] * flat_ref[
-                        o, pl.ds(sz.reach * i_k + k, 1), pl.ds(h * LANES, LANES)
+                        o, pl.ds(sz.reach * (i_k + 2) + k, 1), pl.ds(h * LANES, LANES)
                     ]
+                value = spread_ref[o, pl.ds(sz.reach + k, 1), pl.ds(h * LANES, LANES)] + lifts[q]
+                crossed = crossed + jnp.where(m >= sz.blocks, line * value, 0.0)
             part = jnp.where(diag, line, 0.0)
             for step in (16, 32, 64):
                 part = part + pltpu.roll(part, step, 1)
             at = pl.ds(pl.multiple_of(i * BSIDE + h * PAD, PAD), PAD)
             t_ref[var, at, lanes] = t_ref[var, at, lanes] + sign * jnp.where(here, part, 0.0)
+    return crossed
 
 
 def start_phi(sz, phi_ref, buf_ref, sems):
@@ -236,7 +241,7 @@
         pltpu.make_async_copy(phi_ref.at[0, 0, 0, o], buf_ref.at[o], sems.at[o]).start()
 
 
-def observe_spread(sz, phi_ref, buf_ref, sems, chosen_ref, spread_ref, flat_ref=None):
+def observe_spread(sz, phi_ref, buf_ref, sems, out_ref, flat):
     parts = [(k, h) for k in range(sz.reach) for h in range(BSIDE * BSIDE // LANES)]
 
     def body(o, carry):
@@ -247,18 +252,18 @@
 
         acc = None
         for k, h in parts:
-            term = block(k, h) * chosen_ref[o, pl.ds(k, 1), pl.ds(h * LANES, LANES)]
+            term = block(k, h) * out_ref[o, pl.ds(sz.reach + k, 1), pl.ds(h * LANES, LANES)]
             acc = term if acc is None else acc + term
-        sources = [(spread_ref, 0, jnp.sum(acc, axis=1, keepdims=True))]
-        if flat_ref is not None:
+        sources = [(0, jnp.sum(acc, axis=1, keepdims=True))]
+        if flat:
             for k in range(sz.reach):
                 total = block(k, 0)
                 for h in range(1, BSIDE * BSIDE // LANES):
                     total = total + block(k, h)
-                sources.append((flat_ref, k, jnp.sum(total, axis=1, keepdims=True)))
+                sources.append((k + 2, jnp.sum(total, axis=1, keepdims=True)))
         for k, h in parts:
-            for ref, first, observed in sources:
-                ref[o, pl.ds(sz.reach * first + k, 1), pl.ds(h * LANES, LANES)] = jnp.sum(
+            for first, observed in sources:
+                out_ref[o, pl.ds(sz.reach * first + k, 1), pl.ds(h * LANES, LANES)] = jnp.sum(
                     block(k, h) * observed, axis=0, keepdims=True
                 )
         return carry
@@ -266,10 +271,11 @@
     lax.fori_loop(0, sz.obs, body, 0)
 
 
-def smooth(sz, v2_ref, ke_ref, y_ref):
+def smooth(sz, v_ref, ke_ref, y_ref):
     xi, yi = lax.axis_index("gx"), lax.axis_index("gy")
+    r, c = sz.rows, sz.cols
     rows, cols = sz.ext
-    v = v2_ref[0]
+    v = v_ref[...]
     beside = (
         pltpu.roll(v, 1, 0)
         + pltpu.roll(v, rows - 1, 0)
@@ -278,29 +284,20 @@
     )
     y_ref[...] = (4.0 + ke_ref[...]) * v - beside
 
-    @pl.when(xi == 0)
-    def _():
-        y_ref[pl.ds(0, PAD), :] = jnp.zeros((PAD, cols), F32)
-
-    @pl.when(xi == sz.tx - 1)
-    def _():
-        y_ref[pl.ds(PAD + sz.rows, PAD), :] = jnp.zeros((PAD, cols), F32)
-
-    @pl.when(yi == 0)
-    def _():
-        y_ref[:, pl.ds(0, LANES)] = jnp.zeros((rows, LANES), F32)
-
-    @pl.when(yi == sz.ty - 1)
-    def _():
-        y_ref[:, pl.ds(LANES + sz.cols, LANES)] = jnp.zeros((rows, LANES), F32)
-
-    inner = pl.ds(LANES, sz.cols)
-    mid = y_ref[pl.ds(PAD, sz.rows), :]
-    side = pltpu.roll(mid, 1, 1) + pltpu.roll(mid, cols - 1, 1)
-    beside = y_ref[pl.ds(PAD - 1, sz.rows), inner] + y_ref[pl.ds(PAD + 1, sz.rows), inner]
-    beside = beside + side[:, LANES : LANES + sz.cols]
-    kappa = ke_ref[pl.ds(PAD, sz.rows), inner]
-    return (4.0 + kappa) * mid[:, LANES : LANES + sz.cols] - beside
+    row = iota((PAD, c), 0)
+    keep = ((row < PAD // 2) & (xi < sz.tx - 1)) | ((row >= PAD // 2) & (xi > 0))
+    below = pl.ds(r, PAD)
+    y_ref[below, pl.ds(0, c)] = jnp.where(keep, y_ref[below, pl.ds(0, c)], 0.0)
+    lane = iota((r, LANES), 1)
+    keep = ((lane < LANES // 2) & (yi < sz.ty - 1)) | ((lane >= LANES // 2) & (yi > 0))
+    side = pl.ds(c, LANES)
+    y_ref[pl.ds(0, r), side] = jnp.where(keep, y_ref[pl.ds(0, r), side], 0.0)
+
+    wide = y_ref[pl.ds(0, r), :]
+    beside = (pltpu.roll(wide, 1, 1) + pltpu.roll(wide, cols - 1, 1))[:, 0:c]
+    tall = y_ref[:, pl.ds(0, c)]
+    beside = beside + (pltpu.roll(tall, 1, 0) + pltpu.roll(tall, rows - 1, 0))[0:r]
+    return (4.0 + ke_ref[pl.ds(0, r), pl.ds(0, c)]) * wide[:, 0:c] - beside
 
 
 def device_at(sz, x, y, v):
@@ -395,57 +392,43 @@
 
 def data_kernel(sz, stage, *refs):
     if stage == 0:
-        x_ref, xp_ref, cols_ref, phi_ref, spread_ref = refs[:5]
-        flat_ref = None
+        x_ref, xp_ref, cols_ref, phi_ref, out_ref = refs[:5]
     else:
-        to_ref, tm_ref, s_ref, sp_ref, cols_ref, phi_ref, spread_ref = refs[:7]
-        flat_ref = refs[7] if stage == 1 else None
-    v2_ref, chosen_ref, buf_ref, sems = refs[-4:]
+        to_ref, tm_ref, s_ref, sp_ref, cols_ref, phi_ref, out_ref = refs[:7]
+    v2_ref, buf_ref, sems = refs[-3:]
     start_phi(sz, phi_ref, buf_ref, sems)
     if stage == 0:
         v2_ref[0] = x_ref[0]
         v2_ref[1] = xp_ref[0]
     else:
-        scale = s_ref[pl.ds(PAD, sz.rows), pl.ds(LANES, sz.cols)]
+        scale = s_ref[pl.ds(0, sz.rows), pl.ds(0, sz.cols)]
         v2_ref[0] = scale * (to_ref[0] + tm_ref[1])
         v2_ref[1] = sp_ref[0] * (tm_ref[0] + to_ref[1])
-    gather_patches(sz, v2_ref, cols_ref, chosen_ref)
-    observe_spread(sz, phi_ref, buf_ref, sems, chosen_ref, spread_ref, flat_ref)
+    gather_patches(sz, v2_ref, cols_ref, out_ref)
+    observe_spread(sz, phi_ref, buf_ref, sems, out_ref, stage == 0)
 
 
 def first_kernel(sz, recv_ref, x0_ref, s_ref, k_ref, b_ref, spread_ref, cols_ref, w_ref,
-                 t_ref, pay_ref, se_ref, ke_ref, v2_ref, y_ref):
+                 t_ref, pay_ref, se_ref, ke_ref, v_ref, y_ref):
     vi = lax.axis_index("vert")
     r, c, g = sz.rows, sz.cols, sz.groups
-    mid, inner = pl.ds(PAD, r), pl.ds(LANES, c)
-    for (at, width), ref, src in zip(
-        FIELDS, (v2_ref.at[0], se_ref, ke_ref), (x0_ref, s_ref, k_ref)
-    ):
+    for (at, width), ref, src in zip(FIELDS, (v_ref, se_ref, ke_ref), (x0_ref, s_ref, k_ref)):
         first = at * 2 * g
-        clear_bands(sz, ref)
-        ref[mid, inner] = src[0]
 
         def beside(dx, dy, count):
             return from_neighbour(sz, recv_ref, dx, dy, first, count, vi)
 
-        put_sides(sz, ref, beside(0, -1, width), beside(0, 1, width))
-        up, down = beside(-1, 0, width * g), beside(1, 0, width * g)
-        for j in range(g):
-            lanes = pl.ds(LANES + j * LANES, LANES)
-            ref[pl.ds(PAD - width, width), lanes] = up[j * width : (j + 1) * width]
-            ref[pl.ds(PAD + r, width), lanes] = down[j * width : (j + 1) * width]
-        if width == 2:
-            put_corners(sz, ref, beside)
-    t_ref[0] = b_ref[0] - w_ref[0] * smooth(sz, v2_ref, ke_ref, y_ref)
+        ref[pl.ds(0, r), pl.ds(0, c)] = src[0]
+        put_borders(sz, ref, width, beside)
+    t_ref[0] = b_ref[0] - w_ref[0] * smooth(sz, v_ref, ke_ref, y_ref)
     t_ref[1] = jnp.zeros((r, c), F32)
     scatter_patches(sz, t_ref, cols_ref, spread_ref, -1.0)
     pack_payload(sz, t_ref, pay_ref)
 
 
-def precondition(sz, recv_ref, lg_ref, to_ref, tm_ref, se_ref, sp_ref, v2_ref, res_ref, lift_ref):
+def precondition(sz, recv_ref, lg_ref, to_ref, tm_ref, se_ref, v_ref, state_ref, lift_ref):
     r, c, g = sz.rows, sz.cols, sz.groups
     lane = iota((1, LANES), 1)
-    mid, inner = pl.ds(PAD, r), pl.ds(LANES, c)
 
     def add_head(s, vec):
         return vec + recv_ref[s, pl.ds(0, sz.head), :]
@@ -461,51 +444,30 @@
     lift = jnp.broadcast_to(jnp.sum(acc, axis=1, keepdims=True), (sz.lift_rows, LANES))
     lift_ref[...] = lift
 
-    ext = v2_ref.at[0]
-    clear_bands(sz, ext)
     whole = to_ref[0] + tm_ref[1]
-    res_ref[...] = whole
-    ext[mid, inner] = whole
+    state_ref[0] = whole
+    v_ref[pl.ds(0, r), pl.ds(0, c)] = whole
 
     def beside(dx, dy, count):
         return from_neighbour(sz, recv_ref, dx, dy, sz.head, count)
 
-    put_sides(sz, ext, beside(0, -1, 2), beside(0, 1, 2))
-    up, down = beside(-1, 0, 2 * g), beside(1, 0, 2 * g)
-    for j in range(g):
-        lanes = pl.ds(LANES + j * LANES, LANES)
-        ext[pl.ds(PAD - 2, 2), lanes] = up[2 * j : 2 * j + 2]
-        ext[pl.ds(PAD + r, 2), lanes] = down[2 * j : 2 * j + 2]
-    put_corners(sz, ext, beside)
-
-    bands = [(0, PAD)] + [(PAD + a * PATCH, PATCH) for a in range(sz.px)] + [(PAD + r, PAD)]
+    put_borders(sz, v_ref, 2, beside)
     wide = sz.py + 2
-    for a, (first, count) in enumerate(bands):
-        rows = pl.ds(first, count)
-        for j in range(g + 2):
-            lanes = pl.ds(j * LANES, LANES)
-            if j == 0:
-                line = lift[a * wide : a * wide + 1]
-            elif j == g + 1:
-                line = lift[a * wide + wide - 1 : a * wide + wide]
-            else:
-                at = a * wide + 2 * j - 1
-                line = jnp.where(lane < PATCH, lift[at : at + 1], lift[at + 1 : at + 2])
-            ext[rows, lanes] = se_ref[rows, lanes] * ext[rows, lanes] + line
-    for a in range(sz.px):
-        rows = pl.ds(a * PATCH, PATCH)
-        for j in range(g):
-            lanes = pl.ds(j * LANES, LANES)
-            at = sz.ext_patches + a * sz.py + 2 * j
-            line = jnp.where(lane < PATCH, lift[at : at + 1], lift[at + 1 : at + 2])
-            other = tm_ref[0, rows, lanes] + to_ref[1, rows, lanes]
-            v2_ref[1, pl.ds(PAD + a * PATCH, PATCH), pl.ds(LANES + j * LANES, LANES)] = (
-                sp_ref[0, rows, lanes] * other + line
-            )
-
-
-def fold(product):
-    return jnp.sum(product, axis=0, keepdims=True)
+
+    def line(band, j):
+        low, high = (2 * j + 1, 2 * j + 2) if j < g else (wide - 1, 0)
+        low, high = band * wide + low, band * wide + high
+        return jnp.where(lane < PATCH, lift[low : low + 1], lift[high : high + 1])
+
+    row = iota((PAD, LANES), 0)
+    for j in range(g + 1):
+        lanes = pl.ds(j * LANES, LANES)
+        for a in range(sz.px):
+            rows = pl.ds(a * PATCH, PATCH)
+            v_ref[rows, lanes] = se_ref[rows, lanes] * v_ref[rows, lanes] + line(a + 1, j)
+        rows = pl.ds(r, PAD)
+        both = jnp.where(row < PAD // 2, line(sz.px + 1, j), line(0, j))
+        v_ref[rows, lanes] = se_ref[rows, lanes] * v_ref[rows, lanes] + both
 
 
 def row_dot(sz, left, right):
@@ -516,24 +478,24 @@
     return total
 
 
-def apply_kernel(sz, last, recv_ref, lg_ref, to_ref, tm_ref, se_ref, ke_ref, sp_ref, cols_ref,
-                 w_ref, dots_ref, spread_ref, flat_ref, t_ref, pay_ref, res_ref, pre_ref,
-                 out_dots_ref, v2_ref, y_ref, lift_ref):
+def apply_kernel(sz, last, recv_ref, lg_ref, to_ref, tm_ref, se_ref, ke_ref, cols_ref,
+                 w_ref, dots_ref, spread_ref, flat_ref, t_ref, pay_ref, state_ref, out_dots_ref,
+                 v_ref, y_ref, lift_ref):
     r, c = sz.rows, sz.cols
-    mid, inner = pl.ds(PAD, r), pl.ds(LANES, c)
-    precondition(sz, recv_ref, lg_ref, to_ref, tm_ref, se_ref, sp_ref, v2_ref, res_ref, lift_ref)
-    t_ref[0] = w_ref[0] * smooth(sz, v2_ref, ke_ref, y_ref)
+    precondition(sz, recv_ref, lg_ref, to_ref, tm_ref, se_ref, v_ref, state_ref, lift_ref)
+    t_ref[0] = w_ref[0] * smooth(sz, v_ref, ke_ref, y_ref)
     t_ref[1] = jnp.zeros((r, c), F32)
-    scatter_patches(sz, t_ref, cols_ref, spread_ref, 1.0, flat_ref, lift_ref)
-    own = v2_ref[0, mid, inner]
-    pre_ref[...] = own
-    gamma = row_dot(sz, res_ref[...], own)
-    curve = row_dot(sz, own, t_ref[0]) + row_dot(sz, v2_ref[1, mid, inner], t_ref[1])
+    crossed = scatter_patches(sz, t_ref, cols_ref, spread_ref, 1.0, flat_ref, lift_ref)
+    own = v_ref[pl.ds(0, r), pl.ds(0, c)]
+    state_ref[1] = own
+    gamma = row_dot(sz, state_ref[0], own)
+    curve = row_dot(sz, own, t_ref[0]) + crossed
     if last:
-        lines = jnp.concatenate(
-            [dots_ref[0:2], gamma, curve, jnp.zeros((PAD - 4, LANES), F32)], axis=0
-        )
-        out_dots_ref[...] = lines
+        out_dots_ref[...] = dots_ref[...]
+        lane = iota((1, LANES), 1)
+        lines = jnp.zeros((1, LANES), F32)
+        for i, part in enumerate((dots_ref[0:1], dots_ref[1:2], gamma, curve)):
+            lines = jnp.where(lane == i, jnp.sum(part, axis=1, keepdims=True), lines)
 
         def fill(s, carry):
             pay_ref[s] = lines
@@ -547,15 +509,17 @@
         pack_payload(sz, t_ref, pay_ref)
 
 
-def final_kernel(sz, recv_ref, x0_ref, r_ref, p_ref, w_ref, z_ref, to_ref, tm_ref, x_ref, res_ref):
+def final_kernel(sz, recv_ref, x0_ref, rp_ref, wz_ref, to_ref, tm_ref, x_ref, res_ref):
     def add(s, lines):
         return lines + recv_ref[s]
 
     lines = lax.fori_loop(
         1, sz.devices, add, recv_ref[0], unroll=True if sz.devices <= 16 else 1
     )
-    sums = jnp.sum(lines, axis=1, keepdims=True)
-    gamma, delta, cross, far = (sums[i : i + 1] for i in range(4))
+    lane = iota((1, LANES), 1)
+    gamma, delta, cross, far = (
+        jnp.sum(jnp.where(lane == i, lines, 0.0), axis=1, keepdims=True) for i in range(4)
+    )
     step = gamma / delta
     gamma_new = step * step * cross - gamma
     growth = step * cross / delta
@@ -563,9 +527,9 @@
     step_new = gamma_new / curve
     along = step + step_new * growth
     back = step_new * step
-    x_ref[0] = x0_ref[0] + (along * p_ref[...] - back * z_ref[...])
+    x_ref[0] = x0_ref[0] + (along * rp_ref[1] - back * wz_ref[1])
     image = to_ref[0] + tm_ref[1]
-    res_ref[0] = r_ref[...] - (along * w_ref[...] - back * image)
+    res_ref[0] = rp_ref[0] - (along * wz_ref[0] - back * image)
 
 
 def shape(*dims):
@@ -576,7 +540,6 @@
     block = BSIDE * BSIDE
     return [
         pltpu.VMEM((2, sz.rows, sz.cols), F32),
-        pltpu.VMEM((sz.obs, sz.reach, block), F32),
         pltpu.VMEM((sz.obs, sz.reach, block, block), F32),
         pltpu.SemaphoreType.DMA((sz.obs,)),
     ]
@@ -589,6 +552,7 @@
 def local(right_side, initial_guess, kappa_sq, smooth_weight, precond_scale, phi_vals, phi_cols,
           coarse_slots, slot_count, coarse_rows):
     tx, ty = lax.axis_size("gx"), lax.axis_size("gy")
+    phi_cols = jnp.swapaxes(phi_cols, 3, 4)
     sz = Sizes(tx, ty, right_side.shape[1:], phi_vals.shape[3], phi_vals.shape[4],
                coarse_rows.shape[2])
     swap = [(0, 1), (1, 0)]
@@ -618,67 +582,65 @@
     block = BSIDE * BSIDE
     pair = shape(2, r, c)
     payload = shape(sz.devices, sz.head + PAD, LANES)
-    spread_shape = shape(sz.obs, sz.reach, block)
-    flat_shape = shape(sz.obs, sz.reach * sz.reach, block)
 
     def data(stage, *fields):
         return pl.pallas_call(
             functools.partial(data_kernel, sz, stage),
-            out_shape=[spread_shape, flat_shape] if stage == 1 else [spread_shape],
+            out_shape=shape(sz.obs, sz.reach * (2 + sz.reach * (stage == 0)), block),
             in_specs=[VMEM] * len(fields) + [SMEM, ANY],
-            out_specs=[VMEM] * (2 if stage == 1 else 1),
+            out_specs=VMEM,
             scratch_shapes=data_space(sz),
             compiler_params=DATA_PARAMS,
             cost_estimate=cost(4),
         )(*fields, phi_cols, phi_vals)
 
-    (spread,) = data(0, initial_guess, x_partner)
+    flat = data(0, initial_guess, x_partner)
     parts, sent, s_ext, k_ext = pl.pallas_call(
         functools.partial(first_kernel, sz),
         out_shape=[pair, payload, shape(*sz.ext), shape(*sz.ext)],
         in_specs=[VMEM] * 6 + [SMEM, SMEM],
         out_specs=[VMEM] * 4,
-        scratch_shapes=[pltpu.VMEM((1,) + sz.ext, F32), pltpu.VMEM(sz.ext, F32)],
+        scratch_shapes=[pltpu.VMEM(sz.ext, F32)] * 2,
         compiler_params=PARAMS,
         cost_estimate=cost(3),
-    )(edges, initial_guess, precond_scale, kappa_sq, right_side, spread, phi_cols, smooth_weight)
-
-    def apply(last, received, parts, mirrored, dots, spread, flat):
+    )(edges, initial_guess, precond_scale, kappa_sq, right_side, flat, phi_cols, smooth_weight)
+
+    def apply(last, received, parts, mirrored, dots, spread):
         return pl.pallas_call(
             functools.partial(apply_kernel, sz, last),
-            out_shape=[pair, shape(sz.devices, PAD, LANES) if last else payload,
-                       shape(r, c), shape(r, c), shape(PAD, LANES)],
-            in_specs=[VMEM] * 7 + [SMEM, SMEM] + [VMEM] * 3,
-            out_specs=[VMEM] * 5,
-            scratch_shapes=[pltpu.VMEM((2,) + sz.ext, F32), pltpu.VMEM(sz.ext, F32),
+            out_shape=[pair, shape(sz.devices, 1, LANES) if last else payload,
+                       pair, shape(PAD, LANES)],
+            in_specs=[VMEM] * 6 + [SMEM, SMEM] + [VMEM] * 3,
+            out_specs=[VMEM] * 4,
+            scratch_shapes=[pltpu.VMEM(sz.ext, F32), pltpu.VMEM(sz.ext, F32),
                             pltpu.VMEM((sz.lift_rows, LANES), F32)],
             compiler_params=PARAMS,
             cost_estimate=cost(3),
-        )(received, lift_matrix, parts, mirrored, s_ext, k_ext, s_partner, phi_cols,
+        )(received, lift_matrix, parts, mirrored, s_ext, k_ext, phi_cols,
           smooth_weight, dots, spread, flat)
 
     dots = jnp.zeros((PAD, LANES), F32)
     mirrored = lax.ppermute(parts, "vert", swap)
     received = exchange(sent)
-    spread, flat = data(1, parts, mirrored, s_ext, s_partner)
-    parts, sent, residual, precond, dots = apply(
-        False, received, parts, mirrored, dots, spread, flat
+    spread = data(1, parts, mirrored, s_ext, s_partner)
+    parts, sent, early, dots = apply(
+        False, received, parts, mirrored, dots, spread
     )
     mirrored = lax.ppermute(parts, "vert", swap)
     received = exchange(sent)
-    (spread,) = data(2, parts, mirrored, s_ext, s_partner)
-    parts, sent, image, second, dots = apply(
-        True, received, parts, mirrored, dots, spread, flat
+    spread = data(2, parts, mirrored, s_ext, s_partner)
+    parts, sent, late, dots = apply(
+        True, received, parts, mirrored, dots, spread
     )
     mirrored = lax.ppermute(parts, "vert", swap)
     return tuple(pl.pallas_call(
         functools.partial(final_kernel, sz),
         out_shape=[shape(1, r, c)] * 2,
-        in_specs=[VMEM] * 8,
+        in_specs=[VMEM] * 6,
         out_specs=[VMEM] * 2,
         compiler_params=PARAMS,
         cost_estimate=cost(1),
-    )(exchange(sent), initial_guess, residual, precond, image, second, parts, mirrored))
+    )(exchange(sent), initial_guess, early, late, parts, mirrored))
 
 
 def solution(mesh):

time: 73.4 us -> 71.4 us (0.973)
  local copies, waits for them, and re-layouts: 4.48 us -> 2.5 us
  Pallas kernels: 28.8 us -> 27.8 us
  waiting for transfers between devices: 5.97 us -> 6.94 us
    unnamed x29 -> x26, local copies, waits for them, and re-layouts: 4.48 us -> 2.5 us
    ppermute x1, waiting for transfers between devices: 0.01 us -> 0.75 us  [local(): x_partner = lax.ppermute(initial_guess, 'vert', swap)]
  transfers between devices with their start and end apart: 11 -> 11, of which waited for: 4 -> 4; matrix products, arithmetic and copies ran while one was open for 1% -> 0% of each run, Pallas kernels for 21% -> 21%
where the time goes in v2:
time: 71.4 us; the launch traced here: 70.8 us
  Pallas kernels  27.8 us (39%)
  starting transfers between devices  22 us (31%)
  blocking collectives  9.26 us (13%)
  waiting for transfers between devices  6.94 us (10%)
  local copies, waits for them, and re-layouts  2.5 us (4%)
  between operations  2.23 us (3%)
    all_to_all x3, starting transfers between devices, exchange(): return lax.all_to_all(array, ALL, 0, 0, tiled=True)  16.9 us
    pallas_call x3, Pallas kernels, data(): pl.pallas_call(functools.partial(data_kernel, sz, stage), out_shape=shape...  15.1 us
    all_to_all x1, blocking collectives, exchange(): return lax.all_to_all(array, ALL, 0, 0, tiled=True)  9.26 us
    pallas_call x2, Pallas kernels, apply(): pl.pallas_call(functools.partial(apply_kernel, sz, last), out_shape=[pair...  5.63 us
    all_to_all x3, waiting for transfers between devices, exchange(): return lax.all_to_all(array, ALL, 0, 0, tiled=True)  4.84 us
    ppermute x3, starting transfers between devices, local(): lax.ppermute(shares[k], 'gx', [(i, i ^ k) for i in range(tx)])  4.39 us
    pallas_call x1, Pallas kernels, local(): pl.pallas_call(functools.partial(setup_kernel, sz), out_shape=[shape(sz.d...  3.24 us
    pallas_call x1, Pallas kernels, local(): pl.pallas_call(functools.partial(first_kernel, sz), out_shape=[pair, payl...  2.9 us
  transfers between devices with their start and end apart: 11, of which 4 were waited for; matrix products, arithmetic and copies ran while one was open for 0% of the time, Pallas kernels for 21%

profile of v2, /device:TPU:0, one launch (start us, length us, event | category | flops | bytes accessed | tf_op | source)
XLA Modules:
  0.0 70.8 jit_solution(17372688330364201430)
XLA Ops:
  1.4 3.2 %shard_map.113 = (f32[16,24,128]{2,1,0:T(8,128)}, f32[168,128]{1,0:T(8,128)}, f32[168,128]{1,0:T(8,128)}, f32[168,128]{1,0:T(8,128)}, f32[168,128]{1,0:T(8,128)}) custom-call(f32[1,128,512]{2,1,0:T(8,128)} %x0_ref.5, f32[1,128,512]{2,1,0:T(8,128)} %s_ref.3, f32[1,128,512]{2,1,0:T(8,128)} %k_ref.3, f32[1,136,272]{2,1,0:T(8,128)} %rows_ref.1, ...), custom_call_target="tpu_custom_call" | custom-call | bytes 4500000 | tf_op jit(solution)/shard_map/pallas_call | solution.py:566
  4.7 7.5 %all-to-all-start = ((f32[16,24,128]{2,1,0:T(8,128)}), f32[16,24,128]{2,1,0:T(8,128)S(1)}, u32[]{:S(2)}, u32[]{:S(2)}) async-start(f32[16,24,128]{2,1,0:T(8,128)} %get-tuple-element.18), calls=%async_computation | async-start | bytes 393216 | tf_op jit(solution)/shard_map/all_to_all | solution.py:563
  12.2 0.4 collective-permute-start
  13.2 0.7 %collective-permute-done.refs_1_ = f32[1,128,512]{2,1,0:T(8,128)S(1)} collective-permute-done((f32[1,128,512]{2,1,0:T(8,128)}, f32[1,128,512]{2,1,0:T(8,128)S(1)}, u32[]{:S(2)}, u32[]{:S(2)}) %collective-permute-start) | collective-permute-done | bytes 262176 | tf_op jit(solution)/shard_map/ppermute | solution.py:559
  14.0 0.9 %copy-done = f32[1,128,512]{2,1,0:T(8,128)S(1)} copy-done((f32[1,128,512]{2,1,0:T(8,128)S(1)}, f32[1,128,512]{2,1,0:T(8,128)}, u32[]{:S(2)}) %copy-start) | copy-done | bytes 262168
  14.9 0.7 copy-done.7
  15.6 5.5 %shard_map.114.spread_ref.flat_ref = f32[16,8,256]{2,1,0:T(8,128)S(1)} custom-call(f32[1,128,512]{2,1,0:T(8,128)S(1)} %copy-done, f32[1,128,512]{2,1,0:T(8,128)S(1)} %collective-permute-done.refs_1_, s32[1,1,1,2,16]{4,3,2,1,0:T(2,128)S(1)} %bitcast.1, f32[1,1,1,16,2,256,256]{6,5,4,3,2,1,0:T(8,128)} %refs_5_.3), custom_call_target="tpu_custom_call" | custom-call | bytes 12000000 | tf_op jit(solution)/shard_map/pallas_call | solution.py:587
  21.2 2.9 %shard_map.115 = (f32[2,128,512]{2,1,0:T(8,128)S(1)}, f32[16,16,128]{2,1,0:T(8,128)}, f32[136,640]{1,0:T(8,128)S(1)}, f32[136,640]{1,0:T(8,128)S(1)}) custom-call(f32[16,24,128]{2,1,0:T(8,128)S(1)} %all-to-all-done.recv_ref, f32[1,128,512]{2,1,0:T(8,128)S(1)} %copy-done.1, f32[1,128,512]{2,1,0:T(8,128)S(1)} %copy-done.3, f32[1,128,512]{2,1,0:T(8,128)S(1)} %copy-done.2, ...), custom_call_target="tpu_custom_call" | custom-call | bytes 9000000 | tf_op jit(solution)/shard_map/pallas_call | solution.py:598
  24.1 0.3 collective-permute-start.4
  24.5 1.7 %collective-permute-start.1 = (f32[168,128]{1,0:T(8,128)S(1)}, f32[168,128]{1,0:T(8,128)S(1)}, u32[]{:S(2)}, u32[]{:S(2)}) collective-permute-start(f32[168,128]{1,0:T(8,128)S(1)} %copy-done.12), channel_id=1, source_target_pairs={{0,4},{4,0},{8,12},{12,8},{1,5},{5,1},{9,13},{13,9},{2,6},{6,2},{1... | collective-permute-start | bytes 258056 | tf_op jit(solution)/shard_map/ppermute | solution.py:577
  26.2 2.3 %collective-permute-start.2 = (f32[168,128]{1,0:T(8,128)S(1)}, f32[168,128]{1,0:T(8,128)S(1)}, u32[]{:S(2)}, u32[]{:S(2)}) collective-permute-start(f32[168,128]{1,0:T(8,128)S(1)} %copy-done.11), channel_id=1, source_target_pairs={{0,8},{4,12},{8,0},{12,4},{1,9},{5,13},{9,1},{13,5},{2,10},{6,14},... | collective-permute-start | bytes 258056 | tf_op jit(solution)/shard_map/ppermute | solution.py:577
  28.5 0.3 collective-permute-start.3
  28.9 5.8 %all-to-all-start.1 = ((f32[16,16,128]{2,1,0:T(8,128)}), f32[16,16,128]{2,1,0:T(8,128)S(1)}, u32[]{:S(2)}, u32[]{:S(2)}) async-start(f32[16,16,128]{2,1,0:T(8,128)} %get-tuple-element.19), calls=%async_computation.1 | async-start | bytes 262144 | tf_op jit(solution)/shard_map/all_to_all | solution.py:563
  34.7 1.3 %collective-permute-done.2 = f32[168,128]{1,0:T(8,128)S(1)} collective-permute-done((f32[168,128]{1,0:T(8,128)S(1)}, f32[168,128]{1,0:T(8,128)S(1)}, u32[]{:S(2)}, u32[]{:S(2)}) %collective-permute-start.2) | collective-permute-done | bytes 86048 | tf_op jit(solution)/shard_map/ppermute | solution.py:577
  36.1 4.8 %shard_map.116.spread_ref = f32[16,4,256]{2,1,0:T(4,128)S(1)} custom-call(f32[2,128,512]{2,1,0:T(8,128)S(1)} %get-tuple-element.24.refs_0_.to_ref, f32[2,128,512]{2,1,0:T(8,128)S(1)} %collective-permute-done.4.refs_1_.tm_ref, f32[136,640]{1,0:T(8,128)S(1)} %get-tuple-element.25.refs_2_.se_ref, f32[1,128,512]{2,1,0:T(8,128)S(1)} %collective-permute-done.5.refs_3_, ...), custom_call_target="tpu_custom_call" | custom-call | bytes 12000000 | tf_op jit(solution)/shard_map/pallas_call | solution.py:587
  40.8 1.8 %all-to-all-done.1.recv_ref = f32[16,16,128]{2,1,0:T(8,128)S(1)} async-done(((f32[16,16,128]{2,1,0:T(8,128)}), f32[16,16,128]{2,1,0:T(8,128)S(1)}, u32[]{:S(2)}, u32[]{:S(2)}) %all-to-all-start.1) | async-done | bytes 131104 | tf_op jit(solution)/shard_map/all_to_all | solution.py:563
  42.6 3.0 %shard_map.117 = (f32[2,128,512]{2,1,0:T(8,128)S(1)}, f32[16,16,128]{2,1,0:T(8,128)}, f32[2,128,512]{2,1,0:T(8,128)S(1)}, f32[8,128]{1,0:T(8,128)S(1)}) custom-call(f32[16,16,128]{2,1,0:T(8,128)S(1)} %all-to-all-done.1.recv_ref, f32[168,128]{1,0:T(8,128)S(1)} %add_add_fusion.lg_ref, f32[2,128,512]{2,1,0:T(8,128)S(1)} %get-tuple-element.24.refs_0_.to_ref, ...), custom_call_target="tpu_custom_call" | custom-call | bytes 9000000 | tf_op jit(solution)/shard_map/pallas_call | solution.py:609
  45.6 0.8 %copy-done.4 = f32[2,128,512]{2,1,0:T(8,128)} copy-done((f32[2,128,512]{2,1,0:T(8,128)}, f32[2,128,512]{2,1,0:T(8,128)S(1)}, u32[]{:S(2)}) %copy-start.4) | copy-done | bytes 524312
  46.5 3.6 %all-to-all-start.2 = ((f32[16,16,128]{2,1,0:T(8,128)}), f32[16,16,128]{2,1,0:T(8,128)S(1)}, u32[]{:S(2)}, u32[]{:S(2)}) async-start(f32[16,16,128]{2,1,0:T(8,128)} %get-tuple-element.27), calls=%async_computation.2 | async-start | bytes 262144 | tf_op jit(solution)/shard_map/all_to_all | solution.py:563
  50.1 4.8 %shard_map.118.spread_ref = f32[16,4,256]{2,1,0:T(4,128)S(1)} custom-call(f32[2,128,512]{2,1,0:T(8,128)S(1)} %get-tuple-element.28.refs_0_.to_ref, f32[2,128,512]{2,1,0:T(8,128)S(1)} %collective-permute-done.6.refs_1_.tm_ref, f32[136,640]{1,0:T(8,128)S(1)} %get-tuple-element.25.refs_2_.se_ref, f32[1,128,512]{2,1,0:T(8,128)S(1)} %collective-permute-done.5.refs_3_, ...), custom_call_target="tpu_custom_call" | custom-call | bytes 12000000 | tf_op jit(solution)/shard_map/pallas_call | solution.py:587
  54.9 3.1 %all-to-all-done.2.recv_ref = f32[16,16,128]{2,1,0:T(8,128)S(1)} async-done(((f32[16,16,128]{2,1,0:T(8,128)}), f32[16,16,128]{2,1,0:T(8,128)S(1)}, u32[]{:S(2)}, u32[]{:S(2)}) %all-to-all-start.2) | async-done | bytes 131104 | tf_op jit(solution)/shard_map/all_to_all | solution.py:563
  58.0 2.6 %shard_map.119 = (f32[2,128,512]{2,1,0:T(8,128)S(1)}, f32[16,1,128]{2,1,0:T(1,128)S(1)}, f32[2,128,512]{2,1,0:T(8,128)S(1)}, f32[8,128]{1,0:T(8,128)}) custom-call(f32[16,16,128]{2,1,0:T(8,128)S(1)} %all-to-all-done.2.recv_ref, f32[168,128]{1,0:T(8,128)S(1)} %add_add_fusion.lg_ref, f32[2,128,512]{2,1,0:T(8,128)S(1)} %get-tuple-element.28.refs_0_.to_ref, ...), custom_call_target="tpu_custom_call" | custom-call | bytes 9000000 | tf_op jit(solution)/shard_map/pallas_call | solution.py:609
  60.6 9.3 %all_to_all.20.recv_ref = f32[16,1,128]{2,1,0:T(1,128)S(1)} all-to-all(f32[16,1,128]{2,1,0:T(1,128)S(1)} %get-tuple-element.30), channel_id=1, replica_groups=mesh['groups'=2,'gx'=4,'gy'=2,'vert'=2] {'gx','gy','vert'}, dimensions={0} | all-to-all | bytes 16384 | tf_op jit(solution)/shard_map/all_to_all | solution.py:563
  69.9 1.0 %shard_map.120 = (f32[1,128,512]{2,1,0:T(8,128)}, f32[1,128,512]{2,1,0:T(8,128)}) custom-call(f32[16,1,128]{2,1,0:T(1,128)S(1)} %all_to_all.20.recv_ref, f32[1,128,512]{2,1,0:T(8,128)S(1)} %copy-done.1, f32[2,128,512]{2,1,0:T(8,128)S(1)} %copy-done.5, f32[2,128,512]{2,1,0:T(8,128)S(1)} %get-tuple-element.32.wz_ref, ...), custom_call_target="tpu_custom_call" | custom-call | bytes 3000000 | tf_op jit(solution)/shard_map/pallas_call | solution.py:636
  (35 shorter events, 0.1 us)
Async XLA Ops:
  0.6 20.5 %copy-start.1 = (f32[1,128,512]{2,1,0:T(8,128)S(1)}, f32[1,128,512]{2,1,0:T(8,128)}, u32[]{:S(2)}) copy-start(f32[1,128,512]{2,1,0:T(8,128)} %x0_ref.5) | copy-start | bytes 786436
  0.6 20.5 %copy-start.3 = (f32[1,128,512]{2,1,0:T(8,128)S(1)}, f32[1,128,512]{2,1,0:T(8,128)}, u32[]{:S(2)}) copy-start(f32[1,128,512]{2,1,0:T(8,128)} %s_ref.3) | copy-start | bytes 786436
  0.7 20.5 %copy-start.2 = (f32[1,128,512]{2,1,0:T(8,128)S(1)}, f32[1,128,512]{2,1,0:T(8,128)}, u32[]{:S(2)}) copy-start(f32[1,128,512]{2,1,0:T(8,128)} %k_ref.3) | copy-start | bytes 786436
  0.7 20.5 %copy-start.8 = (s32[1,1,1,16,2]{3,4,2,1,0:T(2,128)S(1)}, s32[1,1,1,16,2]{3,4,2,1,0:T(2,128)}, u32[]{:S(2)}) copy-start(s32[1,1,1,16,2]{3,4,2,1,0:T(2,128)} %param.16) | copy-start | bytes 388
  0.7 20.5 %copy-start.6 = (f32[1,128,512]{2,1,0:T(8,128)S(1)}, f32[1,128,512]{2,1,0:T(8,128)}, u32[]{:S(2)}) copy-start(f32[1,128,512]{2,1,0:T(8,128)} %b_ref.1) | copy-start | bytes 786436
  4.7 19.8 %copy-start.12 = (f32[168,128]{1,0:T(8,128)S(1)}, f32[168,128]{1,0:T(8,128)}, u32[]{:S(2)}) copy-start(f32[168,128]{1,0:T(8,128)} %get-tuple-element.21) | copy-start | bytes 258052
  4.7 21.5 %copy-start.11 = (f32[168,128]{1,0:T(8,128)S(1)}, f32[168,128]{1,0:T(8,128)}, u32[]{:S(2)}) copy-start(f32[168,128]{1,0:T(8,128)} %get-tuple-element.22) | copy-start | bytes 258052
  4.7 23.8 %copy-start.10 = (f32[168,128]{1,0:T(8,128)S(1)}, f32[168,128]{1,0:T(8,128)}, u32[]{:S(2)}) copy-start(f32[168,128]{1,0:T(8,128)} %get-tuple-element.23) | copy-start | bytes 258052
  4.7 31.3 %copy-start.9 = (f32[168,128]{1,0:T(8,128)S(1)}, f32[168,128]{1,0:T(8,128)}, u32[]{:S(2)}) copy-start(f32[168,128]{1,0:T(8,128)} %get-tuple-element.20) | copy-start | bytes 258052
  4.7 16.5 %all-to-all-start = ((f32[16,24,128]{2,1,0:T(8,128)}), f32[16,24,128]{2,1,0:T(8,128)S(1)}, u32[]{:S(2)}, u32[]{:S(2)}) async-start(f32[16,24,128]{2,1,0:T(8,128)} %get-tuple-element.18), calls=%async_computation | async-start | bytes 393216 | tf_op jit(solution)/shard_map/all_to_all | solution.py:563
  12.2 1.8 %collective-permute-start = (f32[1,128,512]{2,1,0:T(8,128)}, f32[1,128,512]{2,1,0:T(8,128)S(1)}, u32[]{:S(2)}, u32[]{:S(2)}) collective-permute-start(f32[1,128,512]{2,1,0:T(8,128)} %x0_ref.5), channel_id=1, source_target_pairs={{0,1},{1,0},{2,3},{3,2},{4,5},{5,4},{6,7},{7,6},{8,9},{9,8},{10,11... | collective-permute-start | bytes 786440 | tf_op jit(solution)/shard_map/ppermute | solution.py:559
  14.0 1.0 %copy-start = (f32[1,128,512]{2,1,0:T(8,128)S(1)}, f32[1,128,512]{2,1,0:T(8,128)}, u32[]{:S(2)}) copy-start(f32[1,128,512]{2,1,0:T(8,128)} %x0_ref.5) | copy-start | bytes 786436
  14.9 0.7 copy-start.7
  24.1 11.9 %collective-permute-start.4 = (f32[2,128,512]{2,1,0:T(8,128)S(1)}, f32[2,128,512]{2,1,0:T(8,128)S(1)}, u32[]{:S(2)}, u32[]{:S(2)}) collective-permute-start(f32[2,128,512]{2,1,0:T(8,128)S(1)} %get-tuple-element.24.refs_0_.to_ref), channel_id=1, source_target_pairs={{0,1},{1,0},{2,3},{3,2},{4,5},{5,4},{6,7},{7,6},{8,9},{9,8},{10,11... | collective-permute-start | bytes 1572872 | tf_op jit(solution)/shard_map/ppermute | solution.py:623
  24.5 10.2 %collective-permute-start.1 = (f32[168,128]{1,0:T(8,128)S(1)}, f32[168,128]{1,0:T(8,128)S(1)}, u32[]{:S(2)}, u32[]{:S(2)}) collective-permute-start(f32[168,128]{1,0:T(8,128)S(1)} %copy-done.12), channel_id=1, source_target_pairs={{0,4},{4,0},{8,12},{12,8},{1,5},{5,1},{9,13},{13,9},{2,6},{6,2},{1... | collective-permute-start | bytes 258056 | tf_op jit(solution)/shard_map/ppermute | solution.py:577
  26.2 9.8 %collective-permute-start.2 = (f32[168,128]{1,0:T(8,128)S(1)}, f32[168,128]{1,0:T(8,128)S(1)}, u32[]{:S(2)}, u32[]{:S(2)}) collective-permute-start(f32[168,128]{1,0:T(8,128)S(1)} %copy-done.11), channel_id=1, source_target_pairs={{0,8},{4,12},{8,0},{12,4},{1,9},{5,13},{9,1},{13,5},{2,10},{6,14},... | collective-permute-start | bytes 258056 | tf_op jit(solution)/shard_map/ppermute | solution.py:577
  28.5 7.5 %collective-permute-start.3 = (f32[168,128]{1,0:T(8,128)S(1)}, f32[168,128]{1,0:T(8,128)S(1)}, u32[]{:S(2)}, u32[]{:S(2)}) collective-permute-start(f32[168,128]{1,0:T(8,128)S(1)} %copy-done.10), channel_id=1, source_target_pairs={{0,12},{4,8},{8,4},{12,0},{1,13},{5,9},{9,5},{13,1},{2,14},{6,10},... | collective-permute-start | bytes 258056 | tf_op jit(solution)/shard_map/ppermute | solution.py:577
  28.9 7.2 %collective-permute-start.5 = (f32[1,128,512]{2,1,0:T(8,128)S(1)}, f32[1,128,512]{2,1,0:T(8,128)S(1)}, u32[]{:S(2)}, u32[]{:S(2)}) collective-permute-start(f32[1,128,512]{2,1,0:T(8,128)S(1)} %copy-done.3), channel_id=1, source_target_pairs={{0,1},{1,0},{2,3},{3,2},{4,5},{5,4},{6,7},{7,6},{8,9},{9,8},{10,11... | collective-permute-start | bytes 786440 | tf_op jit(solution)/shard_map/ppermute | solution.py:560
  28.9 13.7 %all-to-all-start.1 = ((f32[16,16,128]{2,1,0:T(8,128)}), f32[16,16,128]{2,1,0:T(8,128)S(1)}, u32[]{:S(2)}, u32[]{:S(2)}) async-start(f32[16,16,128]{2,1,0:T(8,128)} %get-tuple-element.19), calls=%async_computation.1 | async-start | bytes 262144 | tf_op jit(solution)/shard_map/all_to_all | solution.py:563
  45.6 0.8 %copy-start.4 = (f32[2,128,512]{2,1,0:T(8,128)}, f32[2,128,512]{2,1,0:T(8,128)S(1)}, u32[]{:S(2)}) copy-start(f32[2,128,512]{2,1,0:T(8,128)S(1)} %get-tuple-element.31.rp_ref) | copy-start | bytes 1572868
  46.5 23.4 %copy-start.5 = (f32[2,128,512]{2,1,0:T(8,128)S(1)}, f32[2,128,512]{2,1,0:T(8,128)}, u32[]{:S(2)}) copy-start(f32[2,128,512]{2,1,0:T(8,128)} %copy-done.4) | copy-start | bytes 1572868
  46.5 3.7 %collective-permute-start.6 = (f32[2,128,512]{2,1,0:T(8,128)S(1)}, f32[2,128,512]{2,1,0:T(8,128)S(1)}, u32[]{:S(2)}, u32[]{:S(2)}) collective-permute-start(f32[2,128,512]{2,1,0:T(8,128)S(1)} %get-tuple-element.28.refs_0_.to_ref), channel_id=1, source_target_pairs={{0,1},{1,0},{2,3},{3,2},{4,5},{5,4},{6,7},{7,6},{8,9},{9,8},{10,11... | collective-permute-start | bytes 1572872 | tf_op jit(solution)/shard_map/ppermute | solution.py:629
  46.5 11.6 %all-to-all-start.2 = ((f32[16,16,128]{2,1,0:T(8,128)}), f32[16,16,128]{2,1,0:T(8,128)S(1)}, u32[]{:S(2)}, u32[]{:S(2)}) async-start(f32[16,16,128]{2,1,0:T(8,128)} %get-tuple-element.27), calls=%async_computation.2 | async-start | bytes 262144 | tf_op jit(solution)/shard_map/all_to_all | solution.py:563
  60.6 9.3 %collective-permute-start.7 = (f32[2,128,512]{2,1,0:T(8,128)S(1)}, f32[2,128,512]{2,1,0:T(8,128)S(1)}, u32[]{:S(2)}, u32[]{:S(2)}) collective-permute-start(f32[2,128,512]{2,1,0:T(8,128)S(1)} %get-tuple-element.33.to_ref), channel_id=1, source_target_pairs={{0,1},{1,0},{2,3},{3,2},{4,5},{5,4},{6,7},{7,6},{8,9},{9,8},{10,11... | collective-permute-start | bytes 1572872 | tf_op jit(solution)/shard_map/ppermute | solution.py:635

commit v3 on v2

--- a/solution.py
+++ b/solution.py
@@ -96,6 +96,11 @@
                 blank = jnp.zeros((sz.lift_rows, LANES - part.shape[1]), F32)
                 part = jnp.concatenate([part, blank], axis=1)
             out_ref[pl.ds(i * sz.lift_rows, sz.lift_rows), :] = part
+
+
+def put_rows(pay_ref, dest, first, block):
+    for i in range(block.shape[0]):
+        pay_ref[dest, first + i] = block[i : i + 1]
 
 
 def setup_kernel(sz, x0_ref, s_ref, k_ref, rows_ref, slots_ref, count_ref, pay_ref, *refs):
@@ -120,9 +125,10 @@
             for at, width in FIELDS:
                 rows = pl.ds(0 if dx < 0 else r - width, width)
                 for j in range(g):
-                    pay_ref[dest, pl.ds(at * 2 * g + j * width, width), :] = tiles_ref[
-                        at, rows, pl.ds(j * LANES, LANES)
-                    ]
+                    put_rows(
+                        pay_ref, dest, at * 2 * g + j * width,
+                        tiles_ref[at, rows, pl.ds(j * LANES, LANES)],
+                    )
 
     for dy in (-1, 1):
         @pl.when((yi + dy >= 0) & (yi + dy < sz.ty))
@@ -131,9 +137,8 @@
             lanes = pl.ds(0 if dy < 0 else c - LANES, LANES)
             for at, width in FIELDS:
                 first = 0 if dy < 0 else LANES - width
-                pay_ref[dest, pl.ds(at * 2 * g, width), :] = tiles_ref[at, :, lanes].T[
-                    first : first + width
-                ]
+                pair = tiles_ref[at, :, lanes].T[first : first + width]
+                put_rows(pay_ref, dest, at * 2 * g, pair)
 
         for dx in (-1, 1):
             @pl.when((xi + dx >= 0) & (xi + dx < sz.tx) & (yi + dy >= 0) & (yi + dy < sz.ty))
@@ -143,7 +148,7 @@
                 rows = pl.ds(0 if dx < 0 else r - 1, 1)
                 for at, width in FIELDS:
                     if width == 2:
-                        pay_ref[dest, pl.ds(at * 2 * g, 1), :] = tiles_ref[at, rows, lanes]
+                        put_rows(pay_ref, dest, at * 2 * g, tiles_ref[at, rows, lanes])
 
 
 def put_borders(sz, ref, width, beside):
@@ -218,6 +223,7 @@
         i, j = n // per_row, lax.rem(n, per_row)
         lanes = pl.ds(pl.multiple_of((j // per_lanes) * LANES, LANES), LANES)
         here = lane // BSIDE == lax.rem(j, per_lanes)
+        both = []
         for h in range(2):
             line = spread_ref[q // sz.reach, pl.ds(q % sz.reach, 1), pl.ds(h * LANES, LANES)]
             if flat_ref is not None:
@@ -231,8 +237,9 @@
             part = jnp.where(diag, line, 0.0)
             for step in (16, 32, 64):
                 part = part + pltpu.roll(part, step, 1)
-            at = pl.ds(pl.multiple_of(i * BSIDE + h * PAD, PAD), PAD)
-            t_ref[var, at, lanes] = t_ref[var, at, lanes] + sign * jnp.where(here, part, 0.0)
+            both.append(jnp.where(here, part, 0.0))
+        at = pl.ds(pl.multiple_of(i * BSIDE, BSIDE), BSIDE)
+        t_ref[var, at, lanes] = t_ref[var, at, lanes] + sign * jnp.concatenate(both, axis=0)
     return crossed
 
 
@@ -386,7 +393,8 @@
     if var is None:
         found = recv_ref[source, rows, :] + recv_ref[source + 1, rows, :]
     else:
-        found = recv_ref[source + var, rows, :]
+        found = [recv_ref[source + var, row] for row in range(first, first + count)]
+        found = jnp.concatenate(found, axis=0)
     return jnp.where(inside, found, 0.0)
 
 
@@ -405,7 +413,7 @@
         v2_ref[0] = scale * (to_ref[0] + tm_ref[1])
         v2_ref[1] = sp_ref[0] * (tm_ref[0] + to_ref[1])
     gather_patches(sz, v2_ref, cols_ref, out_ref)
-    observe_spread(sz, phi_ref, buf_ref, sems, out_ref, stage == 0)
+    observe_spread(sz, phi_ref, buf_ref, sems, out_ref, stage == 1)
 
 
 def first_kernel(sz, recv_ref, x0_ref, s_ref, k_ref, b_ref, spread_ref, cols_ref, w_ref,
@@ -565,7 +573,7 @@
     cap = coarse_slots.shape[1]
     edges, *shares = pl.pallas_call(
         functools.partial(setup_kernel, sz),
-        out_shape=[shape(sz.devices, PAD * (-(-5 * sz.groups // PAD)), LANES)]
+        out_shape=[shape(sz.devices, 5 * sz.groups, 1, LANES)]
         + [shape(sz.vec_rows * sz.lift_rows, LANES)] * tx,
         in_specs=[ANY] * 4 + [VMEM, SMEM],
         out_specs=[VMEM] * (1 + tx),
@@ -576,6 +584,7 @@
     )(initial_guess, precond_scale, kappa_sq, coarse_rows, coarse_slots, slot_count)
     got = [lax.ppermute(shares[k], "gx", [(i, i ^ k) for i in range(tx)]) for k in range(1, tx)]
     lift_matrix = sum(got, shares[0])
+    edges, x_partner = lax.optimization_barrier((edges, x_partner))
     edges = exchange(edges)
 
     r, c = sz.rows, sz.cols
@@ -586,7 +595,7 @@
     def data(stage, *fields):
         return pl.pallas_call(
             functools.partial(data_kernel, sz, stage),
-            out_shape=shape(sz.obs, sz.reach * (2 + sz.reach * (stage == 0)), block),
+            out_shape=shape(sz.obs, sz.reach * (2 + sz.reach * (stage == 1)), block),
             in_specs=[VMEM] * len(fields) + [SMEM, ANY],
             out_specs=VMEM,
             scratch_shapes=data_space(sz),
@@ -594,7 +603,7 @@
             cost_estimate=cost(4),
         )(*fields, phi_cols, phi_vals)
 
-    flat = data(0, initial_guess, x_partner)
+    first_spread = data(0, initial_guess, x_partner)
     parts, sent, s_ext, k_ext = pl.pallas_call(
         functools.partial(first_kernel, sz),
         out_shape=[pair, payload, shape(*sz.ext), shape(*sz.ext)],
@@ -603,9 +612,9 @@
         scratch_shapes=[pltpu.VMEM(sz.ext, F32)] * 2,
         compiler_params=PARAMS,
         cost_estimate=cost(3),
-    )(edges, initial_guess, precond_scale, kappa_sq, right_side, flat, phi_cols, smooth_weight)
-
-    def apply(last, received, parts, mirrored, dots, spread):
+    )(edges, initial_guess, precond_scale, kappa_sq, right_side, first_spread, phi_cols, smooth_weight)
+
+    def apply(last, received, parts, mirrored, dots, spread, flat):
         return pl.pallas_call(
             functools.partial(apply_kernel, sz, last),
             out_shape=[pair, shape(sz.devices, 1, LANES) if last else payload,
@@ -622,15 +631,15 @@
     dots = jnp.zeros((PAD, LANES), F32)
     mirrored = lax.ppermute(parts, "vert", swap)
     received = exchange(sent)
-    spread = data(1, parts, mirrored, s_ext, s_partner)
+    flat = data(1, parts, mirrored, s_ext, s_partner)
     parts, sent, early, dots = apply(
-        False, received, parts, mirrored, dots, spread
+        False, received, parts, mirrored, dots, flat, flat
     )
     mirrored = lax.ppermute(parts, "vert", swap)
     received = exchange(sent)
     spread = data(2, parts, mirrored, s_ext, s_partner)
     parts, sent, late, dots = apply(
-        True, received, parts, mirrored, dots, spread
+        True, received, parts, mirrored, dots, spread, flat
     )
     mirrored = lax.ppermute(parts, "vert", swap)
     return tuple(pl.pallas_call(

time: 71.4 us -> 69.4 us (0.972)
  starting transfers between devices: 22 us -> 20.8 us
    all_to_all x3, starting transfers between devices: 16.9 us -> 15.9 us  [exchange(): return lax.all_to_all(array, ALL, 0, 0, tiled=True)]
    ppermute x1, waiting for transfers between devices: 0.75 us -> 0.01 us  [local(): x_partner = lax.ppermute(initial_guess, 'vert', swap)]
  transfers between devices with their start and end apart: 11 -> 11, of which waited for: 4 -> 4; matrix products, arithmetic and copies ran while one was open for 0% -> 0% of each run, Pallas kernels for 21% -> 27%
where the time goes in v3:
time: 69.4 us; the launch traced here: 68.9 us
  Pallas kernels  27.3 us (39%)
  starting transfers between devices  20.8 us (30%)
  blocking collectives  9.26 us (13%)
  waiting for transfers between devices  6.86 us (10%)
  local copies, waits for them, and re-layouts  2.5 us (4%)
  between operations  2.13 us (3%)
    all_to_all x3, starting transfers between devices, exchange(): return lax.all_to_all(array, ALL, 0, 0, tiled=True)  15.9 us
    pallas_call x3, Pallas kernels, data(): pl.pallas_call(functools.partial(data_kernel, sz, stage), out_shape=shape...  15.1 us
    all_to_all x1, blocking collectives, exchange(): return lax.all_to_all(array, ALL, 0, 0, tiled=True)  9.26 us
    all_to_all x3, waiting for transfers between devices, exchange(): return lax.all_to_all(array, ALL, 0, 0, tiled=True)  5.44 us
    pallas_call x2, Pallas kernels, apply(): pl.pallas_call(functools.partial(apply_kernel, sz, last), out_shape=[pair...  5.35 us
    ppermute x3, starting transfers between devices, local(): lax.ppermute(shares[k], 'gx', [(i, i ^ k) for i in range(tx)])  4.39 us
    pallas_call x1, Pallas kernels, local(): pl.pallas_call(functools.partial(setup_kernel, sz), out_shape=[shape(sz.d...  3.23 us
    pallas_call x1, Pallas kernels, local(): pl.pallas_call(functools.partial(first_kernel, sz), out_shape=[pair, payl...  2.67 us
  transfers between devices with their start and end apart: 11, of which 4 were waited for; matrix products, arithmetic and copies ran while one was open for 0% of the time, Pallas kernels for 27%

profile of v3, /device:TPU:0, one launch (start us, length us, event | category | flops | bytes accessed | tf_op | source)
XLA Modules:
  0.0 68.9 jit_solution(15265649703973438014)
XLA Ops:
  0.6 0.0 copy-start.1
  0.7 0.5 collective-permute-start
  1.9 3.2 %shard_map.113 = (f32[16,20,1,128]{3,2,1,0:T(1,128)}, f32[168,128]{1,0:T(8,128)}, f32[168,128]{1,0:T(8,128)}, f32[168,128]{1,0:T(8,128)}, f32[168,128]{1,0:T(8,128)}) custom-call(f32[1,128,512]{2,1,0:T(8,128)} %x0_ref.5, f32[1,128,512]{2,1,0:T(8,128)} %s_ref.3, f32[1,128,512]{2,1,0:T(8,128)} %k_ref.3, f32[1,136,272]{2,1,0:T(8,128)} %rows_ref.1, ...), custom_call_target="tpu_custom_call" | custom-call | bytes 4500000 | tf_op jit(solution)/shard_map/pallas_call | solution.py:574
  5.1 7.1 %all-to-all-start = ((f32[16,20,1,128]{3,2,1,0:T(1,128)}), f32[16,20,1,128]{3,2,1,0:T(1,128)S(1)}, u32[]{:S(2)}, u32[]{:S(2)}) async-start(f32[16,20,1,128]{3,2,1,0:T(1,128)} %get-tuple-element.21), calls=%async_computation | async-start | bytes 327680 | tf_op jit(solution)/shard_map/all_to_all | solution.py:571
  12.9 0.9 %copy-done = f32[1,128,512]{2,1,0:T(8,128)S(1)} copy-done((f32[1,128,512]{2,1,0:T(8,128)S(1)}, f32[1,128,512]{2,1,0:T(8,128)}, u32[]{:S(2)}) %copy-start) | copy-done | bytes 262168
  13.9 0.7 copy-done.7
  14.5 4.8 %shard_map.114.spread_ref = f32[16,4,256]{2,1,0:T(4,128)S(1)} custom-call(f32[1,128,512]{2,1,0:T(8,128)S(1)} %copy-done, f32[1,128,512]{2,1,0:T(8,128)S(1)} %collective-permute-done.refs_1_, s32[1,1,1,2,16]{4,3,2,1,0:T(2,128)S(1)} %bitcast.1, f32[1,1,1,16,2,256,256]{6,5,4,3,2,1,0:T(8,128)} %refs_5_.3), custom_call_target="tpu_custom_call" | custom-call | bytes 12000000 | tf_op jit(solution)/shard_map/pallas_call | solution.py:596
  19.3 1.4 %all-to-all-done.recv_ref = f32[16,20,1,128]{3,2,1,0:T(1,128)S(1)} async-done(((f32[16,20,1,128]{3,2,1,0:T(1,128)}), f32[16,20,1,128]{3,2,1,0:T(1,128)S(1)}, u32[]{:S(2)}, u32[]{:S(2)}) %all-to-all-start) | async-done | bytes 163872 | tf_op jit(solution)/shard_map/all_to_all | solution.py:571
  20.8 2.7 %shard_map.115 = (f32[2,128,512]{2,1,0:T(8,128)S(1)}, f32[16,16,128]{2,1,0:T(8,128)}, f32[136,640]{1,0:T(8,128)S(1)}, f32[136,640]{1,0:T(8,128)S(1)}) custom-call(f32[16,20,1,128]{3,2,1,0:T(1,128)S(1)} %all-to-all-done.recv_ref, f32[1,128,512]{2,1,0:T(8,128)S(1)} %copy-done.1, f32[1,128,512]{2,1,0:T(8,128)S(1)} %copy-done.3, f32[1,128,512]{2,1,0:T(8,128)S(1)} %copy-done.2, ...), custom_call_target="tpu_custom_call" | custom-call | bytes 9000000 | tf_op jit(solution)/shard_map/pallas_call | solution.py:607
  23.4 0.7 %collective-permute-start.1 = (f32[168,128]{1,0:T(8,128)S(1)}, f32[168,128]{1,0:T(8,128)S(1)}, u32[]{:S(2)}, u32[]{:S(2)}) collective-permute-start(f32[168,128]{1,0:T(8,128)S(1)} %copy-done.12), channel_id=1, source_target_pairs={{0,4},{4,0},{8,12},{12,8},{1,5},{5,1},{9,13},{13,9},{2,6},{6,2},{1... | collective-permute-start | bytes 258056 | tf_op jit(solution)/shard_map/ppermute | solution.py:585
  24.2 2.3 %collective-permute-start.2 = (f32[168,128]{1,0:T(8,128)S(1)}, f32[168,128]{1,0:T(8,128)S(1)}, u32[]{:S(2)}, u32[]{:S(2)}) collective-permute-start(f32[168,128]{1,0:T(8,128)S(1)} %copy-done.11), channel_id=1, source_target_pairs={{0,8},{4,12},{8,0},{12,4},{1,9},{5,13},{9,1},{13,5},{2,10},{6,14},... | collective-permute-start | bytes 258056 | tf_op jit(solution)/shard_map/ppermute | solution.py:585
  26.5 1.3 %collective-permute-start.3 = (f32[168,128]{1,0:T(8,128)S(1)}, f32[168,128]{1,0:T(8,128)S(1)}, u32[]{:S(2)}, u32[]{:S(2)}) collective-permute-start(f32[168,128]{1,0:T(8,128)S(1)} %copy-done.10), channel_id=1, source_target_pairs={{0,12},{4,8},{8,4},{12,0},{1,13},{5,9},{9,5},{13,1},{2,14},{6,10},... | collective-permute-start | bytes 258056 | tf_op jit(solution)/shard_map/ppermute | solution.py:585
  27.8 4.8 %all-to-all-start.1 = ((f32[16,16,128]{2,1,0:T(8,128)}), f32[16,16,128]{2,1,0:T(8,128)S(1)}, u32[]{:S(2)}, u32[]{:S(2)}) async-start(f32[16,16,128]{2,1,0:T(8,128)} %get-tuple-element.23), calls=%async_computation.1 | async-start | bytes 262144 | tf_op jit(solution)/shard_map/all_to_all | solution.py:571
  32.7 1.4 %collective-permute-done.2 = f32[168,128]{1,0:T(8,128)S(1)} collective-permute-done((f32[168,128]{1,0:T(8,128)S(1)}, f32[168,128]{1,0:T(8,128)S(1)}, u32[]{:S(2)}, u32[]{:S(2)}) %collective-permute-start.2) | collective-permute-done | bytes 86048 | tf_op jit(solution)/shard_map/ppermute | solution.py:585
  34.1 5.6 %shard_map.116.spread_ref.flat_ref = f32[16,8,256]{2,1,0:T(8,128)S(1)} custom-call(f32[2,128,512]{2,1,0:T(8,128)S(1)} %get-tuple-element.28.refs_0_.to_ref, f32[2,128,512]{2,1,0:T(8,128)S(1)} %collective-permute-done.4.refs_1_.tm_ref, f32[136,640]{1,0:T(8,128)S(1)} %get-tuple-element.29.refs_2_.se_ref, f32[1,128,512]{2,1,0:T(8,128)S(1)} %collective-permute-done.5.refs_3_, ...), custom_call_target="tpu_custom_call" | custom-call | bytes 12000000 | tf_op jit(solution)/shard_map/pallas_call | solution.py:596
  39.7 0.9 %all-to-all-done.1.recv_ref = f32[16,16,128]{2,1,0:T(8,128)S(1)} async-done(((f32[16,16,128]{2,1,0:T(8,128)}), f32[16,16,128]{2,1,0:T(8,128)S(1)}, u32[]{:S(2)}, u32[]{:S(2)}) %all-to-all-start.1) | async-done | bytes 131104 | tf_op jit(solution)/shard_map/all_to_all | solution.py:571
  40.6 2.9 %shard_map.117 = (f32[2,128,512]{2,1,0:T(8,128)S(1)}, f32[16,16,128]{2,1,0:T(8,128)}, f32[2,128,512]{2,1,0:T(8,128)S(1)}, f32[8,128]{1,0:T(8,128)S(1)}) custom-call(f32[16,16,128]{2,1,0:T(8,128)S(1)} %all-to-all-done.1.recv_ref, f32[168,128]{1,0:T(8,128)S(1)} %add_add_fusion.lg_ref, f32[2,128,512]{2,1,0:T(8,128)S(1)} %get-tuple-element.28.refs_0_.to_ref, ...), custom_call_target="tpu_custom_call" | custom-call | bytes 9000000 | tf_op jit(solution)/shard_map/pallas_call | solution.py:618
  43.5 0.8 %copy-done.4 = f32[2,128,512]{2,1,0:T(8,128)} copy-done((f32[2,128,512]{2,1,0:T(8,128)}, f32[2,128,512]{2,1,0:T(8,128)S(1)}, u32[]{:S(2)}) %copy-start.4) | copy-done | bytes 524312
  44.3 3.9 %all-to-all-start.2 = ((f32[16,16,128]{2,1,0:T(8,128)}), f32[16,16,128]{2,1,0:T(8,128)S(1)}, u32[]{:S(2)}, u32[]{:S(2)}) async-start(f32[16,16,128]{2,1,0:T(8,128)} %get-tuple-element.31), calls=%async_computation.2 | async-start | bytes 262144 | tf_op jit(solution)/shard_map/all_to_all | solution.py:571
  48.3 4.8 %shard_map.118.spread_ref = f32[16,4,256]{2,1,0:T(4,128)S(1)} custom-call(f32[2,128,512]{2,1,0:T(8,128)S(1)} %get-tuple-element.32.refs_0_.to_ref, f32[2,128,512]{2,1,0:T(8,128)S(1)} %collective-permute-done.6.refs_1_.tm_ref, f32[136,640]{1,0:T(8,128)S(1)} %get-tuple-element.29.refs_2_.se_ref, f32[1,128,512]{2,1,0:T(8,128)S(1)} %collective-permute-done.5.refs_3_, ...), custom_call_target="tpu_custom_call" | custom-call | bytes 12000000 | tf_op jit(solution)/shard_map/pallas_call | solution.py:596
  53.1 3.1 %all-to-all-done.2.recv_ref = f32[16,16,128]{2,1,0:T(8,128)S(1)} async-done(((f32[16,16,128]{2,1,0:T(8,128)}), f32[16,16,128]{2,1,0:T(8,128)S(1)}, u32[]{:S(2)}, u32[]{:S(2)}) %all-to-all-start.2) | async-done | bytes 131104 | tf_op jit(solution)/shard_map/all_to_all | solution.py:571
  56.2 2.4 %shard_map.119 = (f32[2,128,512]{2,1,0:T(8,128)S(1)}, f32[16,1,128]{2,1,0:T(1,128)S(1)}, f32[2,128,512]{2,1,0:T(8,128)S(1)}, f32[8,128]{1,0:T(8,128)}) custom-call(f32[16,16,128]{2,1,0:T(8,128)S(1)} %all-to-all-done.2.recv_ref, f32[168,128]{1,0:T(8,128)S(1)} %add_add_fusion.lg_ref, f32[2,128,512]{2,1,0:T(8,128)S(1)} %get-tuple-element.32.refs_0_.to_ref, ...), custom_call_target="tpu_custom_call" | custom-call | bytes 9000000 | tf_op jit(solution)/shard_map/pallas_call | solution.py:618
  58.7 9.3 %all_to_all.20.recv_ref = f32[16,1,128]{2,1,0:T(1,128)S(1)} all-to-all(f32[16,1,128]{2,1,0:T(1,128)S(1)} %get-tuple-element.34), channel_id=1, replica_groups=mesh['groups'=2,'gx'=4,'gy'=2,'vert'=2] {'gx','gy','vert'}, dimensions={0} | all-to-all | bytes 16384 | tf_op jit(solution)/shard_map/all_to_all | solution.py:571
  67.9 1.0 %shard_map.120 = (f32[1,128,512]{2,1,0:T(8,128)}, f32[1,128,512]{2,1,0:T(8,128)}) custom-call(f32[16,1,128]{2,1,0:T(1,128)S(1)} %all_to_all.20.recv_ref, f32[1,128,512]{2,1,0:T(8,128)S(1)} %copy-done.1, f32[2,128,512]{2,1,0:T(8,128)S(1)} %copy-done.5, f32[2,128,512]{2,1,0:T(8,128)S(1)} %get-tuple-element.36.wz_ref, ...), custom_call_target="tpu_custom_call" | custom-call | bytes 3000000 | tf_op jit(solution)/shard_map/pallas_call | solution.py:645
  (35 shorter events, 0.1 us)
Async XLA Ops:
  0.6 20.1 %copy-start.1 = (f32[1,128,512]{2,1,0:T(8,128)S(1)}, f32[1,128,512]{2,1,0:T(8,128)}, u32[]{:S(2)}) copy-start(f32[1,128,512]{2,1,0:T(8,128)} %x0_ref.5) | copy-start | bytes 786436
  0.6 20.1 %copy-start.3 = (f32[1,128,512]{2,1,0:T(8,128)S(1)}, f32[1,128,512]{2,1,0:T(8,128)}, u32[]{:S(2)}) copy-start(f32[1,128,512]{2,1,0:T(8,128)} %s_ref.3) | copy-start | bytes 786436
  0.7 20.1 %copy-start.2 = (f32[1,128,512]{2,1,0:T(8,128)S(1)}, f32[1,128,512]{2,1,0:T(8,128)}, u32[]{:S(2)}) copy-start(f32[1,128,512]{2,1,0:T(8,128)} %k_ref.3) | copy-start | bytes 786436
  0.7 20.1 %copy-start.8 = (s32[1,1,1,16,2]{3,4,2,1,0:T(2,128)S(1)}, s32[1,1,1,16,2]{3,4,2,1,0:T(2,128)}, u32[]{:S(2)}) copy-start(s32[1,1,1,16,2]{3,4,2,1,0:T(2,128)} %param.16) | copy-start | bytes 388
  0.7 20.1 %copy-start.6 = (f32[1,128,512]{2,1,0:T(8,128)S(1)}, f32[1,128,512]{2,1,0:T(8,128)}, u32[]{:S(2)}) copy-start(f32[1,128,512]{2,1,0:T(8,128)} %b_ref.1) | copy-start | bytes 786436
  0.7 4.4 %collective-permute-start = (f32[1,128,512]{2,1,0:T(8,128)}, f32[1,128,512]{2,1,0:T(8,128)S(1)}, u32[]{:S(2)}, u32[]{:S(2)}) collective-permute-start(f32[1,128,512]{2,1,0:T(8,128)} %x0_ref.5), channel_id=1, source_target_pairs={{0,1},{1,0},{2,3},{3,2},{4,5},{5,4},{6,7},{7,6},{8,9},{9,8},{10,11... | collective-permute-start | bytes 786440 | tf_op jit(solution)/shard_map/ppermute | solution.py:567
  5.1 19.1 %copy-start.11 = (f32[168,128]{1,0:T(8,128)S(1)}, f32[168,128]{1,0:T(8,128)}, u32[]{:S(2)}) copy-start(f32[168,128]{1,0:T(8,128)} %get-tuple-element.26) | copy-start | bytes 258052
  5.1 21.4 %copy-start.10 = (f32[168,128]{1,0:T(8,128)S(1)}, f32[168,128]{1,0:T(8,128)}, u32[]{:S(2)}) copy-start(f32[168,128]{1,0:T(8,128)} %get-tuple-element.27) | copy-start | bytes 258052
  5.1 29.0 %copy-start.9 = (f32[168,128]{1,0:T(8,128)S(1)}, f32[168,128]{1,0:T(8,128)}, u32[]{:S(2)}) copy-start(f32[168,128]{1,0:T(8,128)} %get-tuple-element.24) | copy-start | bytes 258052
  5.1 15.6 %all-to-all-start = ((f32[16,20,1,128]{3,2,1,0:T(1,128)}), f32[16,20,1,128]{3,2,1,0:T(1,128)S(1)}, u32[]{:S(2)}, u32[]{:S(2)}) async-start(f32[16,20,1,128]{3,2,1,0:T(1,128)} %get-tuple-element.21), calls=%async_computation | async-start | bytes 327680 | tf_op jit(solution)/shard_map/all_to_all | solution.py:571
  12.9 1.0 %copy-start = (f32[1,128,512]{2,1,0:T(8,128)S(1)}, f32[1,128,512]{2,1,0:T(8,128)}, u32[]{:S(2)}) copy-start(f32[1,128,512]{2,1,0:T(8,128)} %x0_ref.5) | copy-start | bytes 786436
  13.9 0.7 copy-start.7
  14.5 8.9 %copy-start.12 = (f32[168,128]{1,0:T(8,128)S(1)}, f32[168,128]{1,0:T(8,128)}, u32[]{:S(2)}) copy-start(f32[168,128]{1,0:T(8,128)} %get-tuple-element.25) | copy-start | bytes 258052
  23.4 10.7 %collective-permute-start.4 = (f32[2,128,512]{2,1,0:T(8,128)S(1)}, f32[2,128,512]{2,1,0:T(8,128)S(1)}, u32[]{:S(2)}, u32[]{:S(2)}) collective-permute-start(f32[2,128,512]{2,1,0:T(8,128)S(1)} %get-tuple-element.28.refs_0_.to_ref), channel_id=1, source_target_pairs={{0,1},{1,0},{2,3},{3,2},{4,5},{5,4},{6,7},{7,6},{8,9},{9,8},{10,11... | collective-permute-start | bytes 1572872 | tf_op jit(solution)/shard_map/ppermute | solution.py:632
  23.4 9.2 %collective-permute-start.1 = (f32[168,128]{1,0:T(8,128)S(1)}, f32[168,128]{1,0:T(8,128)S(1)}, u32[]{:S(2)}, u32[]{:S(2)}) collective-permute-start(f32[168,128]{1,0:T(8,128)S(1)} %copy-done.12), channel_id=1, source_target_pairs={{0,4},{4,0},{8,12},{12,8},{1,5},{5,1},{9,13},{13,9},{2,6},{6,2},{1... | collective-permute-start | bytes 258056 | tf_op jit(solution)/shard_map/ppermute | solution.py:585
  24.2 9.9 %collective-permute-start.2 = (f32[168,128]{1,0:T(8,128)S(1)}, f32[168,128]{1,0:T(8,128)S(1)}, u32[]{:S(2)}, u32[]{:S(2)}) collective-permute-start(f32[168,128]{1,0:T(8,128)S(1)} %copy-done.11), channel_id=1, source_target_pairs={{0,8},{4,12},{8,0},{12,4},{1,9},{5,13},{9,1},{13,5},{2,10},{6,14},... | collective-permute-start | bytes 258056 | tf_op jit(solution)/shard_map/ppermute | solution.py:585
  26.5 7.6 %collective-permute-start.3 = (f32[168,128]{1,0:T(8,128)S(1)}, f32[168,128]{1,0:T(8,128)S(1)}, u32[]{:S(2)}, u32[]{:S(2)}) collective-permute-start(f32[168,128]{1,0:T(8,128)S(1)} %copy-done.10), channel_id=1, source_target_pairs={{0,12},{4,8},{8,4},{12,0},{1,13},{5,9},{9,5},{13,1},{2,14},{6,10},... | collective-permute-start | bytes 258056 | tf_op jit(solution)/shard_map/ppermute | solution.py:585
  27.8 6.3 %collective-permute-start.5 = (f32[1,128,512]{2,1,0:T(8,128)S(1)}, f32[1,128,512]{2,1,0:T(8,128)S(1)}, u32[]{:S(2)}, u32[]{:S(2)}) collective-permute-start(f32[1,128,512]{2,1,0:T(8,128)S(1)} %copy-done.3), channel_id=1, source_target_pairs={{0,1},{1,0},{2,3},{3,2},{4,5},{5,4},{6,7},{7,6},{8,9},{9,8},{10,11... | collective-permute-start | bytes 786440 | tf_op jit(solution)/shard_map/ppermute | solution.py:568
  27.8 12.8 %all-to-all-start.1 = ((f32[16,16,128]{2,1,0:T(8,128)}), f32[16,16,128]{2,1,0:T(8,128)S(1)}, u32[]{:S(2)}, u32[]{:S(2)}) async-start(f32[16,16,128]{2,1,0:T(8,128)} %get-tuple-element.23), calls=%async_computation.1 | async-start | bytes 262144 | tf_op jit(solution)/shard_map/all_to_all | solution.py:571
  43.5 0.8 %copy-start.4 = (f32[2,128,512]{2,1,0:T(8,128)}, f32[2,128,512]{2,1,0:T(8,128)S(1)}, u32[]{:S(2)}) copy-start(f32[2,128,512]{2,1,0:T(8,128)S(1)} %get-tuple-element.35.rp_ref) | copy-start | bytes 1572868
  44.3 23.6 %copy-start.5 = (f32[2,128,512]{2,1,0:T(8,128)S(1)}, f32[2,128,512]{2,1,0:T(8,128)}, u32[]{:S(2)}) copy-start(f32[2,128,512]{2,1,0:T(8,128)} %copy-done.4) | copy-start | bytes 1572868
  44.3 4.0 %collective-permute-start.6 = (f32[2,128,512]{2,1,0:T(8,128)S(1)}, f32[2,128,512]{2,1,0:T(8,128)S(1)}, u32[]{:S(2)}, u32[]{:S(2)}) collective-permute-start(f32[2,128,512]{2,1,0:T(8,128)S(1)} %get-tuple-element.32.refs_0_.to_ref), channel_id=1, source_target_pairs={{0,1},{1,0},{2,3},{3,2},{4,5},{5,4},{6,7},{7,6},{8,9},{9,8},{10,11... | collective-permute-start | bytes 1572872 | tf_op jit(solution)/shard_map/ppermute | solution.py:638
  44.3 11.9 %all-to-all-start.2 = ((f32[16,16,128]{2,1,0:T(8,128)}), f32[16,16,128]{2,1,0:T(8,128)S(1)}, u32[]{:S(2)}, u32[]{:S(2)}) async-start(f32[16,16,128]{2,1,0:T(8,128)} %get-tuple-element.31), calls=%async_computation.2 | async-start | bytes 262144 | tf_op jit(solution)/shard_map/all_to_all | solution.py:571
  58.7 9.3 %collective-permute-start.7 = (f32[2,128,512]{2,1,0:T(8,128)S(1)}, f32[2,128,512]{2,1,0:T(8,128)S(1)}, u32[]{:S(2)}, u32[]{:S(2)}) collective-permute-start(f32[2,128,512]{2,1,0:T(8,128)S(1)} %get-tuple-element.37.to_ref), channel_id=1, source_target_pairs={{0,1},{1,0},{2,3},{3,2},{4,5},{5,4},{6,7},{7,6},{8,9},{9,8},{10,11... | collective-permute-start | bytes 1572872 | tf_op jit(solution)/shard_map/ppermute | solution.py:644

commit v4 on v3

--- a/solution.py
+++ b/solution.py
@@ -400,7 +400,7 @@
 
 def data_kernel(sz, stage, *refs):
     if stage == 0:
-        x_ref, xp_ref, cols_ref, phi_ref, out_ref = refs[:5]
+        x_ref, xp_ref, cols_ref, phi_ref, terms_ref, out_ref = refs[:6]
     else:
         to_ref, tm_ref, s_ref, sp_ref, cols_ref, phi_ref, out_ref = refs[:7]
     v2_ref, buf_ref, sems = refs[-3:]
@@ -414,9 +414,12 @@
         v2_ref[1] = sp_ref[0] * (tm_ref[0] + to_ref[1])
     gather_patches(sz, v2_ref, cols_ref, out_ref)
     observe_spread(sz, phi_ref, buf_ref, sems, out_ref, stage == 1)
-
-
-def first_kernel(sz, recv_ref, x0_ref, s_ref, k_ref, b_ref, spread_ref, cols_ref, w_ref,
+    if stage == 0:
+        terms_ref[...] = jnp.zeros_like(terms_ref)
+        scatter_patches(sz, terms_ref, cols_ref, out_ref, -1.0)
+
+
+def first_kernel(sz, recv_ref, x0_ref, s_ref, k_ref, b_ref, terms_ref, w_ref,
                  t_ref, pay_ref, se_ref, ke_ref, v_ref, y_ref):
     vi = lax.axis_index("vert")
     r, c, g = sz.rows, sz.cols, sz.groups
@@ -428,9 +431,8 @@
 
         ref[pl.ds(0, r), pl.ds(0, c)] = src[0]
         put_borders(sz, ref, width, beside)
-    t_ref[0] = b_ref[0] - w_ref[0] * smooth(sz, v_ref, ke_ref, y_ref)
-    t_ref[1] = jnp.zeros((r, c), F32)
-    scatter_patches(sz, t_ref, cols_ref, spread_ref, -1.0)
+    t_ref[0] = (b_ref[0] + terms_ref[0]) - w_ref[0] * smooth(sz, v_ref, ke_ref, y_ref)
+    t_ref[1] = terms_ref[1]
     pack_payload(sz, t_ref, pay_ref)
 
 
@@ -593,26 +595,27 @@
     payload = shape(sz.devices, sz.head + PAD, LANES)
 
     def data(stage, *fields):
+        lines = (sz.obs, sz.reach * (2 + sz.reach * (stage == 1)))
         return pl.pallas_call(
             functools.partial(data_kernel, sz, stage),
-            out_shape=shape(sz.obs, sz.reach * (2 + sz.reach * (stage == 1)), block),
+            out_shape=pair if stage == 0 else shape(*lines, block),
             in_specs=[VMEM] * len(fields) + [SMEM, ANY],
             out_specs=VMEM,
-            scratch_shapes=data_space(sz),
+            scratch_shapes=[pltpu.VMEM(lines + (block,), F32)] * (stage == 0) + data_space(sz),
             compiler_params=DATA_PARAMS,
             cost_estimate=cost(4),
         )(*fields, phi_cols, phi_vals)
 
-    first_spread = data(0, initial_guess, x_partner)
+    terms = data(0, initial_guess, x_partner)
     parts, sent, s_ext, k_ext = pl.pallas_call(
         functools.partial(first_kernel, sz),
         out_shape=[pair, payload, shape(*sz.ext), shape(*sz.ext)],
-        in_specs=[VMEM] * 6 + [SMEM, SMEM],
+        in_specs=[VMEM] * 6 + [SMEM],
         out_specs=[VMEM] * 4,
         scratch_shapes=[pltpu.VMEM(sz.ext, F32)] * 2,
         compiler_params=PARAMS,
         cost_estimate=cost(3),
-    )(edges, initial_guess, precond_scale, kappa_sq, right_side, first_spread, phi_cols, smooth_weight)
+    )(edges, initial_guess, precond_scale, kappa_sq, right_side, terms, smooth_weight)
 
     def apply(last, received, parts, mirrored, dots, spread, flat):
         return pl.pallas_call(

time: 69.4 us -> 69 us (level)
    pallas_call x1, Pallas kernels: 2.67 us -> 1.62 us  [local(): pl.pallas_call(functools.partial(first_kernel, sz), out_shape=[pair, payl...]
  transfers between devices with their start and end apart: 11 -> 11, of which waited for: 4 -> 4; matrix products, arithmetic and copies ran while one was open for 0% -> 0% of each run, Pallas kernels for 27% -> 28%
where the time goes in v4:
time: 69 us; the launch traced here: 68.4 us
  Pallas kernels  26.8 us (39%)
  starting transfers between devices  21.4 us (31%)
  blocking collectives  9.26 us (13%)
  waiting for transfers between devices  6.28 us (9%)
  local copies, waits for them, and re-layouts  2.5 us (4%)
  between operations  2.13 us (3%)
    all_to_all x3, starting transfers between devices, exchange(): return lax.all_to_all(array, ALL, 0, 0, tiled=True)  16.5 us
    pallas_call x3, Pallas kernels, data(): pl.pallas_call(functools.partial(data_kernel, sz, stage), out_shape=pair...  15.7 us
    all_to_all x1, blocking collectives, exchange(): return lax.all_to_all(array, ALL, 0, 0, tiled=True)  9.26 us
    pallas_call x2, Pallas kernels, apply(): pl.pallas_call(functools.partial(apply_kernel, sz, last), out_shape=[pair...  5.35 us
    all_to_all x3, waiting for transfers between devices, exchange(): return lax.all_to_all(array, ALL, 0, 0, tiled=True)  4.89 us
    ppermute x3, starting transfers between devices, local(): lax.ppermute(shares[k], 'gx', [(i, i ^ k) for i in range(tx)])  4.39 us
    pallas_call x1, Pallas kernels, local(): pl.pallas_call(functools.partial(setup_kernel, sz), out_shape=[shape(sz.d...  3.23 us
    unnamed x26, local copies, waits for them, and re-layouts  2.49 us
  transfers between devices with their start and end apart: 11, of which 4 were waited for; matrix products, arithmetic and copies ran while one was open for 0% of the time, Pallas kernels for 28%

profile of v4, /device:TPU:0, one launch (start us, length us, event | category | flops | bytes accessed | tf_op | source)
XLA Modules:
  0.0 68.4 jit_solution(3387187705921578877)
XLA Ops:
  0.6 0.0 copy-start.1
  0.7 0.5 collective-permute-start
  1.9 3.2 %shard_map.113 = (f32[16,20,1,128]{3,2,1,0:T(1,128)}, f32[168,128]{1,0:T(8,128)}, f32[168,128]{1,0:T(8,128)}, f32[168,128]{1,0:T(8,128)}, f32[168,128]{1,0:T(8,128)}) custom-call(f32[1,128,512]{2,1,0:T(8,128)} %x0_ref.5, f32[1,128,512]{2,1,0:T(8,128)} %s_ref.3, f32[1,128,512]{2,1,0:T(8,128)} %k_ref.3, f32[1,136,272]{2,1,0:T(8,128)} %rows_ref.1, ...), custom_call_target="tpu_custom_call" | custom-call | bytes 4500000 | tf_op jit(solution)/shard_map/pallas_call | solution.py:576
  5.1 7.1 %all-to-all-start = ((f32[16,20,1,128]{3,2,1,0:T(1,128)}), f32[16,20,1,128]{3,2,1,0:T(1,128)S(1)}, u32[]{:S(2)}, u32[]{:S(2)}) async-start(f32[16,20,1,128]{3,2,1,0:T(1,128)} %get-tuple-element.21), calls=%async_computation | async-start | bytes 327680 | tf_op jit(solution)/shard_map/all_to_all | solution.py:573
  12.9 0.9 %copy-done = f32[1,128,512]{2,1,0:T(8,128)S(1)} copy-done((f32[1,128,512]{2,1,0:T(8,128)S(1)}, f32[1,128,512]{2,1,0:T(8,128)}, u32[]{:S(2)}) %copy-start) | copy-done | bytes 262168
  13.9 0.7 copy-done.7
  14.5 5.3 %shard_map.114.terms_ref = f32[2,128,512]{2,1,0:T(8,128)S(1)} custom-call(f32[1,128,512]{2,1,0:T(8,128)S(1)} %copy-done, f32[1,128,512]{2,1,0:T(8,128)S(1)} %collective-permute-done.refs_1_, s32[1,1,1,2,16]{4,3,2,1,0:T(2,128)S(1)} %bitcast.1, f32[1,1,1,16,2,256,256]{6,5,4,3,2,1,0:T(8,128)} %refs_5_.3), custom_call_target="tpu_custom_call" | custom-call | bytes 12000000 | tf_op jit(solution)/shard_map/pallas_call | solution.py:599
  19.9 0.8 %all-to-all-done.recv_ref = f32[16,20,1,128]{3,2,1,0:T(1,128)S(1)} async-done(((f32[16,20,1,128]{3,2,1,0:T(1,128)}), f32[16,20,1,128]{3,2,1,0:T(1,128)S(1)}, u32[]{:S(2)}, u32[]{:S(2)}) %all-to-all-start) | async-done | bytes 163872 | tf_op jit(solution)/shard_map/all_to_all | solution.py:573
  20.7 1.6 %shard_map.115 = (f32[2,128,512]{2,1,0:T(8,128)S(1)}, f32[16,16,128]{2,1,0:T(8,128)}, f32[136,640]{1,0:T(8,128)S(1)}, f32[136,640]{1,0:T(8,128)S(1)}) custom-call(f32[16,20,1,128]{3,2,1,0:T(1,128)S(1)} %all-to-all-done.recv_ref, f32[1,128,512]{2,1,0:T(8,128)S(1)} %copy-done.1, f32[1,128,512]{2,1,0:T(8,128)S(1)} %copy-done.3, f32[1,128,512]{2,1,0:T(8,128)S(1)} %copy-done.2, ...), custom_call_target="tpu_custom_call" | custom-call | bytes 9000000 | tf_op jit(solution)/shard_map/pallas_call | solution.py:610
  22.4 1.3 %collective-permute-start.1 = (f32[168,128]{1,0:T(8,128)S(1)}, f32[168,128]{1,0:T(8,128)S(1)}, u32[]{:S(2)}, u32[]{:S(2)}) collective-permute-start(f32[168,128]{1,0:T(8,128)S(1)} %copy-done.12), channel_id=1, source_target_pairs={{0,4},{4,0},{8,12},{12,8},{1,5},{5,1},{9,13},{13,9},{2,6},{6,2},{1... | collective-permute-start | bytes 258056 | tf_op jit(solution)/shard_map/ppermute | solution.py:587
  23.7 2.4 %collective-permute-start.2 = (f32[168,128]{1,0:T(8,128)S(1)}, f32[168,128]{1,0:T(8,128)S(1)}, u32[]{:S(2)}, u32[]{:S(2)}) collective-permute-start(f32[168,128]{1,0:T(8,128)S(1)} %copy-done.11), channel_id=1, source_target_pairs={{0,8},{4,12},{8,0},{12,4},{1,9},{5,13},{9,1},{13,5},{2,10},{6,14},... | collective-permute-start | bytes 258056 | tf_op jit(solution)/shard_map/ppermute | solution.py:587
  26.0 0.7 %collective-permute-start.3 = (f32[168,128]{1,0:T(8,128)S(1)}, f32[168,128]{1,0:T(8,128)S(1)}, u32[]{:S(2)}, u32[]{:S(2)}) collective-permute-start(f32[168,128]{1,0:T(8,128)S(1)} %copy-done.10), channel_id=1, source_target_pairs={{0,12},{4,8},{8,4},{12,0},{1,13},{5,9},{9,5},{13,1},{2,14},{6,10},... | collective-permute-start | bytes 258056 | tf_op jit(solution)/shard_map/ppermute | solution.py:587
  26.8 5.4 %all-to-all-start.1 = ((f32[16,16,128]{2,1,0:T(8,128)}), f32[16,16,128]{2,1,0:T(8,128)S(1)}, u32[]{:S(2)}, u32[]{:S(2)}) async-start(f32[16,16,128]{2,1,0:T(8,128)} %get-tuple-element.23), calls=%async_computation.1 | async-start | bytes 262144 | tf_op jit(solution)/shard_map/all_to_all | solution.py:573
  32.2 1.4 %collective-permute-done.2 = f32[168,128]{1,0:T(8,128)S(1)} collective-permute-done((f32[168,128]{1,0:T(8,128)S(1)}, f32[168,128]{1,0:T(8,128)S(1)}, u32[]{:S(2)}, u32[]{:S(2)}) %collective-permute-start.2) | collective-permute-done | bytes 86048 | tf_op jit(solution)/shard_map/ppermute | solution.py:587
  33.6 5.6 %shard_map.116.spread_ref.flat_ref = f32[16,8,256]{2,1,0:T(8,128)S(1)} custom-call(f32[2,128,512]{2,1,0:T(8,128)S(1)} %get-tuple-element.28.refs_0_.to_ref, f32[2,128,512]{2,1,0:T(8,128)S(1)} %collective-permute-done.4.refs_1_.tm_ref, f32[136,640]{1,0:T(8,128)S(1)} %get-tuple-element.29.refs_2_.se_ref, f32[1,128,512]{2,1,0:T(8,128)S(1)} %collective-permute-done.5.refs_3_, ...), custom_call_target="tpu_custom_call" | custom-call | bytes 12000000 | tf_op jit(solution)/shard_map/pallas_call | solution.py:599
  39.2 0.9 %all-to-all-done.1.recv_ref = f32[16,16,128]{2,1,0:T(8,128)S(1)} async-done(((f32[16,16,128]{2,1,0:T(8,128)}), f32[16,16,128]{2,1,0:T(8,128)S(1)}, u32[]{:S(2)}, u32[]{:S(2)}) %all-to-all-start.1) | async-done | bytes 131104 | tf_op jit(solution)/shard_map/all_to_all | solution.py:573
  40.1 2.9 %shard_map.117 = (f32[2,128,512]{2,1,0:T(8,128)S(1)}, f32[16,16,128]{2,1,0:T(8,128)}, f32[2,128,512]{2,1,0:T(8,128)S(1)}, f32[8,128]{1,0:T(8,128)S(1)}) custom-call(f32[16,16,128]{2,1,0:T(8,128)S(1)} %all-to-all-done.1.recv_ref, f32[168,128]{1,0:T(8,128)S(1)} %add_add_fusion.lg_ref, f32[2,128,512]{2,1,0:T(8,128)S(1)} %get-tuple-element.28.refs_0_.to_ref, ...), custom_call_target="tpu_custom_call" | custom-call | bytes 9000000 | tf_op jit(solution)/shard_map/pallas_call | solution.py:621
  43.0 0.8 %copy-done.4 = f32[2,128,512]{2,1,0:T(8,128)} copy-done((f32[2,128,512]{2,1,0:T(8,128)}, f32[2,128,512]{2,1,0:T(8,128)S(1)}, u32[]{:S(2)}) %copy-start.4) | copy-done | bytes 524312
  43.8 3.9 %all-to-all-start.2 = ((f32[16,16,128]{2,1,0:T(8,128)}), f32[16,16,128]{2,1,0:T(8,128)S(1)}, u32[]{:S(2)}, u32[]{:S(2)}) async-start(f32[16,16,128]{2,1,0:T(8,128)} %get-tuple-element.31), calls=%async_computation.2 | async-start | bytes 262144 | tf_op jit(solution)/shard_map/all_to_all | solution.py:573
  47.8 4.8 %shard_map.118.spread_ref = f32[16,4,256]{2,1,0:T(4,128)S(1)} custom-call(f32[2,128,512]{2,1,0:T(8,128)S(1)} %get-tuple-element.32.refs_0_.to_ref, f32[2,128,512]{2,1,0:T(8,128)S(1)} %collective-permute-done.6.refs_1_.tm_ref, f32[136,640]{1,0:T(8,128)S(1)} %get-tuple-element.29.refs_2_.se_ref, f32[1,128,512]{2,1,0:T(8,128)S(1)} %collective-permute-done.5.refs_3_, ...), custom_call_target="tpu_custom_call" | custom-call | bytes 12000000 | tf_op jit(solution)/shard_map/pallas_call | solution.py:599
  52.6 3.1 %all-to-all-done.2.recv_ref = f32[16,16,128]{2,1,0:T(8,128)S(1)} async-done(((f32[16,16,128]{2,1,0:T(8,128)}), f32[16,16,128]{2,1,0:T(8,128)S(1)}, u32[]{:S(2)}, u32[]{:S(2)}) %all-to-all-start.2) | async-done | bytes 131104 | tf_op jit(solution)/shard_map/all_to_all | solution.py:573
  55.7 2.4 %shard_map.119 = (f32[2,128,512]{2,1,0:T(8,128)S(1)}, f32[16,1,128]{2,1,0:T(1,128)S(1)}, f32[2,128,512]{2,1,0:T(8,128)S(1)}, f32[8,128]{1,0:T(8,128)}) custom-call(f32[16,16,128]{2,1,0:T(8,128)S(1)} %all-to-all-done.2.recv_ref, f32[168,128]{1,0:T(8,128)S(1)} %add_add_fusion.lg_ref, f32[2,128,512]{2,1,0:T(8,128)S(1)} %get-tuple-element.32.refs_0_.to_ref, ...), custom_call_target="tpu_custom_call" | custom-call | bytes 9000000 | tf_op jit(solution)/shard_map/pallas_call | solution.py:621
  58.2 9.3 %all_to_all.20.recv_ref = f32[16,1,128]{2,1,0:T(1,128)S(1)} all-to-all(f32[16,1,128]{2,1,0:T(1,128)S(1)} %get-tuple-element.34), channel_id=1, replica_groups=mesh['groups'=2,'gx'=4,'gy'=2,'vert'=2] {'gx','gy','vert'}, dimensions={0} | all-to-all | bytes 16384 | tf_op jit(solution)/shard_map/all_to_all | solution.py:573
  67.4 1.0 %shard_map.120 = (f32[1,128,512]{2,1,0:T(8,128)}, f32[1,128,512]{2,1,0:T(8,128)}) custom-call(f32[16,1,128]{2,1,0:T(1,128)S(1)} %all_to_all.20.recv_ref, f32[1,128,512]{2,1,0:T(8,128)S(1)} %copy-done.1, f32[2,128,512]{2,1,0:T(8,128)S(1)} %copy-done.5, f32[2,128,512]{2,1,0:T(8,128)S(1)} %get-tuple-element.36.wz_ref, ...), custom_call_target="tpu_custom_call" | custom-call | bytes 3000000 | tf_op jit(solution)/shard_map/pallas_call | solution.py:648
  (35 shorter events, 0.1 us)
Async XLA Ops:
  0.6 20.1 %copy-start.1 = (f32[1,128,512]{2,1,0:T(8,128)S(1)}, f32[1,128,512]{2,1,0:T(8,128)}, u32[]{:S(2)}) copy-start(f32[1,128,512]{2,1,0:T(8,128)} %x0_ref.5) | copy-start | bytes 786436
  0.6 20.1 %copy-start.3 = (f32[1,128,512]{2,1,0:T(8,128)S(1)}, f32[1,128,512]{2,1,0:T(8,128)}, u32[]{:S(2)}) copy-start(f32[1,128,512]{2,1,0:T(8,128)} %s_ref.3) | copy-start | bytes 786436
  0.7 20.1 %copy-start.2 = (f32[1,128,512]{2,1,0:T(8,128)S(1)}, f32[1,128,512]{2,1,0:T(8,128)}, u32[]{:S(2)}) copy-start(f32[1,128,512]{2,1,0:T(8,128)} %k_ref.3) | copy-start | bytes 786436
  0.7 33.0 %copy-start.8 = (s32[1,1,1,16,2]{3,4,2,1,0:T(2,128)S(1)}, s32[1,1,1,16,2]{3,4,2,1,0:T(2,128)}, u32[]{:S(2)}) copy-start(s32[1,1,1,16,2]{3,4,2,1,0:T(2,128)} %param.16) | copy-start | bytes 388
  0.7 20.1 %copy-start.6 = (f32[1,128,512]{2,1,0:T(8,128)S(1)}, f32[1,128,512]{2,1,0:T(8,128)}, u32[]{:S(2)}) copy-start(f32[1,128,512]{2,1,0:T(8,128)} %b_ref.1) | copy-start | bytes 786436
  0.7 4.4 %collective-permute-start = (f32[1,128,512]{2,1,0:T(8,128)}, f32[1,128,512]{2,1,0:T(8,128)S(1)}, u32[]{:S(2)}, u32[]{:S(2)}) collective-permute-start(f32[1,128,512]{2,1,0:T(8,128)} %x0_ref.5), channel_id=1, source_target_pairs={{0,1},{1,0},{2,3},{3,2},{4,5},{5,4},{6,7},{7,6},{8,9},{9,8},{10,11... | collective-permute-start | bytes 786440 | tf_op jit(solution)/shard_map/ppermute | solution.py:569
  5.1 18.6 %copy-start.11 = (f32[168,128]{1,0:T(8,128)S(1)}, f32[168,128]{1,0:T(8,128)}, u32[]{:S(2)}) copy-start(f32[168,128]{1,0:T(8,128)} %get-tuple-element.26) | copy-start | bytes 258052
  5.1 20.9 %copy-start.10 = (f32[168,128]{1,0:T(8,128)S(1)}, f32[168,128]{1,0:T(8,128)}, u32[]{:S(2)}) copy-start(f32[168,128]{1,0:T(8,128)} %get-tuple-element.27) | copy-start | bytes 258052
  5.1 28.5 %copy-start.9 = (f32[168,128]{1,0:T(8,128)S(1)}, f32[168,128]{1,0:T(8,128)}, u32[]{:S(2)}) copy-start(f32[168,128]{1,0:T(8,128)} %get-tuple-element.24) | copy-start | bytes 258052
  5.1 15.6 %all-to-all-start = ((f32[16,20,1,128]{3,2,1,0:T(1,128)}), f32[16,20,1,128]{3,2,1,0:T(1,128)S(1)}, u32[]{:S(2)}, u32[]{:S(2)}) async-start(f32[16,20,1,128]{3,2,1,0:T(1,128)} %get-tuple-element.21), calls=%async_computation | async-start | bytes 327680 | tf_op jit(solution)/shard_map/all_to_all | solution.py:573
  12.9 1.0 %copy-start = (f32[1,128,512]{2,1,0:T(8,128)S(1)}, f32[1,128,512]{2,1,0:T(8,128)}, u32[]{:S(2)}) copy-start(f32[1,128,512]{2,1,0:T(8,128)} %x0_ref.5) | copy-start | bytes 786436
  13.9 0.7 copy-start.7
  14.5 7.8 %copy-start.12 = (f32[168,128]{1,0:T(8,128)S(1)}, f32[168,128]{1,0:T(8,128)}, u32[]{:S(2)}) copy-start(f32[168,128]{1,0:T(8,128)} %get-tuple-element.25) | copy-start | bytes 258052
  22.4 11.2 %collective-permute-start.4 = (f32[2,128,512]{2,1,0:T(8,128)S(1)}, f32[2,128,512]{2,1,0:T(8,128)S(1)}, u32[]{:S(2)}, u32[]{:S(2)}) collective-permute-start(f32[2,128,512]{2,1,0:T(8,128)S(1)} %get-tuple-element.28.refs_0_.to_ref), channel_id=1, source_target_pairs={{0,1},{1,0},{2,3},{3,2},{4,5},{5,4},{6,7},{7,6},{8,9},{9,8},{10,11... | collective-permute-start | bytes 1572872 | tf_op jit(solution)/shard_map/ppermute | solution.py:635
  22.4 9.8 %collective-permute-start.1 = (f32[168,128]{1,0:T(8,128)S(1)}, f32[168,128]{1,0:T(8,128)S(1)}, u32[]{:S(2)}, u32[]{:S(2)}) collective-permute-start(f32[168,128]{1,0:T(8,128)S(1)} %copy-done.12), channel_id=1, source_target_pairs={{0,4},{4,0},{8,12},{12,8},{1,5},{5,1},{9,13},{13,9},{2,6},{6,2},{1... | collective-permute-start | bytes 258056 | tf_op jit(solution)/shard_map/ppermute | solution.py:587
  23.7 9.9 %collective-permute-start.2 = (f32[168,128]{1,0:T(8,128)S(1)}, f32[168,128]{1,0:T(8,128)S(1)}, u32[]{:S(2)}, u32[]{:S(2)}) collective-permute-start(f32[168,128]{1,0:T(8,128)S(1)} %copy-done.11), channel_id=1, source_target_pairs={{0,8},{4,12},{8,0},{12,4},{1,9},{5,13},{9,1},{13,5},{2,10},{6,14},... | collective-permute-start | bytes 258056 | tf_op jit(solution)/shard_map/ppermute | solution.py:587
  26.0 7.5 %collective-permute-start.3 = (f32[168,128]{1,0:T(8,128)S(1)}, f32[168,128]{1,0:T(8,128)S(1)}, u32[]{:S(2)}, u32[]{:S(2)}) collective-permute-start(f32[168,128]{1,0:T(8,128)S(1)} %copy-done.10), channel_id=1, source_target_pairs={{0,12},{4,8},{8,4},{12,0},{1,13},{5,9},{9,5},{13,1},{2,14},{6,10},... | collective-permute-start | bytes 258056 | tf_op jit(solution)/shard_map/ppermute | solution.py:587
  26.8 6.8 %collective-permute-start.5 = (f32[1,128,512]{2,1,0:T(8,128)S(1)}, f32[1,128,512]{2,1,0:T(8,128)S(1)}, u32[]{:S(2)}, u32[]{:S(2)}) collective-permute-start(f32[1,128,512]{2,1,0:T(8,128)S(1)} %copy-done.3), channel_id=1, source_target_pairs={{0,1},{1,0},{2,3},{3,2},{4,5},{5,4},{6,7},{7,6},{8,9},{9,8},{10,11... | collective-permute-start | bytes 786440 | tf_op jit(solution)/shard_map/ppermute | solution.py:570
  26.8 13.3 %all-to-all-start.1 = ((f32[16,16,128]{2,1,0:T(8,128)}), f32[16,16,128]{2,1,0:T(8,128)S(1)}, u32[]{:S(2)}, u32[]{:S(2)}) async-start(f32[16,16,128]{2,1,0:T(8,128)} %get-tuple-element.23), calls=%async_computation.1 | async-start | bytes 262144 | tf_op jit(solution)/shard_map/all_to_all | solution.py:573
  43.0 0.8 %copy-start.4 = (f32[2,128,512]{2,1,0:T(8,128)}, f32[2,128,512]{2,1,0:T(8,128)S(1)}, u32[]{:S(2)}) copy-start(f32[2,128,512]{2,1,0:T(8,128)S(1)} %get-tuple-element.35.rp_ref) | copy-start | bytes 1572868
  43.8 23.6 %copy-start.5 = (f32[2,128,512]{2,1,0:T(8,128)S(1)}, f32[2,128,512]{2,1,0:T(8,128)}, u32[]{:S(2)}) copy-start(f32[2,128,512]{2,1,0:T(8,128)} %copy-done.4) | copy-start | bytes 1572868
  43.8 4.0 %collective-permute-start.6 = (f32[2,128,512]{2,1,0:T(8,128)S(1)}, f32[2,128,512]{2,1,0:T(8,128)S(1)}, u32[]{:S(2)}, u32[]{:S(2)}) collective-permute-start(f32[2,128,512]{2,1,0:T(8,128)S(1)} %get-tuple-element.32.refs_0_.to_ref), channel_id=1, source_target_pairs={{0,1},{1,0},{2,3},{3,2},{4,5},{5,4},{6,7},{7,6},{8,9},{9,8},{10,11... | collective-permute-start | bytes 1572872 | tf_op jit(solution)/shard_map/ppermute | solution.py:641
  43.8 11.9 %all-to-all-start.2 = ((f32[16,16,128]{2,1,0:T(8,128)}), f32[16,16,128]{2,1,0:T(8,128)S(1)}, u32[]{:S(2)}, u32[]{:S(2)}) async-start(f32[16,16,128]{2,1,0:T(8,128)} %get-tuple-element.31), calls=%async_computation.2 | async-start | bytes 262144 | tf_op jit(solution)/shard_map/all_to_all | solution.py:573
  58.2 9.3 %collective-permute-start.7 = (f32[2,128,512]{2,1,0:T(8,128)S(1)}, f32[2,128,512]{2,1,0:T(8,128)S(1)}, u32[]{:S(2)}, u32[]{:S(2)}) collective-permute-start(f32[2,128,512]{2,1,0:T(8,128)S(1)} %get-tuple-element.37.to_ref), channel_id=1, source_target_pairs={{0,1},{1,0},{2,3},{3,2},{4,5},{5,4},{6,7},{7,6},{8,9},{9,8},{10,11... | collective-permute-start | bytes 1572872 | tf_op jit(solution)/shard_map/ppermute | solution.py:647

commit v5 on v4

--- a/solution.py
+++ b/solution.py
@@ -104,17 +104,21 @@
 
 
 def setup_kernel(sz, x0_ref, s_ref, k_ref, rows_ref, slots_ref, count_ref, pay_ref, *refs):
-    outs, (tiles_ref, held_ref, sems) = refs[: sz.tx], refs[sz.tx :]
+    outs, (tiles_ref, held_ref, live_ref, sems) = refs[: sz.tx], refs[sz.tx :]
     copies = [
         pltpu.make_async_copy(ref.at[0], tiles_ref.at[at], sems.at[at])
         for at, ref in enumerate((x0_ref, s_ref, k_ref))
     ]
-    copies = [pltpu.make_async_copy(rows_ref.at[0], held_ref, sems.at[3])] + copies
+    copies = [
+        pltpu.make_async_copy(rows_ref.at[0], held_ref, sems.at[3]),
+        pltpu.make_async_copy(slots_ref, live_ref, sems.at[4]),
+    ] + copies
     for copy in copies:
         copy.start()
     copies[0].wait()
-    share_rows(sz, slots_ref, count_ref, held_ref, outs)
-    for copy in copies[1:]:
+    copies[1].wait()
+    share_rows(sz, live_ref, count_ref, held_ref, outs)
+    for copy in copies[2:]:
         copy.wait()
     xi, yi, vi = lax.axis_index("gx"), lax.axis_index("gy"), lax.axis_index("vert")
     r, c, g = sz.rows, sz.cols, sz.groups
@@ -577,10 +581,10 @@
         functools.partial(setup_kernel, sz),
         out_shape=[shape(sz.devices, 5 * sz.groups, 1, LANES)]
         + [shape(sz.vec_rows * sz.lift_rows, LANES)] * tx,
-        in_specs=[ANY] * 4 + [VMEM, SMEM],
+        in_specs=[ANY] * 5 + [SMEM],
         out_specs=[VMEM] * (1 + tx),
         scratch_shapes=[pltpu.VMEM((3, sz.rows, sz.cols), F32), pltpu.VMEM((cap, sz.nco), F32),
-                        pltpu.SemaphoreType.DMA((4,))],
+                        pltpu.VMEM((1, cap), jnp.int32), pltpu.SemaphoreType.DMA((5,))],
         compiler_params=EDGE_PARAMS,
         cost_estimate=cost(1.5),
     )(initial_guess, precond_scale, kappa_sq, coarse_rows, coarse_slots, slot_count)

time: 69 us -> 68.3 us (0.990)
  transfers between devices with their start and end apart: 11 -> 11, of which waited for: 4 -> 4; matrix products, arithmetic and copies ran while one was open for 0% -> 0% of each run, Pallas kernels for 28% -> 27%
where the time goes in v5:
time: 68.3 us; the launch traced here: 67.8 us
  Pallas kernels  26.2 us (38%)
  starting transfers between devices  21.4 us (31%)
  blocking collectives  9.26 us (14%)
  waiting for transfers between devices  6.28 us (9%)
  local copies, waits for them, and re-layouts  2.5 us (4%)
  between operations  2.13 us (3%)
    all_to_all x3, starting transfers between devices, exchange(): return lax.all_to_all(array, ALL, 0, 0, tiled=True)  16.5 us
    pallas_call x3, Pallas kernels, data(): pl.pallas_call(functools.partial(data_kernel, sz, stage), out_shape=pair...  15.7 us
    all_to_all x1, blocking collectives, exchange(): return lax.all_to_all(array, ALL, 0, 0, tiled=True)  9.26 us
    pallas_call x2, Pallas kernels, apply(): pl.pallas_call(functools.partial(apply_kernel, sz, last), out_shape=[pair...  5.34 us
    all_to_all x3, waiting for transfers between devices, exchange(): return lax.all_to_all(array, ALL, 0, 0, tiled=True)  4.89 us
    ppermute x3, starting transfers between devices, local(): lax.ppermute(shares[k], 'gx', [(i, i ^ k) for i in range(tx)])  4.39 us
    pallas_call x1, Pallas kernels, local(): pl.pallas_call(functools.partial(setup_kernel, sz), out_shape=[shape(sz.d...  2.56 us
    unnamed x26, local copies, waits for them, and re-layouts  2.49 us
  transfers between devices with their start and end apart: 11, of which 4 were waited for; matrix products, arithmetic and copies ran while one was open for 0% of the time, Pallas kernels for 27%

profile of v5, /device:TPU:0, one launch (start us, length us, event | category | flops | bytes accessed | tf_op | source)
XLA Modules:
  0.0 67.8 jit_solution(14337800780840236958)
XLA Ops:
  0.6 0.0 copy-start.1
  0.7 0.5 collective-permute-start
  1.9 2.6 %shard_map.113 = (f32[16,20,1,128]{3,2,1,0:T(1,128)}, f32[168,128]{1,0:T(8,128)}, f32[168,128]{1,0:T(8,128)}, f32[168,128]{1,0:T(8,128)}, f32[168,128]{1,0:T(8,128)}) custom-call(f32[1,128,512]{2,1,0:T(8,128)} %x0_ref.5, f32[1,128,512]{2,1,0:T(8,128)} %s_ref.3, f32[1,128,512]{2,1,0:T(8,128)} %k_ref.3, f32[1,136,272]{2,1,0:T(8,128)} %rows_ref.1, ...), custom_call_target="tpu_custom_call" | custom-call | bytes 4500000 | tf_op jit(solution)/shard_map/pallas_call | solution.py:580
  4.5 7.1 %all-to-all-start = ((f32[16,20,1,128]{3,2,1,0:T(1,128)}), f32[16,20,1,128]{3,2,1,0:T(1,128)S(1)}, u32[]{:S(2)}, u32[]{:S(2)}) async-start(f32[16,20,1,128]{3,2,1,0:T(1,128)} %get-tuple-element.21), calls=%async_computation | async-start | bytes 327680 | tf_op jit(solution)/shard_map/all_to_all | solution.py:577
  12.3 0.9 %copy-done = f32[1,128,512]{2,1,0:T(8,128)S(1)} copy-done((f32[1,128,512]{2,1,0:T(8,128)S(1)}, f32[1,128,512]{2,1,0:T(8,128)}, u32[]{:S(2)}) %copy-start) | copy-done | bytes 262168
  13.2 0.7 copy-done.7
  13.9 5.3 %shard_map.114.terms_ref = f32[2,128,512]{2,1,0:T(8,128)S(1)} custom-call(f32[1,128,512]{2,1,0:T(8,128)S(1)} %copy-done, f32[1,128,512]{2,1,0:T(8,128)S(1)} %collective-permute-done.refs_1_, s32[1,1,1,2,16]{4,3,2,1,0:T(2,128)S(1)} %bitcast.1, f32[1,1,1,16,2,256,256]{6,5,4,3,2,1,0:T(8,128)} %refs_5_.3), custom_call_target="tpu_custom_call" | custom-call | bytes 12000000 | tf_op jit(solution)/shard_map/pallas_call | solution.py:603
  19.2 0.8 %all-to-all-done.recv_ref = f32[16,20,1,128]{3,2,1,0:T(1,128)S(1)} async-done(((f32[16,20,1,128]{3,2,1,0:T(1,128)}), f32[16,20,1,128]{3,2,1,0:T(1,128)S(1)}, u32[]{:S(2)}, u32[]{:S(2)}) %all-to-all-start) | async-done | bytes 163872 | tf_op jit(solution)/shard_map/all_to_all | solution.py:577
  20.1 1.6 %shard_map.115 = (f32[2,128,512]{2,1,0:T(8,128)S(1)}, f32[16,16,128]{2,1,0:T(8,128)}, f32[136,640]{1,0:T(8,128)S(1)}, f32[136,640]{1,0:T(8,128)S(1)}) custom-call(f32[16,20,1,128]{3,2,1,0:T(1,128)S(1)} %all-to-all-done.recv_ref, f32[1,128,512]{2,1,0:T(8,128)S(1)} %copy-done.1, f32[1,128,512]{2,1,0:T(8,128)S(1)} %copy-done.3, f32[1,128,512]{2,1,0:T(8,128)S(1)} %copy-done.2, ...), custom_call_target="tpu_custom_call" | custom-call | bytes 9000000 | tf_op jit(solution)/shard_map/pallas_call | solution.py:614
  21.7 1.3 %collective-permute-start.1 = (f32[168,128]{1,0:T(8,128)S(1)}, f32[168,128]{1,0:T(8,128)S(1)}, u32[]{:S(2)}, u32[]{:S(2)}) collective-permute-start(f32[168,128]{1,0:T(8,128)S(1)} %copy-done.12), channel_id=1, source_target_pairs={{0,4},{4,0},{8,12},{12,8},{1,5},{5,1},{9,13},{13,9},{2,6},{6,2},{1... | collective-permute-start | bytes 258056 | tf_op jit(solution)/shard_map/ppermute | solution.py:591
  23.0 2.4 %collective-permute-start.2 = (f32[168,128]{1,0:T(8,128)S(1)}, f32[168,128]{1,0:T(8,128)S(1)}, u32[]{:S(2)}, u32[]{:S(2)}) collective-permute-start(f32[168,128]{1,0:T(8,128)S(1)} %copy-done.11), channel_id=1, source_target_pairs={{0,8},{4,12},{8,0},{12,4},{1,9},{5,13},{9,1},{13,5},{2,10},{6,14},... | collective-permute-start | bytes 258056 | tf_op jit(solution)/shard_map/ppermute | solution.py:591
  25.4 0.7 %collective-permute-start.3 = (f32[168,128]{1,0:T(8,128)S(1)}, f32[168,128]{1,0:T(8,128)S(1)}, u32[]{:S(2)}, u32[]{:S(2)}) collective-permute-start(f32[168,128]{1,0:T(8,128)S(1)} %copy-done.10), channel_id=1, source_target_pairs={{0,12},{4,8},{8,4},{12,0},{1,13},{5,9},{9,5},{13,1},{2,14},{6,10},... | collective-permute-start | bytes 258056 | tf_op jit(solution)/shard_map/ppermute | solution.py:591
  26.1 5.4 %all-to-all-start.1 = ((f32[16,16,128]{2,1,0:T(8,128)}), f32[16,16,128]{2,1,0:T(8,128)S(1)}, u32[]{:S(2)}, u32[]{:S(2)}) async-start(f32[16,16,128]{2,1,0:T(8,128)} %get-tuple-element.23), calls=%async_computation.1 | async-start | bytes 262144 | tf_op jit(solution)/shard_map/all_to_all | solution.py:577
  31.5 1.4 %collective-permute-done.2 = f32[168,128]{1,0:T(8,128)S(1)} collective-permute-done((f32[168,128]{1,0:T(8,128)S(1)}, f32[168,128]{1,0:T(8,128)S(1)}, u32[]{:S(2)}, u32[]{:S(2)}) %collective-permute-start.2) | collective-permute-done | bytes 86048 | tf_op jit(solution)/shard_map/ppermute | solution.py:591
  33.0 5.6 %shard_map.116.spread_ref.flat_ref = f32[16,8,256]{2,1,0:T(8,128)S(1)} custom-call(f32[2,128,512]{2,1,0:T(8,128)S(1)} %get-tuple-element.28.refs_0_.to_ref, f32[2,128,512]{2,1,0:T(8,128)S(1)} %collective-permute-done.4.refs_1_.tm_ref, f32[136,640]{1,0:T(8,128)S(1)} %get-tuple-element.29.refs_2_.se_ref, f32[1,128,512]{2,1,0:T(8,128)S(1)} %collective-permute-done.5.refs_3_, ...), custom_call_target="tpu_custom_call" | custom-call | bytes 12000000 | tf_op jit(solution)/shard_map/pallas_call | solution.py:603
  38.5 0.9 %all-to-all-done.1.recv_ref = f32[16,16,128]{2,1,0:T(8,128)S(1)} async-done(((f32[16,16,128]{2,1,0:T(8,128)}), f32[16,16,128]{2,1,0:T(8,128)S(1)}, u32[]{:S(2)}, u32[]{:S(2)}) %all-to-all-start.1) | async-done | bytes 131104 | tf_op jit(solution)/shard_map/all_to_all | solution.py:577
  39.4 2.9 %shard_map.117 = (f32[2,128,512]{2,1,0:T(8,128)S(1)}, f32[16,16,128]{2,1,0:T(8,128)}, f32[2,128,512]{2,1,0:T(8,128)S(1)}, f32[8,128]{1,0:T(8,128)S(1)}) custom-call(f32[16,16,128]{2,1,0:T(8,128)S(1)} %all-to-all-done.1.recv_ref, f32[168,128]{1,0:T(8,128)S(1)} %add_add_fusion.lg_ref, f32[2,128,512]{2,1,0:T(8,128)S(1)} %get-tuple-element.28.refs_0_.to_ref, ...), custom_call_target="tpu_custom_call" | custom-call | bytes 9000000 | tf_op jit(solution)/shard_map/pallas_call | solution.py:625
  42.4 0.8 %copy-done.4 = f32[2,128,512]{2,1,0:T(8,128)} copy-done((f32[2,128,512]{2,1,0:T(8,128)}, f32[2,128,512]{2,1,0:T(8,128)S(1)}, u32[]{:S(2)}) %copy-start.4) | copy-done | bytes 524312
  43.2 3.9 %all-to-all-start.2 = ((f32[16,16,128]{2,1,0:T(8,128)}), f32[16,16,128]{2,1,0:T(8,128)S(1)}, u32[]{:S(2)}, u32[]{:S(2)}) async-start(f32[16,16,128]{2,1,0:T(8,128)} %get-tuple-element.31), calls=%async_computation.2 | async-start | bytes 262144 | tf_op jit(solution)/shard_map/all_to_all | solution.py:577
  47.1 4.8 %shard_map.118.spread_ref = f32[16,4,256]{2,1,0:T(4,128)S(1)} custom-call(f32[2,128,512]{2,1,0:T(8,128)S(1)} %get-tuple-element.32.refs_0_.to_ref, f32[2,128,512]{2,1,0:T(8,128)S(1)} %collective-permute-done.6.refs_1_.tm_ref, f32[136,640]{1,0:T(8,128)S(1)} %get-tuple-element.29.refs_2_.se_ref, f32[1,128,512]{2,1,0:T(8,128)S(1)} %collective-permute-done.5.refs_3_, ...), custom_call_target="tpu_custom_call" | custom-call | bytes 12000000 | tf_op jit(solution)/shard_map/pallas_call | solution.py:603
  51.9 3.1 %all-to-all-done.2.recv_ref = f32[16,16,128]{2,1,0:T(8,128)S(1)} async-done(((f32[16,16,128]{2,1,0:T(8,128)}), f32[16,16,128]{2,1,0:T(8,128)S(1)}, u32[]{:S(2)}, u32[]{:S(2)}) %all-to-all-start.2) | async-done | bytes 131104 | tf_op jit(solution)/shard_map/all_to_all | solution.py:577
  55.1 2.4 %shard_map.119 = (f32[2,128,512]{2,1,0:T(8,128)S(1)}, f32[16,1,128]{2,1,0:T(1,128)S(1)}, f32[2,128,512]{2,1,0:T(8,128)S(1)}, f32[8,128]{1,0:T(8,128)}) custom-call(f32[16,16,128]{2,1,0:T(8,128)S(1)} %all-to-all-done.2.recv_ref, f32[168,128]{1,0:T(8,128)S(1)} %add_add_fusion.lg_ref, f32[2,128,512]{2,1,0:T(8,128)S(1)} %get-tuple-element.32.refs_0_.to_ref, ...), custom_call_target="tpu_custom_call" | custom-call | bytes 9000000 | tf_op jit(solution)/shard_map/pallas_call | solution.py:625
  57.5 9.3 %all_to_all.20.recv_ref = f32[16,1,128]{2,1,0:T(1,128)S(1)} all-to-all(f32[16,1,128]{2,1,0:T(1,128)S(1)} %get-tuple-element.34), channel_id=1, replica_groups=mesh['groups'=2,'gx'=4,'gy'=2,'vert'=2] {'gx','gy','vert'}, dimensions={0} | all-to-all | bytes 16384 | tf_op jit(solution)/shard_map/all_to_all | solution.py:577
  66.8 1.0 %shard_map.120 = (f32[1,128,512]{2,1,0:T(8,128)}, f32[1,128,512]{2,1,0:T(8,128)}) custom-call(f32[16,1,128]{2,1,0:T(1,128)S(1)} %all_to_all.20.recv_ref, f32[1,128,512]{2,1,0:T(8,128)S(1)} %copy-done.1, f32[2,128,512]{2,1,0:T(8,128)S(1)} %copy-done.5, f32[2,128,512]{2,1,0:T(8,128)S(1)} %get-tuple-element.36.wz_ref, ...), custom_call_target="tpu_custom_call" | custom-call | bytes 3000000 | tf_op jit(solution)/shard_map/pallas_call | solution.py:652
  (35 shorter events, 0.1 us)
Async XLA Ops:
  0.6 19.4 %copy-start.1 = (f32[1,128,512]{2,1,0:T(8,128)S(1)}, f32[1,128,512]{2,1,0:T(8,128)}, u32[]{:S(2)}) copy-start(f32[1,128,512]{2,1,0:T(8,128)} %x0_ref.5) | copy-start | bytes 786436
  0.6 19.4 %copy-start.3 = (f32[1,128,512]{2,1,0:T(8,128)S(1)}, f32[1,128,512]{2,1,0:T(8,128)}, u32[]{:S(2)}) copy-start(f32[1,128,512]{2,1,0:T(8,128)} %s_ref.3) | copy-start | bytes 786436
  0.7 19.4 %copy-start.2 = (f32[1,128,512]{2,1,0:T(8,128)S(1)}, f32[1,128,512]{2,1,0:T(8,128)}, u32[]{:S(2)}) copy-start(f32[1,128,512]{2,1,0:T(8,128)} %k_ref.3) | copy-start | bytes 786436
  0.7 32.3 %copy-start.8 = (s32[1,1,1,16,2]{3,4,2,1,0:T(2,128)S(1)}, s32[1,1,1,16,2]{3,4,2,1,0:T(2,128)}, u32[]{:S(2)}) copy-start(s32[1,1,1,16,2]{3,4,2,1,0:T(2,128)} %param.16) | copy-start | bytes 388
  0.7 19.4 %copy-start.6 = (f32[1,128,512]{2,1,0:T(8,128)S(1)}, f32[1,128,512]{2,1,0:T(8,128)}, u32[]{:S(2)}) copy-start(f32[1,128,512]{2,1,0:T(8,128)} %b_ref.1) | copy-start | bytes 786436
  0.7 3.8 %collective-permute-start = (f32[1,128,512]{2,1,0:T(8,128)}, f32[1,128,512]{2,1,0:T(8,128)S(1)}, u32[]{:S(2)}, u32[]{:S(2)}) collective-permute-start(f32[1,128,512]{2,1,0:T(8,128)} %x0_ref.5), channel_id=1, source_target_pairs={{0,1},{1,0},{2,3},{3,2},{4,5},{5,4},{6,7},{7,6},{8,9},{9,8},{10,11... | collective-permute-start | bytes 786440 | tf_op jit(solution)/shard_map/ppermute | solution.py:573
  4.4 18.6 %copy-start.11 = (f32[168,128]{1,0:T(8,128)S(1)}, f32[168,128]{1,0:T(8,128)}, u32[]{:S(2)}) copy-start(f32[168,128]{1,0:T(8,128)} %get-tuple-element.26) | copy-start | bytes 258052
  4.4 20.9 %copy-start.10 = (f32[168,128]{1,0:T(8,128)S(1)}, f32[168,128]{1,0:T(8,128)}, u32[]{:S(2)}) copy-start(f32[168,128]{1,0:T(8,128)} %get-tuple-element.27) | copy-start | bytes 258052
  4.4 28.5 %copy-start.9 = (f32[168,128]{1,0:T(8,128)S(1)}, f32[168,128]{1,0:T(8,128)}, u32[]{:S(2)}) copy-start(f32[168,128]{1,0:T(8,128)} %get-tuple-element.24) | copy-start | bytes 258052
  4.5 15.6 %all-to-all-start = ((f32[16,20,1,128]{3,2,1,0:T(1,128)}), f32[16,20,1,128]{3,2,1,0:T(1,128)S(1)}, u32[]{:S(2)}, u32[]{:S(2)}) async-start(f32[16,20,1,128]{3,2,1,0:T(1,128)} %get-tuple-element.21), calls=%async_computation | async-start | bytes 327680 | tf_op jit(solution)/shard_map/all_to_all | solution.py:577
  12.2 1.0 %copy-start = (f32[1,128,512]{2,1,0:T(8,128)S(1)}, f32[1,128,512]{2,1,0:T(8,128)}, u32[]{:S(2)}) copy-start(f32[1,128,512]{2,1,0:T(8,128)} %x0_ref.5) | copy-start | bytes 786436
  13.2 0.7 %copy-start.7 = (s32[1,1,1,16,2]{3,4,2,1,0:T(2,128)S(1)}, s32[1,1,1,16,2]{3,4,2,1,0:T(2,128)}, u32[]{:S(2)}) copy-start(s32[1,1,1,16,2]{3,4,2,1,0:T(2,128)} %param.16) | copy-start | bytes 388
  13.9 7.8 %copy-start.12 = (f32[168,128]{1,0:T(8,128)S(1)}, f32[168,128]{1,0:T(8,128)}, u32[]{:S(2)}) copy-start(f32[168,128]{1,0:T(8,128)} %get-tuple-element.25) | copy-start | bytes 258052
  21.7 11.2 %collective-permute-start.4 = (f32[2,128,512]{2,1,0:T(8,128)S(1)}, f32[2,128,512]{2,1,0:T(8,128)S(1)}, u32[]{:S(2)}, u32[]{:S(2)}) collective-permute-start(f32[2,128,512]{2,1,0:T(8,128)S(1)} %get-tuple-element.28.refs_0_.to_ref), channel_id=1, source_target_pairs={{0,1},{1,0},{2,3},{3,2},{4,5},{5,4},{6,7},{7,6},{8,9},{9,8},{10,11... | collective-permute-start | bytes 1572872 | tf_op jit(solution)/shard_map/ppermute | solution.py:639
  21.7 9.8 %collective-permute-start.1 = (f32[168,128]{1,0:T(8,128)S(1)}, f32[168,128]{1,0:T(8,128)S(1)}, u32[]{:S(2)}, u32[]{:S(2)}) collective-permute-start(f32[168,128]{1,0:T(8,128)S(1)} %copy-done.12), channel_id=1, source_target_pairs={{0,4},{4,0},{8,12},{12,8},{1,5},{5,1},{9,13},{13,9},{2,6},{6,2},{1... | collective-permute-start | bytes 258056 | tf_op jit(solution)/shard_map/ppermute | solution.py:591
  23.0 9.9 %collective-permute-start.2 = (f32[168,128]{1,0:T(8,128)S(1)}, f32[168,128]{1,0:T(8,128)S(1)}, u32[]{:S(2)}, u32[]{:S(2)}) collective-permute-start(f32[168,128]{1,0:T(8,128)S(1)} %copy-done.11), channel_id=1, source_target_pairs={{0,8},{4,12},{8,0},{12,4},{1,9},{5,13},{9,1},{13,5},{2,10},{6,14},... | collective-permute-start | bytes 258056 | tf_op jit(solution)/shard_map/ppermute | solution.py:591
  25.4 7.5 %collective-permute-start.3 = (f32[168,128]{1,0:T(8,128)S(1)}, f32[168,128]{1,0:T(8,128)S(1)}, u32[]{:S(2)}, u32[]{:S(2)}) collective-permute-start(f32[168,128]{1,0:T(8,128)S(1)} %copy-done.10), channel_id=1, source_target_pairs={{0,12},{4,8},{8,4},{12,0},{1,13},{5,9},{9,5},{13,1},{2,14},{6,10},... | collective-permute-start | bytes 258056 | tf_op jit(solution)/shard_map/ppermute | solution.py:591
  26.1 6.8 %collective-permute-start.5 = (f32[1,128,512]{2,1,0:T(8,128)S(1)}, f32[1,128,512]{2,1,0:T(8,128)S(1)}, u32[]{:S(2)}, u32[]{:S(2)}) collective-permute-start(f32[1,128,512]{2,1,0:T(8,128)S(1)} %copy-done.3), channel_id=1, source_target_pairs={{0,1},{1,0},{2,3},{3,2},{4,5},{5,4},{6,7},{7,6},{8,9},{9,8},{10,11... | collective-permute-start | bytes 786440 | tf_op jit(solution)/shard_map/ppermute | solution.py:574
  26.1 13.3 %all-to-all-start.1 = ((f32[16,16,128]{2,1,0:T(8,128)}), f32[16,16,128]{2,1,0:T(8,128)S(1)}, u32[]{:S(2)}, u32[]{:S(2)}) async-start(f32[16,16,128]{2,1,0:T(8,128)} %get-tuple-element.23), calls=%async_computation.1 | async-start | bytes 262144 | tf_op jit(solution)/shard_map/all_to_all | solution.py:577
  42.3 0.8 %copy-start.4 = (f32[2,128,512]{2,1,0:T(8,128)}, f32[2,128,512]{2,1,0:T(8,128)S(1)}, u32[]{:S(2)}) copy-start(f32[2,128,512]{2,1,0:T(8,128)S(1)} %get-tuple-element.35.rp_ref) | copy-start | bytes 1572868
  43.2 23.6 %copy-start.5 = (f32[2,128,512]{2,1,0:T(8,128)S(1)}, f32[2,128,512]{2,1,0:T(8,128)}, u32[]{:S(2)}) copy-start(f32[2,128,512]{2,1,0:T(8,128)} %copy-done.4) | copy-start | bytes 1572868
  43.2 4.0 %collective-permute-start.6 = (f32[2,128,512]{2,1,0:T(8,128)S(1)}, f32[2,128,512]{2,1,0:T(8,128)S(1)}, u32[]{:S(2)}, u32[]{:S(2)}) collective-permute-start(f32[2,128,512]{2,1,0:T(8,128)S(1)} %get-tuple-element.32.refs_0_.to_ref), channel_id=1, source_target_pairs={{0,1},{1,0},{2,3},{3,2},{4,5},{5,4},{6,7},{7,6},{8,9},{9,8},{10,11... | collective-permute-start | bytes 1572872 | tf_op jit(solution)/shard_map/ppermute | solution.py:645
  43.2 11.9 %all-to-all-start.2 = ((f32[16,16,128]{2,1,0:T(8,128)}), f32[16,16,128]{2,1,0:T(8,128)S(1)}, u32[]{:S(2)}, u32[]{:S(2)}) async-start(f32[16,16,128]{2,1,0:T(8,128)} %get-tuple-element.31), calls=%async_computation.2 | async-start | bytes 262144 | tf_op jit(solution)/shard_map/all_to_all | solution.py:577
  57.5 9.3 %collective-permute-start.7 = (f32[2,128,512]{2,1,0:T(8,128)S(1)}, f32[2,128,512]{2,1,0:T(8,128)S(1)}, u32[]{:S(2)}, u32[]{:S(2)}) collective-permute-start(f32[2,128,512]{2,1,0:T(8,128)S(1)} %get-tuple-element.37.to_ref), channel_id=1, source_target_pairs={{0,1},{1,0},{2,3},{3,2},{4,5},{5,4},{6,7},{7,6},{8,9},{9,8},{10,11... | collective-permute-start | bytes 1572872 | tf_op jit(solution)/shard_map/ppermute | solution.py:651
